TPU v7x, 32 devices: a whole 2x2x4 slice. The times are simulated.
32 devices in a mesh: area: 8 (over z, x), harm: 4 (over y, core).
Axes of the slice: x: 2, y: 2, z: 4, core: 2. Of those that a mesh axis runs over, the one named last changes fastest.
Arguments:
- volt: float32 [2, 8, 28, 32, 768], P(None, 'area', 'harm'), may hold values from -3 to 3
- inject: float32 [2, 8, 28, 32, 768], P(None, 'area', 'harm'), may hold values from -6 to 6
- zinv: bfloat16 [2, 8, 28, 768, 768], P(None, 'area', 'harm')
- dev_bus: int32 [8, 2048], P('area'), may hold values from 0 to 767
- dev_count: int32 [8], P('area'), may hold values from 1 to 2048, 8192 in all
- dev_cond: float32 [8, 2048], P('area'), may hold values from 0.1 to 1
- dev_sat: float32 [8, 2048], P('area'), may hold values from 0.2 to 2
- tie_bus: int32 [8, 256], P('area'), may hold values from 0 to 127
- tie_area: int32 [8, 256, 1], P('area'), may hold values from 0 to 7; in each aligned block of 256 rows (0 to 255, 256 to 511, ..., all dimensions but the last counted through in order) at most 64 rows name the same one
- tie_far: int32 [8, 256], P('area'), may hold values from 0 to 127
- tie_res: float32 [8, 256], P('area'), may hold values from 0.5 to 2
- tie_reac: float32 [8, 256], P('area'), may hold values from 0.01 to 0.1
Outputs:
- volt_next: float32 [2, 8, 28, 32, 768], P(None, 'area', 'harm')
Inputs may be any that keep to these rules, and one draw needn't show every extreme that they name: `dev_count`: slot k of an area holds an inverter exactly when k is below its count; the counts sum to 8192 and some area has exactly 2048 inverters. `tie_area`: in one area's list no area is named more than 64 times, and in some list some area is named exactly 64 times; every area is named in some list; a list may name its own area.
All inputs are finite; a program needn't handle non-finite values. No bound on the sum of `dev_count` on one device may be relied on, other than what follows from the above.
Results may differ from a plain program's by a relative error of at most 0.0029.
Values sent between devices are 32-bit elements; how exact they have to be, the bound alone decides.
No kernel may reach another device: no remote copies, remote signals or barrier semaphores. Data moves between devices by JAX's collectives and lax.ppermute only.
A program may use at most 128 MiB of HBM per device.

v0:
```python
import functools

import jax
import jax.numpy as jnp
import numpy as np
from jax import lax
from jax.experimental import pallas as pl
from jax.experimental.pallas import tpu as pltpu
from jax.sharding import PartitionSpec as P

TS = 512
HALF = TS // 2
NBD = 128
LANES = 128
BF16 = jnp.bfloat16
F32 = jnp.float32
NT_DIMS = (((1,), (1,)), ((), ()))
VMEM_BYTES = 40 * 1024 * 1024


def up(value, step):
    return -(-value // step) * step


def split(value):
    high = value.astype(BF16)
    return high, (value - high.astype(F32)).astype(BF16)


def np_split(value):
    value = np.asarray(value, np.float32)
    high = value.astype(jnp.bfloat16)
    return high, (value - high.astype(np.float32)).astype(jnp.bfloat16)


def chunk_sizes(buses):
    sizes = []
    left = buses
    while left > 0:
        sizes.append(min(256, left))
        left -= sizes[-1]
    return sizes


def wave_tables(ranks, h_local):
    order_count = ranks * h_local
    samples = np.arange(HALF)[:, None]
    orders = 2 * np.arange(order_count)[None, :] + 1
    angles = (samples * orders % TS) * (2.0 * np.pi / TS)
    cos, sin = np.cos(angles), np.sin(angles)
    rows = 2 * h_local
    k_pad = up(ranks * rows, 16)
    m_pad = up(rows, 8)
    forward, inverse = [], []
    for rank in range(ranks):
        there = np.zeros((HALF, k_pad))
        back = np.zeros((2 * m_pad, HALF))
        for k in range(ranks):
            own = slice((rank ^ k) * h_local, ((rank ^ k) + 1) * h_local)
            part = np.concatenate([cos[:, own], -sin[:, own]], axis=1)
            there[:, k * rows : (k + 1) * rows] = 2.0 * part
            if k < 2:
                back[k * m_pad : k * m_pad + rows] = (4.0 / TS) * part.T
        high, low = np_split(there)
        forward.append(np.concatenate([high, high, low], axis=1))
        high, low = np_split(back)
        inverse.append(np.concatenate([high, low], axis=0))
    return np.stack(forward), np.stack(inverse), k_pad, m_pad


def wave_kernel(
    scens, rows, k_pad, m_pad, rank_ref, there_ref, back_ref, *refs
):
    sources = refs[:-4]
    own_ref, sib_ref, buf, sems = refs[-4:]
    block = rows * scens
    columns = buf.shape[0]
    copies = []
    for k, source in enumerate(sources):
        for j in range(columns):
            copy = pltpu.make_async_copy(
                source.at[:, pl.ds(j * LANES, LANES)],
                buf.at[j, pl.ds(k * block, block)],
                sems.at[k, j],
            )
            copy.start()
            copies.append(copy)
    used = len(sources) * block
    if k_pad * scens > used:
        buf[:, pl.ds(used, k_pad * scens - used), :] = jnp.zeros(
            (columns, k_pad * scens - used, LANES), F32
        )
    for copy in copies:
        copy.wait()
    for s in range(scens):
        volts = [buf[j, pl.ds(s, k_pad, stride=scens), :] for j in range(columns)]
        high, low = split(jnp.concatenate(volts, axis=1))
        stacked = jnp.concatenate([high, low, high], axis=0)
        wave = jnp.dot(there_ref[0], stacked, preferred_element_type=F32)
        shaped = jnp.tanh(wave.astype(BF16))
        out = jnp.dot(back_ref[0], shaped, preferred_element_type=F32)
        out = out[: 2 * m_pad] + out[2 * m_pad :]
        for j in range(columns):
            at = slice(j * LANES, (j + 1) * LANES)
            own_ref[j, pl.ds(s * m_pad, m_pad), :] = out[:m_pad, at]
            sib_ref[j, pl.ds(s * m_pad, m_pad), :] = out[m_pad:, at]


def wave(rank, tables, sources, scens, rows):
    there, back, k_pad, m_pad = tables
    width = sources[0].shape[1]
    ranks = len(sources)
    columns = width // LANES
    shape = jax.ShapeDtypeStruct((columns, scens * m_pad, LANES), F32)
    grid_spec = pltpu.PrefetchScalarGridSpec(
        num_scalar_prefetch=1,
        grid=(1,),
        in_specs=[
            pl.BlockSpec((1,) + there.shape[1:], lambda i, r: (r[0], 0, 0)),
            pl.BlockSpec((1,) + back.shape[1:], lambda i, r: (r[0], 0, 0)),
        ]
        + [pl.BlockSpec(memory_space=pl.ANY)] * ranks,
        out_specs=[pl.BlockSpec(shape.shape, lambda i, r: (0, 0, 0))] * 2,
        scratch_shapes=[
            pltpu.VMEM((columns, k_pad * scens, LANES), F32),
            pltpu.SemaphoreType.DMA((ranks, columns)),
        ],
    )
    return pl.pallas_call(
        functools.partial(wave_kernel, scens, rows, k_pad, m_pad),
        grid_spec=grid_spec,
        out_shape=[shape, shape],
        compiler_params=pltpu.CompilerParams(vmem_limit_bytes=VMEM_BYTES),
        cost_estimate=pl.CostEstimate(
            flops=2 * scens * width * HALF * 512,
            bytes_accessed=4 * width * scens * (k_pad + 2 * m_pad),
            transcendentals=scens * width * HALF,
        ),
        name="wave",
    )(rank, jnp.asarray(there), jnp.asarray(back), *sources)


def level_kernel(buses, step, count_ref, bus_ref, cond_ref, sat_ref, out_ref):
    slots = bus_ref.shape[1]
    total = jnp.zeros((16, buses), F32)
    for start in range(0, slots, step):
        at = pl.ds(start, step)
        slot_ids = lax.broadcasted_iota(jnp.int32, (1, step), 1) + start
        live = slot_ids < count_ref[0]
        pieces = []
        for ref in (cond_ref, sat_ref):
            rest = jnp.where(live, ref[:, at], 0.0)
            for _ in range(3):
                high = rest.astype(BF16).astype(F32)
                pieces.append(high)
                rest = rest - high
        pieces.append(jnp.zeros((10, step), F32))
        weights = jnp.concatenate(pieces, axis=0).astype(BF16)
        bus_ids = lax.broadcasted_iota(jnp.int32, (buses, step), 0)
        onehot = jnp.where(bus_ids == bus_ref[:, at], 1.0, 0.0).astype(BF16)
        total += lax.dot_general(
            weights, onehot, NT_DIMS, preferred_element_type=F32
        )
    out_ref[0:1, :] = total[0:1] + total[1:2] + total[2:3]
    out_ref[1:2, :] = total[3:4] + total[4:5] + total[5:6]


def levels(dev_count, dev_bus, dev_cond, dev_sat, buses):
    slots = dev_bus.shape[1]
    step = 512 if slots % 512 == 0 else slots
    return pl.pallas_call(
        functools.partial(level_kernel, buses, step),
        in_specs=[
            pl.BlockSpec(memory_space=pltpu.SMEM),
            pl.BlockSpec(memory_space=pltpu.VMEM),
            pl.BlockSpec(memory_space=pltpu.VMEM),
            pl.BlockSpec(memory_space=pltpu.VMEM),
        ],
        out_specs=pl.BlockSpec(memory_space=pltpu.VMEM),
        out_shape=jax.ShapeDtypeStruct((8, buses), F32),
        compiler_params=pltpu.CompilerParams(vmem_limit_bytes=VMEM_BYTES),
        cost_estimate=pl.CostEstimate(
            flops=2 * 256 * slots * buses, bytes_accessed=16 * slots, transcendentals=0
        ),
        name="levels",
    )(dev_count, dev_bus, dev_cond, dev_sat)


def tie_kernel(
    h_local, scens, id_ref, bus_ref, area_ref, far_ref, res_ref, reac_ref, *refs
):
    blocks, out_ref, scaled = refs[:-2], refs[-2], refs[-1]
    ties = bus_ref.shape[1]
    edge_ids = lax.broadcasted_iota(jnp.int32, (NBD, ties), 0)
    far_hit = edge_ids == far_ref[...]
    far = jnp.zeros((2 * h_local * scens, ties), F32)
    for first in range(0, len(blocks), 2):
        pair = range(first, min(first + 2, len(blocks)))
        parts = [split(blocks[q][...]) for q in pair]
        onehot = jnp.concatenate(
            [
                jnp.where(far_hit & (area_ref[...] == id_ref[1 + q]), 1.0, 0.0)
                for q in pair
            ],
            axis=0,
        ).astype(BF16)
        for piece in range(2):
            edges = jnp.concatenate([part[piece] for part in parts], axis=1)
            far += jnp.dot(edges, onehot, preferred_element_type=F32)
    resist = res_ref[...]
    imag_rows = h_local * scens
    for h in range(h_local):
        order = (2 * (id_ref[0] * h_local + h) + 1).astype(F32)
        reactance = reac_ref[...] * order
        denominator = resist * resist + reactance * reactance
        adm_real = resist / denominator
        adm_imag = -reactance / denominator
        real = far[h * scens : (h + 1) * scens]
        imag = far[imag_rows + h * scens : imag_rows + (h + 1) * scens]
        scaled[pl.ds(h * scens, scens), :] = adm_real * real - adm_imag * imag
        scaled[pl.ds(imag_rows + h * scens, scens), :] = (
            adm_real * imag + adm_imag * real
        )
    target = jnp.where(edge_ids == bus_ref[...], 1.0, 0.0).astype(BF16)
    high, low = split(scaled[...])
    out_ref[...] = lax.dot_general(
        high, target, NT_DIMS, preferred_element_type=F32
    ) + lax.dot_general(low, target, NT_DIMS, preferred_element_type=F32)


def tie_currents(ids, tie_lists, blocks, h_local, scens):
    ties = tie_lists[0].shape[1]
    rows = 2 * h_local * scens
    vmem = pl.BlockSpec(memory_space=pltpu.VMEM)
    return pl.pallas_call(
        functools.partial(tie_kernel, h_local, scens),
        in_specs=[pl.BlockSpec(memory_space=pltpu.SMEM)]
        + [vmem] * (len(tie_lists) + len(blocks)),
        out_specs=vmem,
        out_shape=jax.ShapeDtypeStruct((rows, NBD), F32),
        scratch_shapes=[pltpu.VMEM((rows, ties), F32)],
        compiler_params=pltpu.CompilerParams(vmem_limit_bytes=VMEM_BYTES),
        cost_estimate=pl.CostEstimate(
            flops=4 * rows * ties * NBD * (len(blocks) + 1),
            bytes_accessed=4 * rows * NBD * (len(blocks) + 1),
            transcendentals=0,
        ),
        name="ties",
    )(ids, *tie_lists, *blocks)


def solve_kernel(
    scens, h_local, m_pad, start, has_tie, has_total, rank_ref, *refs
):
    half = scens // 2
    refs = list(refs)
    volt_ref, inject_ref, zinv_ref, level_ref, own_ref, sib_ref = refs[:6]
    del refs[:6]
    tie_ref = refs.pop(0) if has_tie else None
    total_ref = refs.pop(0) if has_total else None
    (out_ref,) = refs
    h = pl.program_id(0)
    even = rank_ref[0] % 2 == 0
    cond_level = level_ref[0:1, :]
    sat_level = level_ref[1:2, :]
    parts = []
    for c in range(2):
        at = pl.ds(c * h_local + h, half, stride=m_pad)
        own = jnp.concatenate(
            [own_ref[j, at, :] for j in range(own_ref.shape[0])], axis=1
        )
        sib = jnp.concatenate(
            [sib_ref[j, at, :] for j in range(sib_ref.shape[0])], axis=1
        )
        shaped = jnp.concatenate(
            [jnp.where(even, own, sib), jnp.where(even, sib, own)], axis=0
        )
        rhs = inject_ref[c, 0, 0] + (
            cond_level * volt_ref[c, 0, 0] + sat_level * shaped
        )
        if has_tie:
            ties = tie_ref[c, 0]
            if rhs.shape[1] > NBD:
                rhs = jnp.concatenate([rhs[:, :NBD] + ties, rhs[:, NBD:]], axis=1)
            else:
                rhs = rhs + ties
        parts.append(rhs.astype(BF16))
    both = jnp.concatenate(parts, axis=0)
    by_real = lax.dot_general(
        both, zinv_ref[0, 0, 0], NT_DIMS, preferred_element_type=F32
    )
    by_imag = lax.dot_general(
        both, zinv_ref[1, 0, 0], NT_DIMS, preferred_element_type=F32
    )
    real = by_real[:scens] - by_imag[scens:]
    imag = by_real[scens:] + by_imag[:scens]
    if has_total:
        real = real + total_ref[0, 0, 0]
        imag = imag + total_ref[1, 0, 0]
    out_ref[0, 0, 0] = real
    out_ref[1, 0, 0] = imag


def solve(rank, volt, inject, zinv, level, own, sib, tie, total, start, width, m_pad):
    _, _, h_local, scens, buses = volt.shape
    at = start // width
    assert at * width == start
    wide = pl.BlockSpec((2, 1, 1, scens, width), lambda h, r: (0, 0, h, 0, at))
    whole = pl.BlockSpec((2, 1, 1, scens, buses), lambda h, r: (0, 0, h, 0, 0))
    in_specs = [
        wide,
        wide,
        pl.BlockSpec((2, 1, 1, buses, width), lambda h, r: (0, 0, h, 0, at)),
        pl.BlockSpec((8, width), lambda h, r: (0, at)),
        pl.BlockSpec(own.shape, lambda h, r: (0, 0, 0)),
        pl.BlockSpec(sib.shape, lambda h, r: (0, 0, 0)),
    ]
    operands = [volt, inject, zinv, level, own, sib]
    if tie is not None:
        in_specs.append(pl.BlockSpec((2, 1, scens, NBD), lambda h, r: (0, h, 0, 0)))
        operands.append(tie)
    aliases = {}
    if total is not None:
        aliases = {1 + len(operands): 0}
        in_specs.append(whole)
        operands.append(total)
    return pl.pallas_call(
        functools.partial(
            solve_kernel,
            scens,
            h_local,
            m_pad,
            start,
            tie is not None,
            total is not None,
        ),
        grid_spec=pltpu.PrefetchScalarGridSpec(
            num_scalar_prefetch=1, grid=(h_local,), in_specs=in_specs, out_specs=whole
        ),
        out_shape=jax.ShapeDtypeStruct(volt.shape, F32),
        input_output_aliases=aliases,
        compiler_params=pltpu.CompilerParams(vmem_limit_bytes=VMEM_BYTES),
        cost_estimate=pl.CostEstimate(
            flops=8 * h_local * scens * buses * width,
            bytes_accessed=4 * h_local * buses * width,
            transcendentals=0,
        ),
        name="solve",
    )(rank, *operands)


def per_device(
    volt,
    inject,
    zinv,
    dev_bus,
    dev_count,
    dev_cond,
    dev_sat,
    tie_bus,
    tie_area,
    tie_far,
    tie_res,
    tie_reac,
):
    _, _, h_local, scens, buses = volt.shape
    ranks = lax.axis_size("harm")
    areas = lax.axis_size("area")
    rank = lax.axis_index("harm")
    area = lax.axis_index("area")
    half = scens // 2
    rows = 2 * h_local
    rank_arg = jnp.full((1,), rank, jnp.int32)
    tables = wave_tables(ranks, h_local)
    m_pad = tables[3]
    side = rank % 2

    def swap(value, k):
        return lax.ppermute(value, "harm", [(i, i ^ k) for i in range(ranks)])

    sizes = chunk_sizes(buses)
    starts = [buses - sum(sizes[: i + 1]) for i in range(len(sizes))]
    arrived = []
    for start, width in zip(starts, sizes):
        lanes = volt[..., start : start + width]
        mine = lax.dynamic_slice_in_dim(lanes, side * half, half, axis=3)
        other = lax.dynamic_slice_in_dim(lanes, (1 - side) * half, half, axis=3)
        mine = mine.reshape(rows * half, width)
        other = other.reshape(rows * half, width)
        arrived.append(
            [mine] + [swap(other if k % 2 else mine, k) for k in range(1, ranks)]
        )

    edge = volt[..., :NBD].reshape(rows * scens, NBD)
    ring = [(a, (a + 2) % areas) for a in range(areas)]
    pairs = [(a, a ^ 1) for a in range(areas)]
    blocks = [edge]
    block_ids = [area]
    for step in range(areas // 2):
        blocks.append(lax.ppermute(blocks[2 * step], "area", pairs))
        block_ids.append((area - 2 * step) % areas ^ 1)
        if step + 1 < areas // 2:
            blocks.append(lax.ppermute(blocks[2 * step], "area", ring))
            block_ids.append((area - 2 * (step + 1)) % areas)
    ids = jnp.stack([rank] + block_ids).astype(jnp.int32)

    level = levels(dev_count, dev_bus, dev_cond, dev_sat, buses)
    tie_lists = [
        tie_bus,
        tie_area[:, :, 0],
        tie_far,
        tie_res,
        tie_reac,
    ]
    tie = tie_currents(ids, tie_lists, blocks, h_local, scens)
    tie = tie.reshape(2, h_local, scens, NBD)

    total = None
    for start, width, sources in zip(starts, sizes, arrived):
        own, for_sib = wave(rank_arg, tables, sources, half, rows)
        sib = swap(for_sib, 1)
        total = solve(
            rank_arg,
            volt,
            inject,
            zinv,
            level,
            own,
            sib,
            tie if start == 0 else None,
            total,
            start,
            width,
            m_pad,
        )
    return total


def solution(mesh):
    wide = P(None, "area", "harm", None, None)
    flat = P("area", None)
    in_specs = (
        wide,
        wide,
        wide,
        flat,
        P("area"),
        flat,
        flat,
        flat,
        P("area", None, None),
        flat,
        flat,
        flat,
    )
    return jax.shard_map(
        per_device, mesh=mesh, in_specs=in_specs, out_specs=wide, check_vma=False
    )
```

profile of v0, /device:TPU:0, one launch (start us, length us, event | category | flops | bytes accessed | tf_op | source)
XLA Modules:
  0.0 71.5 jit_solution(5753599675185933036)
XLA Ops:
  0.0 2.2 %fusion = (f32[2,1,7,32,256]{4,3,2,1,0:T(8,128)S(1)}, f32[2,1,7,32,256]{4,3,2,1,0:T(8,128)S(1)}, f32[2,1,7,32,256]{4,3,2,1,0:T(8,128)}) fusion(f32[2,1,7,32,768]{4,3,2,1,0:T(8,128)} %refs_0_.5), kind=kLoop, calls=%fused_computation.6 | loop fusion | bytes 2752512 | tf_op jit(solution)/shard_map/slice | solution.py:385
  2.2 0.1 constant_dynamic-slice_fusion
  2.3 0.5 collective-permute-start.15
  2.8 2.6 %collective-permute-start.16 = (f32[224,256]{1,0:T(8,128)S(1)}, f32[224,256]{1,0:T(8,128)S(1)}, u32[]{:S(2)}, u32[]{:S(2)}) collective-permute-start(f32[224,256]{1,0:T(8,128)S(1)} %bitcast.24), channel_id=1, source_target_pairs={{0,2},{1,3},{2,0},{3,1},{4,6},{5,7},{6,4},{7,5},{8,10},{9,11},{10,... | collective-permute-start | bytes 688136 | tf_op jit(solution)/shard_map/ppermute | solution.py:379
  5.4 1.6 %collective-permute-start.5 = (f32[448,128]{1,0:T(8,128)S(1)}, f32[448,128]{1,0:T(8,128)S(1)}, u32[]{:S(2)}, u32[]{:S(2)}) collective-permute-start(f32[448,128]{1,0:T(8,128)S(1)} %bitcast.19), channel_id=1, source_target_pairs={{0,8},{4,12},{8,16},{12,20},{16,24},{20,28},{24,0},{28,4},{1,9},{5... | collective-permute-start | bytes 688136 | tf_op jit(solution)/shard_map/ppermute | solution.py:403
  7.0 0.3 collective-permute-start.17
  7.3 1.0 %collective-permute-start.11 = (f32[224,256]{1,0:T(8,128)S(1)}, f32[224,256]{1,0:T(8,128)S(1)}, u32[]{:S(2)}, u32[]{:S(2)}) collective-permute-start(f32[224,256]{1,0:T(8,128)S(1)} %bitcast.29), channel_id=1, source_target_pairs={{0,1},{1,0},{2,3},{3,2},{4,5},{5,4},{6,7},{7,6},{8,9},{9,8},{10,11... | collective-permute-start | bytes 688136 | tf_op jit(solution)/shard_map/ppermute | solution.py:379
  8.3 0.5 collective-permute-start.13
  8.8 3.0 %collective-permute-done.16.refs_2_ = f32[224,256]{1,0:T(8,128)S(1)} collective-permute-done((f32[224,256]{1,0:T(8,128)S(1)}, f32[224,256]{1,0:T(8,128)S(1)}, u32[]{:S(2)}, u32[]{:S(2)}) %collective-permute-start.16) | collective-permute-done | bytes 229408 | tf_op jit(solution)/shard_map/ppermute | solution.py:379
  11.8 1.9 %collective-permute-start.12 = (f32[224,256]{1,0:T(8,128)S(1)}, f32[224,256]{1,0:T(8,128)S(1)}, u32[]{:S(2)}, u32[]{:S(2)}) collective-permute-start(f32[224,256]{1,0:T(8,128)S(1)} %bitcast.22), channel_id=1, source_target_pairs={{0,2},{1,3},{2,0},{3,1},{4,6},{5,7},{6,4},{7,5},{8,10},{9,11},{10,... | collective-permute-start | bytes 688136 | tf_op jit(solution)/shard_map/ppermute | solution.py:379
  13.8 1.2 %collective-permute-done.5.refs_2_ = f32[448,128]{1,0:T(8,128)S(1)} collective-permute-done((f32[448,128]{1,0:T(8,128)S(1)}, f32[448,128]{1,0:T(8,128)S(1)}, u32[]{:S(2)}, u32[]{:S(2)}) %collective-permute-start.5) | collective-permute-done | bytes 229408 | tf_op jit(solution)/shard_map/ppermute | solution.py:403
  15.0 0.4 collective-permute-start.7
  15.4 0.8 %collective-permute-done.17.refs_3_ = f32[224,256]{1,0:T(8,128)S(1)} collective-permute-done((f32[224,256]{1,0:T(8,128)S(1)}, f32[224,256]{1,0:T(8,128)S(1)}, u32[]{:S(2)}, u32[]{:S(2)}) %collective-permute-start.17) | collective-permute-done | bytes 229408 | tf_op jit(solution)/shard_map/ppermute | solution.py:379
  16.2 0.6 collective-permute-start
  16.9 3.8 %wave.5 = (f32[2,256,128]{2,1,0:T(8,128)S(1)}, f32[2,256,128]{2,1,0:T(8,128)S(1)}) custom-call(s32[1]{0:T(128)} %bitcast.rank_ref, bf16[4,256,192]{2,1,0:T(8,128)(2,1)S(1)} %copy-done.10, bf16[4,64,256]{2,1,0:T(8,128)(2,1)S(1)} %copy-done.11, f32[224,256]{1,0:T(8,128)S(1)} %bitcast.25, f32[224,256]{1,0:T(8,128)S(1)} %collective-permute-done.15.refs_1_, ...), custom_call_target="tpu_custom_call" | custom-call | flops 1073741824 | bytes 1572864 | tf_op jit(solution)/shard_map/wave/pallas_call | solution.py:129
  20.7 0.0 collective-permute-done.11.refs_1_
  20.7 1.6 %collective-permute-start.2 = (f32[224,256]{1,0:T(8,128)S(1)}, f32[224,256]{1,0:T(8,128)S(1)}, u32[]{:S(2)}, u32[]{:S(2)}) collective-permute-start(f32[224,256]{1,0:T(8,128)S(1)} %bitcast.34), channel_id=1, source_target_pairs={{0,3},{1,2},{2,1},{3,0},{4,7},{5,6},{6,5},{7,4},{8,11},{9,10},{10,... | collective-permute-start | bytes 688136 | tf_op jit(solution)/shard_map/ppermute | solution.py:379
  22.3 4.3 %collective-permute-done.12.refs_2_ = f32[224,256]{1,0:T(8,128)S(1)} collective-permute-done((f32[224,256]{1,0:T(8,128)S(1)}, f32[224,256]{1,0:T(8,128)S(1)}, u32[]{:S(2)}, u32[]{:S(2)}) %collective-permute-start.12) | collective-permute-done | bytes 229408 | tf_op jit(solution)/shard_map/ppermute | solution.py:379
  26.6 1.9 %collective-permute-start.1 = (f32[224,256]{1,0:T(8,128)S(1)}, f32[224,256]{1,0:T(8,128)S(1)}, u32[]{:S(2)}, u32[]{:S(2)}) collective-permute-start(f32[224,256]{1,0:T(8,128)S(1)} %bitcast.26), channel_id=1, source_target_pairs={{0,2},{1,3},{2,0},{3,1},{4,6},{5,7},{6,4},{7,5},{8,10},{9,11},{10,... | collective-permute-start | bytes 688136 | tf_op jit(solution)/shard_map/ppermute | solution.py:379
  28.5 0.0 collective-permute-done.13.refs_3_
  28.5 0.0 collective-permute-start.18
  28.5 0.0 collective-permute-done.7.refs_4_
  28.6 1.6 %collective-permute-start.9 = (f32[448,128]{1,0:T(8,128)}, f32[448,128]{1,0:T(8,128)}, u32[]{:S(2)}, u32[]{:S(2)}) collective-permute-start(f32[448,128]{1,0:T(8,128)} %collective-permute-done.7.refs_4_), channel_id=1, source_target_pairs={{0,8},{4,12},{8,16},{12,20},{16,24},{20,28},{24,0},{28,4},{1,9},{5... | collective-permute-start | bytes 688136 | tf_op jit(solution)/shard_map/ppermute | solution.py:403
  30.2 3.8 %wave.4 = (f32[2,256,128]{2,1,0:T(8,128)S(1)}, f32[2,256,128]{2,1,0:T(8,128)S(1)}) custom-call(s32[1]{0:T(128)} %bitcast.rank_ref, bf16[4,256,192]{2,1,0:T(8,128)(2,1)S(1)} %copy-done.10, bf16[4,64,256]{2,1,0:T(8,128)(2,1)S(1)} %copy-done.11, f32[224,256]{1,0:T(8,128)S(1)} %bitcast.23, f32[224,256]{1,0:T(8,128)S(1)} %collective-permute-done.11.refs_1_, ...), custom_call_target="tpu_custom_call" | custom-call | flops 1073741824 | bytes 1572864 | tf_op jit(solution)/shard_map/wave/pallas_call | solution.py:129
  34.0 0.0 collective-permute-done.refs_1_
  34.0 0.0 copy-start.7
  34.0 0.0 copy-start.8
  34.0 0.0 copy-start.9
  34.0 0.2 collective-permute-start.14
  34.3 1.9 %collective-permute-done.1.refs_2_ = f32[224,256]{1,0:T(8,128)S(1)} collective-permute-done((f32[224,256]{1,0:T(8,128)S(1)}, f32[224,256]{1,0:T(8,128)S(1)}, u32[]{:S(2)}, u32[]{:S(2)}) %collective-permute-start.1) | collective-permute-done | bytes 229408 | tf_op jit(solution)/shard_map/ppermute | solution.py:379
  36.2 1.7 %collective-permute-start.4 = (f32[448,128]{1,0:T(8,128)S(1)}, f32[448,128]{1,0:T(8,128)}, u32[]{:S(2)}, u32[]{:S(2)}) collective-permute-start(f32[448,128]{1,0:T(8,128)S(1)} %bitcast.20), channel_id=1, source_target_pairs={{0,4},{4,0},{8,12},{12,8},{16,20},{20,16},{24,28},{28,24},{1,5},{5... | collective-permute-start | bytes 688136 | tf_op jit(solution)/shard_map/ppermute | solution.py:400
  37.9 0.3 collective-permute-start.6
  38.2 0.0 collective-permute-done.18.refs_5_
  38.2 1.7 %collective-permute-start.8 = (f32[448,128]{1,0:T(8,128)}, f32[448,128]{1,0:T(8,128)}, u32[]{:S(2)}, u32[]{:S(2)}) collective-permute-start(f32[448,128]{1,0:T(8,128)} %collective-permute-done.7.refs_4_), channel_id=1, source_target_pairs={{0,4},{4,0},{8,12},{12,8},{16,20},{20,16},{24,28},{28,24},{1,5},{5... | collective-permute-start | bytes 688136 | tf_op jit(solution)/shard_map/ppermute | solution.py:400
  39.9 0.0 collective-permute-done.9.refs_6_
  39.9 0.3 collective-permute-start.10
  40.2 4.5 %wave.3 = (f32[2,256,128]{2,1,0:T(8,128)S(1)}, f32[2,256,128]{2,1,0:T(8,128)}) custom-call(s32[1]{0:T(128)} %bitcast.rank_ref, bf16[4,256,192]{2,1,0:T(8,128)(2,1)S(1)} %copy-done.10, bf16[4,64,256]{2,1,0:T(8,128)(2,1)S(1)} %copy-done.11, f32[224,256]{1,0:T(8,128)S(1)} %bitcast.27, f32[224,256]{1,0:T(8,128)S(1)} %collective-permute-done.refs_1_, ...), custom_call_target="tpu_custom_call" | custom-call | flops 1073741824 | bytes 1572864 | tf_op jit(solution)/shard_map/wave/pallas_call | solution.py:129
  44.7 0.0 collective-permute-done.14.refs_5_
  44.7 0.1 collective-permute-start.3
  45.5 0.1 stack.36.id_ref
  45.6 0.0 copy-start.1
  45.6 0.9 %levels.1.refs_3_ = f32[8,768]{1,0:T(8,128)S(1)} custom-call(s32[1]{0:T(128)S(6)} %copy.19.count_ref, s32[1,2048]{1,0:T(1,128)S(1)} %copy-done.7, f32[1,2048]{1,0:T(1,128)S(1)} %copy-done.8, f32[1,2048]{1,0:T(1,128)S(1)} %copy-done.9), custom_call_target="tpu_custom_call" | custom-call | flops 805306368 | bytes 32768 | tf_op jit(solution)/shard_map/levels/pallas_call | solution.py:171
  46.6 0.4 copy-done.1
  47.0 7.2 %solve.3.refs_6_ = f32[2,1,7,32,768]{4,3,2,1,0:T(8,128)} custom-call(s32[1]{0:T(128)} %bitcast.rank_ref, f32[2,1,7,32,768]{4,3,2,1,0:T(8,128)S(1)} %copy-done, f32[2,1,7,32,768]{4,3,2,1,0:T(8,128)S(1)} %copy-done.1, bf16[2,1,7,768,768]{4,3,2,1,0:T(8,128)(2,1)} %refs_2_.5, f32[8,768]{1,0:T(8,128)S(1)} %levels.1.refs_3_, ...), custom_call_target="tpu_custom_call" | custom-call | flops 352321536 | bytes 5505024 | tf_op jit(solution)/shard_map/solve/pallas_call | solution.py:327
  54.2 0.0 copy-start.6
  54.2 7.3 %solve.4.refs_7_ = f32[2,1,7,32,768]{4,3,2,1,0:T(8,128)} custom-call(s32[1]{0:T(128)} %bitcast.rank_ref, f32[2,1,7,32,768]{4,3,2,1,0:T(8,128)S(1)} %copy-done, f32[2,1,7,32,768]{4,3,2,1,0:T(8,128)S(1)} %copy-done.1, bf16[2,1,7,768,768]{4,3,2,1,0:T(8,128)(2,1)} %refs_2_.5, f32[8,768]{1,0:T(8,128)S(1)} %levels.1.refs_3_, ...), custom_call_target="tpu_custom_call", output_to_operand_aliasing={{}: (7, {})} | custom-call | flops 352321536 | bytes 5505024 | tf_op jit(solution)/shard_map/solve/pallas_call | solution.py:327
  61.6 2.5 %ties.1 = f32[448,128]{1,0:T(8,128)S(1)} custom-call(s32[9]{0:T(128)S(1)} %stack.36.id_ref, s32[1,256]{1,0:T(1,128)S(1)} %copy-done.2, s32[1,256]{1,0:T(1,128)S(1)} %bitcast.28, s32[1,256]{1,0:T(1,128)S(1)} %copy-done.4, f32[1,256]{1,0:T(1,128)S(1)} %copy-done.5, f32[1,256]{1,0:T(1,128)S(1)} %copy-done.6, f32[448,128]{1,0:T(8,128)S(1)} %bitcast.21, ...), custom_call_target="tpu_custom_call" | custom-call | flops 528482304 | bytes 2064384 | tf_op jit(solution)/shard_map/ties/pallas_call | solution.py:235
  64.1 7.3 %solve.5 = f32[2,1,7,32,768]{4,3,2,1,0:T(8,128)} custom-call(s32[1]{0:T(128)} %bitcast.rank_ref, f32[2,1,7,32,768]{4,3,2,1,0:T(8,128)S(1)} %copy-done, f32[2,1,7,32,768]{4,3,2,1,0:T(8,128)S(1)} %copy-done.1, bf16[2,1,7,768,768]{4,3,2,1,0:T(8,128)(2,1)} %refs_2_.5, f32[8,768]{1,0:T(8,128)S(1)} %levels.1.refs_3_, ...), custom_call_target="tpu_custom_call", output_to_operand_aliasing={{}: (8, {})} | custom-call | flops 352321536 | bytes 5505024 | tf_op jit(solution)/shard_map/solve/pallas_call | solution.py:327
  (29 shorter events, 0.1 us)
Async XLA Ops:
  2.2 3.2 %copy-start = (f32[2,1,7,32,768]{4,3,2,1,0:T(8,128)S(1)}, f32[2,1,7,32,768]{4,3,2,1,0:T(8,128)}, u32[]{:S(2)}) copy-start(f32[2,1,7,32,768]{4,3,2,1,0:T(8,128)} %refs_0_.5) | copy-start | bytes 4128772
  2.2 13.2 %copy-start.12 = (f32[2,1,7,32,256]{4,3,2,1,0:T(8,128)S(1)}, f32[2,1,7,32,256]{4,3,2,1,0:T(8,128)}, u32[]{:S(2)}) copy-start(f32[2,1,7,32,256]{4,3,2,1,0:T(8,128)} %get-tuple-element.19) | copy-start | bytes 1376260
  2.2 14.7 %copy-start.10 = (bf16[4,256,192]{2,1,0:T(8,128)(2,1)S(1)}, bf16[4,256,192]{2,1,0:T(8,128)(2,1)}, u32[]{:S(2)}) copy-start(bf16[4,256,192]{2,1,0:T(8,128)(2,1)} %constant.68.clone.there_ref) | copy-start | bytes 1179652
  2.2 14.7 %copy-start.11 = (bf16[4,64,256]{2,1,0:T(8,128)(2,1)S(1)}, bf16[4,64,256]{2,1,0:T(8,128)(2,1)}, u32[]{:S(2)}) copy-start(bf16[4,64,256]{2,1,0:T(8,128)(2,1)} %constant.69.clone.back_ref) | copy-start | bytes 393220
  2.3 6.0 %collective-permute-start.15 = (f32[224,256]{1,0:T(8,128)S(1)}, f32[224,256]{1,0:T(8,128)S(1)}, u32[]{:S(2)}, u32[]{:S(2)}) collective-permute-start(f32[224,256]{1,0:T(8,128)S(1)} %bitcast.31), channel_id=1, source_target_pairs={{0,1},{1,0},{2,3},{3,2},{4,5},{5,4},{6,7},{7,6},{8,9},{9,8},{10,11... | collective-permute-start | bytes 688136 | tf_op jit(solution)/shard_map/ppermute | solution.py:379
  2.8 9.0 %collective-permute-start.16 = (f32[224,256]{1,0:T(8,128)S(1)}, f32[224,256]{1,0:T(8,128)S(1)}, u32[]{:S(2)}, u32[]{:S(2)}) collective-permute-start(f32[224,256]{1,0:T(8,128)S(1)} %bitcast.24), channel_id=1, source_target_pairs={{0,2},{1,3},{2,0},{3,1},{4,6},{5,7},{6,4},{7,5},{8,10},{9,11},{10,... | collective-permute-start | bytes 688136 | tf_op jit(solution)/shard_map/ppermute | solution.py:379
  5.4 9.6 %collective-permute-start.5 = (f32[448,128]{1,0:T(8,128)S(1)}, f32[448,128]{1,0:T(8,128)S(1)}, u32[]{:S(2)}, u32[]{:S(2)}) collective-permute-start(f32[448,128]{1,0:T(8,128)S(1)} %bitcast.19), channel_id=1, source_target_pairs={{0,8},{4,12},{8,16},{12,20},{16,24},{20,28},{24,0},{28,4},{1,9},{5... | collective-permute-start | bytes 688136 | tf_op jit(solution)/shard_map/ppermute | solution.py:403
  7.0 9.2 %collective-permute-start.17 = (f32[224,256]{1,0:T(8,128)S(1)}, f32[224,256]{1,0:T(8,128)S(1)}, u32[]{:S(2)}, u32[]{:S(2)}) collective-permute-start(f32[224,256]{1,0:T(8,128)S(1)} %bitcast.32), channel_id=1, source_target_pairs={{0,3},{1,2},{2,1},{3,0},{4,7},{5,6},{6,5},{7,4},{8,11},{9,10},{10,... | collective-permute-start | bytes 688136 | tf_op jit(solution)/shard_map/ppermute | solution.py:379
  7.3 13.4 %collective-permute-start.11 = (f32[224,256]{1,0:T(8,128)S(1)}, f32[224,256]{1,0:T(8,128)S(1)}, u32[]{:S(2)}, u32[]{:S(2)}) collective-permute-start(f32[224,256]{1,0:T(8,128)S(1)} %bitcast.29), channel_id=1, source_target_pairs={{0,1},{1,0},{2,3},{3,2},{4,5},{5,4},{6,7},{7,6},{8,9},{9,8},{10,11... | collective-permute-start | bytes 688136 | tf_op jit(solution)/shard_map/ppermute | solution.py:379
  8.3 20.3 %collective-permute-start.13 = (f32[224,256]{1,0:T(8,128)S(1)}, f32[224,256]{1,0:T(8,128)S(1)}, u32[]{:S(2)}, u32[]{:S(2)}) collective-permute-start(f32[224,256]{1,0:T(8,128)S(1)} %bitcast.30), channel_id=1, source_target_pairs={{0,3},{1,2},{2,1},{3,0},{4,7},{5,6},{6,5},{7,4},{8,11},{9,10},{10,... | collective-permute-start | bytes 688136 | tf_op jit(solution)/shard_map/ppermute | solution.py:379
  11.8 14.7 %collective-permute-start.12 = (f32[224,256]{1,0:T(8,128)S(1)}, f32[224,256]{1,0:T(8,128)S(1)}, u32[]{:S(2)}, u32[]{:S(2)}) collective-permute-start(f32[224,256]{1,0:T(8,128)S(1)} %bitcast.22), channel_id=1, source_target_pairs={{0,2},{1,3},{2,0},{3,1},{4,6},{5,7},{6,4},{7,5},{8,10},{9,11},{10,... | collective-permute-start | bytes 688136 | tf_op jit(solution)/shard_map/ppermute | solution.py:379
  15.0 13.5 %collective-permute-start.7 = (f32[448,128]{1,0:T(8,128)S(1)}, f32[448,128]{1,0:T(8,128)}, u32[]{:S(2)}, u32[]{:S(2)}) collective-permute-start(f32[448,128]{1,0:T(8,128)S(1)} %collective-permute-done.5.refs_2_), channel_id=1, source_target_pairs={{0,8},{4,12},{8,16},{12,20},{16,24},{20,28},{24,0},{28,4},{1,9},{5... | collective-permute-start | bytes 688136 | tf_op jit(solution)/shard_map/ppermute | solution.py:403
  16.2 17.8 %collective-permute-start = (f32[224,256]{1,0:T(8,128)S(1)}, f32[224,256]{1,0:T(8,128)S(1)}, u32[]{:S(2)}, u32[]{:S(2)}) collective-permute-start(f32[224,256]{1,0:T(8,128)S(1)} %bitcast.33), channel_id=1, source_target_pairs={{0,1},{1,0},{2,3},{3,2},{4,5},{5,4},{6,7},{7,6},{8,9},{9,8},{10,11... | collective-permute-start | bytes 688136 | tf_op jit(solution)/shard_map/ppermute | solution.py:379
  20.7 17.2 %collective-permute-start.2 = (f32[224,256]{1,0:T(8,128)S(1)}, f32[224,256]{1,0:T(8,128)S(1)}, u32[]{:S(2)}, u32[]{:S(2)}) collective-permute-start(f32[224,256]{1,0:T(8,128)S(1)} %bitcast.34), channel_id=1, source_target_pairs={{0,3},{1,2},{2,1},{3,0},{4,7},{5,6},{6,5},{7,4},{8,11},{9,10},{10,... | collective-permute-start | bytes 688136 | tf_op jit(solution)/shard_map/ppermute | solution.py:379
  26.6 9.6 %collective-permute-start.1 = (f32[224,256]{1,0:T(8,128)S(1)}, f32[224,256]{1,0:T(8,128)S(1)}, u32[]{:S(2)}, u32[]{:S(2)}) collective-permute-start(f32[224,256]{1,0:T(8,128)S(1)} %bitcast.26), channel_id=1, source_target_pairs={{0,2},{1,3},{2,0},{3,1},{4,6},{5,7},{6,4},{7,5},{8,10},{9,11},{10,... | collective-permute-start | bytes 688136 | tf_op jit(solution)/shard_map/ppermute | solution.py:379
  28.5 9.7 %collective-permute-start.18 = (f32[2,256,128]{2,1,0:T(8,128)S(1)}, f32[2,256,128]{2,1,0:T(8,128)S(1)}, u32[]{:S(2)}, u32[]{:S(2)}) collective-permute-start(f32[2,256,128]{2,1,0:T(8,128)S(1)} %get-tuple-element.16), channel_id=1, source_target_pairs={{0,1},{1,0},{2,3},{3,2},{4,5},{5,4},{6,7},{7,6},{8,9},{9,8},{10,11... | collective-permute-start | bytes 786440 | tf_op jit(solution)/shard_map/ppermute | solution.py:379
  28.6 11.4 %collective-permute-start.9 = (f32[448,128]{1,0:T(8,128)}, f32[448,128]{1,0:T(8,128)}, u32[]{:S(2)}, u32[]{:S(2)}) collective-permute-start(f32[448,128]{1,0:T(8,128)} %collective-permute-done.7.refs_4_), channel_id=1, source_target_pairs={{0,8},{4,12},{8,16},{12,20},{16,24},{20,28},{24,0},{28,4},{1,9},{5... | collective-permute-start | bytes 688136 | tf_op jit(solution)/shard_map/ppermute | solution.py:403
  34.0 11.6 %copy-start.7 = (s32[1,2048]{1,0:T(1,128)S(1)}, s32[1,2048]{1,0:T(1,128)}, u32[]{:S(2)}) copy-start(s32[1,2048]{1,0:T(1,128)} %bus_ref.2) | copy-start | bytes 24580
  34.0 11.6 %copy-start.8 = (f32[1,2048]{1,0:T(1,128)S(1)}, f32[1,2048]{1,0:T(1,128)}, u32[]{:S(2)}) copy-start(f32[1,2048]{1,0:T(1,128)} %cond_ref.1) | copy-start | bytes 24580
  34.0 11.6 %copy-start.9 = (f32[1,2048]{1,0:T(1,128)S(1)}, f32[1,2048]{1,0:T(1,128)}, u32[]{:S(2)}) copy-start(f32[1,2048]{1,0:T(1,128)} %sat_ref.1) | copy-start | bytes 24580
  34.0 10.7 %collective-permute-start.14 = (f32[2,256,128]{2,1,0:T(8,128)S(1)}, f32[2,256,128]{2,1,0:T(8,128)S(1)}, u32[]{:S(2)}, u32[]{:S(2)}) collective-permute-start(f32[2,256,128]{2,1,0:T(8,128)S(1)} %get-tuple-element.14), channel_id=1, source_target_pairs={{0,1},{1,0},{2,3},{3,2},{4,5},{5,4},{6,7},{7,6},{8,9},{9,8},{10,11... | collective-permute-start | bytes 786440 | tf_op jit(solution)/shard_map/ppermute | solution.py:379
  36.2 25.4 %collective-permute-start.4 = (f32[448,128]{1,0:T(8,128)S(1)}, f32[448,128]{1,0:T(8,128)}, u32[]{:S(2)}, u32[]{:S(2)}) collective-permute-start(f32[448,128]{1,0:T(8,128)S(1)} %bitcast.20), channel_id=1, source_target_pairs={{0,4},{4,0},{8,12},{12,8},{16,20},{20,16},{24,28},{28,24},{1,5},{5... | collective-permute-start | bytes 688136 | tf_op jit(solution)/shard_map/ppermute | solution.py:400
  37.9 23.6 %collective-permute-start.6 = (f32[448,128]{1,0:T(8,128)S(1)}, f32[448,128]{1,0:T(8,128)}, u32[]{:S(2)}, u32[]{:S(2)}) collective-permute-start(f32[448,128]{1,0:T(8,128)S(1)} %collective-permute-done.5.refs_2_), channel_id=1, source_target_pairs={{0,4},{4,0},{8,12},{12,8},{16,20},{20,16},{24,28},{28,24},{1,5},{5... | collective-permute-start | bytes 688136 | tf_op jit(solution)/shard_map/ppermute | solution.py:400
  38.2 23.3 %collective-permute-start.8 = (f32[448,128]{1,0:T(8,128)}, f32[448,128]{1,0:T(8,128)}, u32[]{:S(2)}, u32[]{:S(2)}) collective-permute-start(f32[448,128]{1,0:T(8,128)} %collective-permute-done.7.refs_4_), channel_id=1, source_target_pairs={{0,4},{4,0},{8,12},{12,8},{16,20},{20,16},{24,28},{28,24},{1,5},{5... | collective-permute-start | bytes 688136 | tf_op jit(solution)/shard_map/ppermute | solution.py:400
  39.9 21.6 %collective-permute-start.10 = (f32[448,128]{1,0:T(8,128)}, f32[448,128]{1,0:T(8,128)}, u32[]{:S(2)}, u32[]{:S(2)}) collective-permute-start(f32[448,128]{1,0:T(8,128)} %collective-permute-done.9.refs_6_), channel_id=1, source_target_pairs={{0,4},{4,0},{8,12},{12,8},{16,20},{20,16},{24,28},{28,24},{1,5},{5... | collective-permute-start | bytes 688136 | tf_op jit(solution)/shard_map/ppermute | solution.py:400
  44.7 19.4 %collective-permute-start.3 = (f32[2,256,128]{2,1,0:T(8,128)}, f32[2,256,128]{2,1,0:T(8,128)S(1)}, u32[]{:S(2)}, u32[]{:S(2)}) collective-permute-start(f32[2,256,128]{2,1,0:T(8,128)} %get-tuple-element.12), channel_id=1, source_target_pairs={{0,1},{1,0},{2,3},{3,2},{4,5},{5,4},{6,7},{7,6},{8,9},{9,8},{10,11... | collective-permute-start | bytes 786440 | tf_op jit(solution)/shard_map/ppermute | solution.py:379
  45.6 1.3 %copy-start.1 = (f32[2,1,7,32,768]{4,3,2,1,0:T(8,128)S(1)}, f32[2,1,7,32,768]{4,3,2,1,0:T(8,128)}, u32[]{:S(2)}) copy-start(f32[2,1,7,32,768]{4,3,2,1,0:T(8,128)} %refs_1_.5) | copy-start | bytes 4128772
  54.2 7.4 %copy-start.2 = (s32[1,256]{1,0:T(1,128)S(1)}, s32[1,256]{1,0:T(1,128)}, u32[]{:S(2)}) copy-start(s32[1,256]{1,0:T(1,128)} %bus_ref.3) | copy-start | bytes 3076
  54.2 7.4 %copy-start.3 = (s32[1,256,1]{1,2,0:T(1,128)S(1)}, s32[1,256,1]{1,2,0:T(1,128)}, u32[]{:S(2)}) copy-start(s32[1,256,1]{1,2,0:T(1,128)} %param.22) | copy-start | bytes 3076
  54.2 7.4 %copy-start.4 = (s32[1,256]{1,0:T(1,128)S(1)}, s32[1,256]{1,0:T(1,128)}, u32[]{:S(2)}) copy-start(s32[1,256]{1,0:T(1,128)} %far_ref.1) | copy-start | bytes 3076
  54.2 7.4 %copy-start.5 = (f32[1,256]{1,0:T(1,128)S(1)}, f32[1,256]{1,0:T(1,128)}, u32[]{:S(2)}) copy-start(f32[1,256]{1,0:T(1,128)} %res_ref.1) | copy-start | bytes 3076
  54.2 7.4 %copy-start.6 = (f32[1,256]{1,0:T(1,128)S(1)}, f32[1,256]{1,0:T(1,128)}, u32[]{:S(2)}) copy-start(f32[1,256]{1,0:T(1,128)} %reac_ref.1) | copy-start | bytes 3076
where the time goes:
time: 72.1 us; the launch traced here: 71.5 us
  Pallas kernels  37.4 us (52%)
  starting transfers between devices  19 us (26%)
  waiting for transfers between devices  11.3 us (16%)
  local copies, waits for them, and re-layouts  2.83 us (4%)
  between operations  0.96 us (1%)
    pallas_call x3, Pallas kernels, solve(): pl.pallas_call(functools.partial(solve_kernel, scens, h_local, m_pad, sta...  21.8 us
    pallas_call x3, Pallas kernels, wave(): pl.pallas_call(functools.partial(wave_kernel, scens, rows, k_pad, m_pad),...  12.1 us
    ppermute x12, starting transfers between devices, swap(): return lax.ppermute(value, 'harm', [(i, i ^ k) for i in range(ranks)])  11.3 us
    ppermute x12, waiting for transfers between devices, swap(): return lax.ppermute(value, 'harm', [(i, i ^ k) for i in range(ranks)])  10 us
    ppermute x4, starting transfers between devices, per_device(): blocks.append(lax.ppermute(blocks[2 * step], 'area', pairs))  4.06 us
    ppermute x3, starting transfers between devices, per_device(): blocks.append(lax.ppermute(blocks[2 * step], 'area', ring))  3.63 us
    pallas_call x1, Pallas kernels, tie_currents(): pl.pallas_call(functools.partial(tie_kernel, h_local, scens), in_specs=[p...  2.52 us
    slice x1, local copies, waits for them, and re-layouts, per_device(): lanes = volt[..., start:start + width]  2.19 us
  transfers between devices with their start and end apart: 19, of which 5 were waited for; matrix products, arithmetic and copies ran while one was open for 0% of the time, Pallas kernels for 42%

commit v1 on v0

v1 whole, which is shorter than its diff:
```python
import functools

import jax
import jax.numpy as jnp
import numpy as np
from jax import lax
from jax.experimental import pallas as pl
from jax.experimental.pallas import tpu as pltpu
from jax.sharding import PartitionSpec as P

TS = 512
HALF = TS // 2
NBD = 128
LANES = 128
BF16 = jnp.bfloat16
F32 = jnp.float32
NT_DIMS = (((1,), (1,)), ((), ()))
VMEM_BYTES = 10 * 1024 * 1024
SMALL = pl.CostEstimate(flops=1000, bytes_accessed=1000, transcendentals=0)


def up(value, step):
    return -(-value // step) * step


def split(value):
    high = value.astype(BF16)
    return high, (value - high.astype(F32)).astype(BF16)


def np_split(value):
    value = np.asarray(value, np.float32)
    high = value.astype(jnp.bfloat16)
    return high, (value - high.astype(np.float32)).astype(jnp.bfloat16)


def chunk_sizes(buses):
    last = 256 if buses > 256 else buses
    return [buses - last, last] if buses > last else [last]


def after(value, *others):
    return lax.optimization_barrier((value, *others))[0] if others else value


def wave_tables(ranks, h_local):
    order_count = ranks * h_local
    samples = np.arange(HALF)[:, None]
    orders = 2 * np.arange(order_count)[None, :] + 1
    angles = (samples * orders % TS) * (2.0 * np.pi / TS)
    cos, sin = np.cos(angles), np.sin(angles)
    rows = 2 * h_local
    k_pad = up(ranks * rows, 16)
    m_pad = up(rows, 8)
    forward, inverse = [], []
    for rank in range(ranks):
        there = np.zeros((HALF, k_pad))
        back = np.zeros((ranks * m_pad, HALF))
        for k in range(ranks):
            own = slice((rank ^ k) * h_local, ((rank ^ k) + 1) * h_local)
            part = np.concatenate([cos[:, own], -sin[:, own]], axis=1)
            there[:, k * rows : (k + 1) * rows] = 2.0 * part
            back[k * m_pad : k * m_pad + rows] = (4.0 / TS) * part.T
        high, low = np_split(there)
        forward.append(np.concatenate([high, high, low], axis=1))
        high, low = np_split(back)
        inverse.append(np.concatenate([high, low], axis=0))
    return np.stack(forward), np.stack(inverse), k_pad, m_pad


def wave_kernel(
    source_count, start, m_pad, has_fetch, rank_ref, there_ref, back_ref, *refs
):
    refs = list(refs)
    fetch = None
    if has_fetch:
        fetch = pltpu.make_async_copy(
            refs.pop(source_count).at[1], refs.pop(-5), refs.pop()
        )
    sources, outs = refs[:source_count], refs[source_count:-3]
    buf, shapes, sems = refs[-3:]
    ranks = len(outs)
    columns, k_pad, scens, _ = buf.shape
    rows = outs[0].shape[1] // scens
    mine = pl.ds(pl.multiple_of(rank_ref[0] * scens, 8), scens)
    copies = []
    used = 0
    for k, source in enumerate(sources):
        into = pl.ds(used, source.shape[0])
        used += source.shape[0]
        for j in range(columns):
            rows_at = mine if source.shape[1] > scens else pl.ds(0, scens)
            part = source.at[:, rows_at, pl.ds(start + j * LANES, LANES)]
            copy = pltpu.make_async_copy(part, buf.at[j, into], sems.at[k, j])
            copy.start()
            copies.append(copy)
    if fetch is not None:
        fetch.start()
    if k_pad > used:
        buf[:, pl.ds(used, k_pad - used)] = jnp.zeros(
            (columns, k_pad - used, scens, LANES), F32
        )
    for copy in copies:
        copy.wait()
    flat = buf.reshape(columns, k_pad * scens, LANES)
    for s in range(scens):
        volts = [flat[j, pl.ds(s, k_pad, stride=scens), :] for j in range(columns)]
        high, low = split(jnp.concatenate(volts, axis=1))
        stacked = jnp.concatenate([high, low, high], axis=0)
        wave = jnp.dot(there_ref[...], stacked, preferred_element_type=F32)
        shapes[s] = jnp.tanh(wave.astype(BF16))
    for s in range(scens):
        out = jnp.dot(back_ref[...], shapes[s], preferred_element_type=F32)
        out = out[: ranks * m_pad] + out[ranks * m_pad :]
        for k in range(ranks):
            for j in range(columns):
                outs[k][j, pl.ds(s, rows, stride=scens), :] = out[
                    k * m_pad : k * m_pad + rows, j * LANES : (j + 1) * LANES
                ]
    if fetch is not None:
        fetch.wait()


def wave(rank, tables, m_pad, sources, scens, start, width, fetch):
    rows = sources[0].shape[0]
    ranks = sum(source.shape[0] for source in sources) // rows
    columns = width // LANES
    k_pad = tables[0].shape[1] // 3
    fetches = [] if fetch is None else [fetch]
    vmem = pl.BlockSpec(memory_space=pltpu.VMEM)
    shape = jax.ShapeDtypeStruct((columns, rows * scens, LANES), F32)
    return pl.pallas_call(
        functools.partial(
            wave_kernel, len(sources), start, m_pad, fetch is not None
        ),
        in_specs=[pl.BlockSpec(memory_space=pltpu.SMEM), vmem, vmem]
        + [pl.BlockSpec(memory_space=pl.ANY)] * (len(sources) + len(fetches)),
        out_specs=[vmem] * (ranks + len(fetches)),
        out_shape=[pltpu.VMEM(shape.shape, F32)]
        + [shape] * (ranks - 1)
        + [pltpu.VMEM(each.shape[1:], each.dtype) for each in fetches],
        scratch_shapes=[
            pltpu.VMEM((columns, k_pad, scens, LANES), F32),
            pltpu.VMEM((scens, HALF, width), BF16),
            pltpu.SemaphoreType.DMA((len(sources), columns)),
        ]
        + [pltpu.SemaphoreType.DMA for _ in fetches],
        compiler_params=pltpu.CompilerParams(vmem_limit_bytes=VMEM_BYTES),
        cost_estimate=SMALL,
        name="wave",
    )(rank, *tables, *sources, *fetches)


def level_kernel(
    step,
    rank_ref,
    count_ref,
    bus_hbm,
    cond_hbm,
    sat_hbm,
    volt_hbm,
    inject_hbm,
    there_ref,
    back_ref,
    zinv_ref,
    base_ref,
    sat_out,
    there_out,
    back_out,
    zinv_out,
    bus_ref,
    cond_ref,
    sat_ref,
    volt_ref,
    inject_ref,
    sems,
):
    pairs = [
        (bus_hbm, bus_ref),
        (cond_hbm, cond_ref),
        (sat_hbm, sat_ref),
        (volt_hbm, volt_ref),
        (inject_hbm, inject_ref),
        (there_ref.at[rank_ref[0]], there_out),
        (back_ref.at[rank_ref[0]], back_out),
        (zinv_ref.at[0], zinv_out),
    ]
    copies = [
        pltpu.make_async_copy(*pair, sems.at[q]) for q, pair in enumerate(pairs)
    ]
    for copy in copies:
        copy.start()
    for copy in copies[:3]:
        copy.wait()
    slots = bus_ref.shape[1]
    buses = volt_ref.shape[-1]
    total = jnp.zeros((16, buses), F32)
    for start in range(0, slots, step):
        at = pl.ds(start, step)
        slot_ids = lax.broadcasted_iota(jnp.int32, (1, step), 1) + start
        live = slot_ids < count_ref[0]
        pieces = []
        for ref in (cond_ref, sat_ref):
            rest = jnp.where(live, ref[:, at], 0.0)
            for _ in range(3):
                high = rest.astype(BF16).astype(F32)
                pieces.append(high)
                rest = rest - high
        pieces.append(jnp.zeros((10, step), F32))
        weights = jnp.concatenate(pieces, axis=0).astype(BF16)
        bus_ids = lax.broadcasted_iota(jnp.int32, (buses, step), 0)
        onehot = jnp.where(bus_ids == bus_ref[:, at], 1.0, 0.0).astype(BF16)
        total += lax.dot_general(
            weights, onehot, NT_DIMS, preferred_element_type=F32
        )
    cond = total[0:1] + total[1:2] + total[2:3]
    sat = total[3:4] + total[4:5] + total[5:6]
    sat_out[...] = jnp.broadcast_to(sat, sat_out.shape)
    for copy in copies[3:5]:
        copy.wait()
    for row in range(volt_ref.shape[0]):
        base_ref[row] = inject_ref[row] + cond * volt_ref[row]
    for copy in copies[5:]:
        copy.wait()


def levels(rank, dev_count, dev_bus, dev_cond, dev_sat, volt, inject, tables, zinv):
    slots = dev_bus.shape[1]
    buses = volt.shape[-1]
    step = 512 if slots % 512 == 0 else slots
    vmem = pl.BlockSpec(memory_space=pltpu.VMEM)
    smem = pl.BlockSpec(memory_space=pltpu.SMEM)
    anywhere = pl.BlockSpec(memory_space=pl.ANY)
    there, back = tables
    inputs = [
        pltpu.with_memory_space_constraint(each, pltpu.HBM)
        for each in (dev_bus, dev_cond, dev_sat, volt, inject, there, back)
    ] + [zinv]
    return pl.pallas_call(
        functools.partial(level_kernel, step),
        in_specs=[smem] * 2 + [anywhere] * len(inputs),
        out_specs=[vmem] * 5,
        out_shape=[
            pltpu.VMEM(volt.shape, F32),
            pltpu.VMEM((8, buses), F32),
            pltpu.VMEM(there.shape[1:], BF16),
            pltpu.VMEM(back.shape[1:], BF16),
            pltpu.VMEM(zinv.shape[1:], BF16),
        ],
        scratch_shapes=[pltpu.VMEM(each.shape, each.dtype) for each in inputs[:5]]
        + [pltpu.SemaphoreType.DMA((len(inputs),))],
        compiler_params=pltpu.CompilerParams(vmem_limit_bytes=VMEM_BYTES),
        cost_estimate=SMALL,
        name="levels",
    )(rank, dev_count, *inputs)


def tie_kernel(
    h_local, scens, areas, shifts, place_ref, *refs
):
    lists, blocks, out_ref = refs[:5], refs[5:-9], refs[-9]
    bus_ref, area_ref, far_ref, res_ref, reac_ref = refs[-8:-3]
    scaled, held, sems = refs[-3:]
    list_copies = []
    for q, pair in enumerate(zip(lists, refs[-8:-3])):
        copy = pltpu.make_async_copy(*pair, sems.at[len(blocks) + q])
        copy.start()
        list_copies.append(copy)
    copies = []
    for q, block in enumerate(blocks):
        copy = pltpu.make_async_copy(block, held.at[q], sems.at[q])
        copy.start()
        copies.append(copy)
    for copy in list_copies:
        copy.wait()
    ties = bus_ref.shape[1]
    edge_ids = lax.broadcasted_iota(jnp.int32, (NBD, ties), 0)
    far_hit = edge_ids == far_ref[...]
    far = jnp.zeros((2 * h_local * scens, ties), F32)

    def origin(q):
        ringed = (place_ref[1] + areas - shifts[q // 2]) % areas
        return ringed ^ 1 if q % 2 else ringed

    for first in range(0, len(blocks), 2):
        pair = range(first, min(first + 2, len(blocks)))
        for q in pair:
            copies[q].wait()
        parts = [split(held[q]) for q in pair]
        onehot = jnp.concatenate(
            [
                jnp.where(far_hit & (area_ref[...] == origin(q)), 1.0, 0.0)
                for q in pair
            ],
            axis=0,
        ).astype(BF16)
        for piece in range(2):
            edges = jnp.concatenate([part[piece] for part in parts], axis=1)
            far += jnp.dot(edges, onehot, preferred_element_type=F32)
    resist = res_ref[...]
    imag_rows = h_local * scens
    for h in range(h_local):
        order = (2 * (place_ref[0] * h_local + h) + 1).astype(F32)
        reactance = reac_ref[...] * order
        denominator = resist * resist + reactance * reactance
        adm_real = resist / denominator
        adm_imag = -reactance / denominator
        real = far[h * scens : (h + 1) * scens]
        imag = far[imag_rows + h * scens : imag_rows + (h + 1) * scens]
        scaled[pl.ds(h * scens, scens), :] = adm_real * real - adm_imag * imag
        scaled[pl.ds(imag_rows + h * scens, scens), :] = (
            adm_real * imag + adm_imag * real
        )
    target = jnp.where(edge_ids == bus_ref[...], 1.0, 0.0).astype(BF16)
    high, low = split(scaled[...])
    out_ref[...] = lax.dot_general(
        high, target, NT_DIMS, preferred_element_type=F32
    ) + lax.dot_general(low, target, NT_DIMS, preferred_element_type=F32)


def tie_currents(place, tie_lists, blocks, areas, shifts, h_local, scens):
    ties = tie_lists[0].shape[1]
    rows = 2 * h_local * scens
    vmem = pl.BlockSpec(memory_space=pltpu.VMEM)
    return pl.pallas_call(
        functools.partial(tie_kernel, h_local, scens, areas, shifts),
        in_specs=[pl.BlockSpec(memory_space=pltpu.SMEM)]
        + [pl.BlockSpec(memory_space=pl.ANY)] * (len(tie_lists) + len(blocks)),
        out_specs=vmem,
        out_shape=pltpu.VMEM((rows, NBD), F32),
        scratch_shapes=[pltpu.VMEM(each.shape, each.dtype) for each in tie_lists]
        + [
            pltpu.VMEM((rows, ties), F32),
            pltpu.VMEM((len(blocks), rows, NBD), F32),
            pltpu.SemaphoreType.DMA((len(blocks) + len(tie_lists),)),
        ],
        compiler_params=pltpu.CompilerParams(vmem_limit_bytes=VMEM_BYTES),
        cost_estimate=SMALL,
        name="ties",
    )(place, *tie_lists, *blocks)


def solve_kernel(start, width, has_tie, has_total, ranks, rank_ref, *refs):
    refs = list(refs)
    base_ref, sat_ref, real_ref, imag_ref = refs[:4]
    shaped_refs = refs[4 : 4 + ranks]
    del refs[: 4 + ranks]
    tie_ref = refs.pop(0) if has_tie else None
    total_ref = refs.pop(0) if has_total else None
    out_ref, full = refs[:2]
    refs = refs[2:]
    lanes = pl.ds(start, width)
    stage, sem = refs if has_total else (out_ref, None)
    _, h_local, scens, _ = base_ref.shape
    columns = shaped_refs[0].shape[0]
    part = scens // ranks
    for k, ref in enumerate(shaped_refs):
        quarter = pl.ds(pl.multiple_of((rank_ref[0] ^ k) * part, 8), part)
        for j in range(columns):
            at = pl.ds(j * LANES, LANES)
            for row in range(2 * h_local):
                full[row, quarter, at] = ref[j, pl.ds(row * part, part), :]
    sat = sat_ref[0:1, lanes]
    copies = []
    for h in range(h_local):
        parts = []
        for c in range(2):
            rhs = base_ref[c, h, :, lanes] + sat * full[c * h_local + h]
            if has_tie:
                ties = tie_ref[c, h]
                if width > NBD:
                    rhs = jnp.concatenate([rhs[:, :NBD] + ties, rhs[:, NBD:]], axis=1)
                else:
                    rhs = rhs + ties
            parts.append(rhs.astype(BF16))
        both = jnp.concatenate(parts, axis=0)
        by_real = lax.dot_general(
            both, real_ref[h, :, lanes], NT_DIMS, preferred_element_type=F32
        )
        by_imag = lax.dot_general(
            both, imag_ref[h, :, lanes], NT_DIMS, preferred_element_type=F32
        )
        real = by_real[:scens] - by_imag[scens:]
        imag = by_real[scens:] + by_imag[:scens]
        if has_total:
            real = real + total_ref[0, h]
            imag = imag + total_ref[1, h]
        stage[0, h] = real
        stage[1, h] = imag
        if sem is not None:
            copy = pltpu.make_async_copy(stage.at[:, h], out_ref.at[:, h], sem.at[h])
            copy.start()
            copies.append(copy)
    for copy in copies:
        copy.wait()


def solve(rank, base, sat, zinvs, shaped, tie, total, start, width):
    _, h_local, scens, _ = base.shape
    ranks = len(shaped)
    vmem = pl.BlockSpec(memory_space=pltpu.VMEM)
    operands = [base, sat, *zinvs] + list(shaped)
    operands += [tie] if tie is not None else []
    operands += [total] if total is not None else []
    scratch = [pltpu.VMEM((2 * h_local, scens, width), F32)]
    out_spec = vmem
    if total is not None:
        out_spec = pl.BlockSpec(memory_space=pl.ANY)
        scratch += [
            pltpu.VMEM(base.shape, F32),
            pltpu.SemaphoreType.DMA((h_local,)),
        ]
    return pl.pallas_call(
        functools.partial(
            solve_kernel, start, width, tie is not None, total is not None, ranks
        ),
        in_specs=[pl.BlockSpec(memory_space=pltpu.SMEM), vmem, vmem]
        + [vmem] * (len(operands) - 2),
        out_specs=out_spec,
        out_shape=jax.ShapeDtypeStruct(base.shape, F32),
        scratch_shapes=scratch,
        compiler_params=pltpu.CompilerParams(vmem_limit_bytes=VMEM_BYTES),
        cost_estimate=SMALL,
        name="solve",
    )(rank, *operands)


def per_device(
    volt,
    inject,
    zinv,
    dev_bus,
    dev_count,
    dev_cond,
    dev_sat,
    tie_bus,
    tie_area,
    tie_far,
    tie_res,
    tie_reac,
):
    _, _, h_local, scens, buses = volt.shape
    ranks = lax.axis_size("harm")
    areas = lax.axis_size("area")
    rank = lax.axis_index("harm")
    area = lax.axis_index("area")
    part = scens // ranks
    rows = 2 * h_local
    place = jnp.stack([rank, area]).astype(jnp.int32)
    there, back, _, m_pad = wave_tables(ranks, h_local)
    zinv = pltpu.with_memory_space_constraint(zinv[:, 0], pltpu.HBM)
    flat = volt.reshape(rows, scens, buses)

    def swap(value, k):
        return lax.ppermute(value, "harm", [(i, i ^ k) for i in range(ranks)])

    sizes = chunk_sizes(buses)
    starts = [buses - sum(sizes[: i + 1]) for i in range(len(sizes))]

    def piece(k):
        at = (0, (rank ^ k) * part, 0)
        return lax.dynamic_slice(flat, at, (rows, part, buses))

    pieces = [piece(k) for k in range(ranks - 1, 1, -1)]
    flat_now, *pieces = lax.optimization_barrier((flat, *pieces))
    far = [swap(each, ranks - 1 - q) for q, each in enumerate(pieces)]
    sibling = swap(flat_now, 1)
    sources = [flat, sibling] + far[::-1]

    edge = volt[..., :NBD].reshape(rows * scens, NBD)

    def shift(value, step):
        return lax.ppermute(
            value, "area", [(a, (a + step) % areas) for a in range(areas)]
        )

    def exchange(value):
        return lax.ppermute(value, "area", [(a, a ^ 1) for a in range(areas)])

    edge = after(edge, *pieces)
    blocks = [edge, exchange(edge)]
    base, sat, there, back, zinv_real = levels(
        place,
        dev_count,
        after(dev_bus, sibling),
        dev_cond,
        dev_sat,
        flat,
        inject.reshape(flat.shape),
        (jnp.asarray(there), jnp.asarray(back)),
        zinv,
    )
    def run_wave(index):
        return wave(
            place,
            (there, back),
            m_pad,
            sources,
            part,
            starts[index],
            sizes[index],
            zinv if index == len(sizes) - 1 else None,
        )

    waves = [list(run_wave(index)) for index in range(len(sizes))]
    zinv_imag = waves[-1].pop()
    shaped = [
        [outs[0]] + [swap(outs[k], k) for k in range(1, ranks)] for outs in waves
    ]
    ring = {2: shift(edge, 2)}
    if areas > 4:
        ring[areas - 2] = shift(edge, areas - 2)
    for step in range(4, areas - 2, 2):
        ring[step] = shift(after(ring[step - 2], sat), 2)
    shifts = [0]
    for step, block in ring.items():
        if step == 2:
            needs = [blocks[-1], far[0], sat]
        else:
            needs = blocks[-1:] if step == areas - 2 else [waves[-1][0]]
        blocks += [block, exchange(after(block, *needs))]
        shifts.append(step)
    base = base.reshape(2, h_local, scens, buses)
    tie_lists = [
        tie_bus,
        tie_area[:, :, 0],
        tie_far,
        tie_res,
        tie_reac,
    ]
    tie_lists = [pltpu.with_memory_space_constraint(t, pltpu.HBM) for t in tie_lists]
    tie = tie_currents(place, tie_lists, blocks, areas, shifts, h_local, scens)
    tie = tie.reshape(2, h_local, scens, NBD)

    total = None
    for start, width, parts in zip(starts, sizes, shaped):
        total = solve(
            place,
            base,
            sat,
            (zinv_real, zinv_imag),
            parts,
            tie if start == 0 else None,
            total,
            start,
            width,
        )
    return total[:, None]


def solution(mesh):
    wide = P(None, "area", "harm", None, None)
    flat = P("area", None)
    in_specs = (
        wide,
        wide,
        wide,
        flat,
        P("area"),
        flat,
        flat,
        flat,
        P("area", None, None),
        flat,
        flat,
        flat,
    )
    return jax.shard_map(
        per_device, mesh=mesh, in_specs=in_specs, out_specs=wide, check_vma=False
    )
```

time: 72.1 us -> 50.5 us (0.70)
  Pallas kernels: 37.4 us -> 22 us
  waiting for transfers between devices: 11.3 us -> 5.04 us
    pallas_call x8 -> x6, Pallas kernels: 37.4 us -> 22 us  [the longest x2 7.15 us: solve(): pl.pallas_call(functools.partial(solve_kernel, start, width, tie is not N...]
    ppermute x12 -> x9, waiting for transfers between devices: 10 us -> 2.8 us  [swap(): return lax.ppermute(value, 'harm', [(i, i ^ k) for i in range(ranks)])]
    ppermute x7, starting transfers between devices: 7.69 us -> 10.5 us  [the longest x3 5.4 us: shift(): lax.ppermute(value, 'area', [(a, (a + step) % areas) for a in range(areas)])]
    slice x1 -> x0, local copies, waits for them, and re-layouts: 2.19 us -> none  [per_device(): lanes = volt[..., start:start + width]]
    ppermute x12 -> x9, starting transfers between devices: 11.3 us -> 9.17 us  [swap(): return lax.ppermute(value, 'harm', [(i, i ^ k) for i in range(ranks)])]
    dynamic_slice x2 -> x1, local copies, waits for them, and re-layouts: 0.1 us -> 2.08 us  [piece(): return lax.dynamic_slice(flat, at, (rows, part, buses))]
    ppermute x7, waiting for transfers between devices: 1.22 us -> 2.24 us  [the longest x3 1.28 us: shift(): lax.ppermute(value, 'area', [(a, (a + step) % areas) for a in range(areas)])]
  transfers between devices with their start and end apart: 19 -> 16, of which waited for: 5 -> 5; matrix products, arithmetic and copies ran while one was open for 0% -> 2% of each run, Pallas kernels for 42% -> 38%
where the time goes in v1:
time: 50.5 us; the launch traced here: 50.3 us
  Pallas kernels  22 us (44%)
  starting transfers between devices  19.6 us (39%)
  waiting for transfers between devices  5.04 us (10%)
  local copies, waits for them, and re-layouts  2.8 us (6%)
  between operations  0.76 us (2%)
    ppermute x9, starting transfers between devices, swap(): return lax.ppermute(value, 'harm', [(i, i ^ k) for i in range(ranks)])  9.17 us
    pallas_call x2, Pallas kernels, solve(): pl.pallas_call(functools.partial(solve_kernel, start, width, tie is not N...  7.15 us
    pallas_call x2, Pallas kernels, wave(): pl.pallas_call(functools.partial(wave_kernel, len(sources), start, m_pad,...  6.24 us
    ppermute x3, starting transfers between devices, shift(): lax.ppermute(value, 'area', [(a, (a + step) % areas) for a in range(areas)])  5.4 us
    ppermute x4, starting transfers between devices, exchange(): return lax.ppermute(value, 'area', [(a, a ^ 1) for a in range(areas)])  5.08 us
    pallas_call x1, Pallas kernels, levels(): pl.pallas_call(functools.partial(level_kernel, step), in_specs=[smem] * 2...  4.9 us
    pallas_call x1, Pallas kernels, tie_currents(): pl.pallas_call(functools.partial(tie_kernel, h_local, scens, areas, shift...  3.73 us
    ppermute x9, waiting for transfers between devices, swap(): return lax.ppermute(value, 'harm', [(i, i ^ k) for i in range(ranks)])  2.8 us
  transfers between devices with their start and end apart: 16, of which 5 were waited for; matrix products, arithmetic and copies ran while one was open for 2% of the time, Pallas kernels for 38%

profile of v1, /device:TPU:0, one launch (start us, length us, event | category | flops | bytes accessed | tf_op | source)
XLA Modules:
  0.0 50.3 jit_solution(14758193583457947537)
XLA Ops:
  0.0 0.0 copy-start
  0.0 2.1 %constant_dynamic-slice_fusion = (f32[14,8,768]{2,1,0:T(8,128)}, f32[14,8,768]{2,1,0:T(8,128)}) fusion(f32[14,32,768]{2,1,0:T(8,128)} %bitcast.12, s32[]{:T(128)S(6)} %select_n.7, s32[]{:T(128)S(6)} %select_n.6), kind=kLoop, calls=%fused_computation.1 | loop fusion | bytes 1376264 | tf_op jit(solution)/shard_map/dynamic_slice | solution.py:462
  2.1 0.0 copy-done
  2.1 0.5 collective-permute-start
  2.5 2.6 %collective-permute-start.2 = (f32[14,8,768]{2,1,0:T(8,128)}, f32[14,8,768]{2,1,0:T(8,128)S(1)}, u32[]{:S(2)}, u32[]{:S(2)}) collective-permute-start(f32[14,8,768]{2,1,0:T(8,128)} %get-tuple-element.36), channel_id=1, source_target_pairs={{0,3},{1,2},{2,1},{3,0},{4,7},{5,6},{6,5},{7,4},{8,11},{9,10},{10,... | collective-permute-start | bytes 1032200 | tf_op jit(solution)/shard_map/ppermute | solution.py:455
  5.2 0.7 %slice.3 = f32[2,1,7,32,128]{4,3,2,1,0:T(8,128)} slice(f32[2,1,7,32,768]{4,3,2,1,0:T(8,128)S(1)} %copy-done), slice={[0:2], [0:1], [0:7], [0:32], [0:128]} | slice | bytes 458752 | tf_op jit(solution)/shard_map/slice | solution.py:470
  5.9 1.6 %collective-permute-start.7 = (f32[448,128]{1,0:T(8,128)}, f32[448,128]{1,0:T(8,128)}, u32[]{:S(2)}, u32[]{:S(2)}) collective-permute-start(f32[448,128]{1,0:T(8,128)} %bitcast.7.refs_5_), channel_id=1, source_target_pairs={{0,8},{4,12},{8,16},{12,20},{16,24},{20,28},{24,0},{28,4},{1,9},{5... | collective-permute-start | bytes 688136 | tf_op jit(solution)/shard_map/ppermute | solution.py:473
  7.5 1.5 %collective-permute-start.6 = (f32[448,128]{1,0:T(8,128)}, f32[448,128]{1,0:T(8,128)}, u32[]{:S(2)}, u32[]{:S(2)}) collective-permute-start(f32[448,128]{1,0:T(8,128)} %bitcast.7.refs_5_), channel_id=1, source_target_pairs={{0,4},{4,0},{8,12},{12,8},{16,20},{20,16},{24,28},{28,24},{1,5},{5... | collective-permute-start | bytes 688136 | tf_op jit(solution)/shard_map/ppermute | solution.py:478
  8.9 0.5 %collective-permute-start.1 = (f32[14,8,768]{2,1,0:T(8,128)}, f32[14,8,768]{2,1,0:T(8,128)S(1)}, u32[]{:S(2)}, u32[]{:S(2)}) collective-permute-start(f32[14,8,768]{2,1,0:T(8,128)} %get-tuple-element.35), channel_id=1, source_target_pairs={{0,2},{1,3},{2,0},{3,1},{4,6},{5,7},{6,4},{7,5},{8,10},{9,11},{10,... | collective-permute-start | bytes 1032200 | tf_op jit(solution)/shard_map/ppermute | solution.py:455
  10.1 0.1 pad_add_fusion.rank_ref.place_ref
  10.2 0.0 collective-permute-done.refs_1_
  10.2 0.0 copy-start.1
  10.2 4.9 %levels.1 = (f32[14,32,768]{2,1,0:T(8,128)S(1)}, f32[8,768]{1,0:T(8,128)S(1)}, bf16[256,192]{1,0:T(8,128)(2,1)S(1)}, bf16[128,256]{1,0:T(8,128)(2,1)S(1)}, bf16[7,768,768]{2,1,0:T(8,128)(2,1)S(1)}) custom-call(s32[2]{0:T(128)S(1)} %pad_add_fusion.rank_ref.place_ref, s32[1]{0:T(128)S(6)} %copy.16.count_ref, s32[1,2048]{1,0:T(1,128)} %bus_hbm, ...), custom_call_target="tpu_custom_call" | custom-call | flops 1000 | bytes 1000 | tf_op jit(solution)/shard_map/levels/pallas_call | solution.py:239
  15.1 0.5 %collective-permute-done.7.refs_7_ = f32[448,128]{1,0:T(8,128)} collective-permute-done((f32[448,128]{1,0:T(8,128)}, f32[448,128]{1,0:T(8,128)}, u32[]{:S(2)}, u32[]{:S(2)}) %collective-permute-start.7) | collective-permute-done | bytes 229408 | tf_op jit(solution)/shard_map/ppermute | solution.py:473
  15.6 1.1 %collective-permute-start.11 = (f32[448,128]{1,0:T(8,128)}, f32[448,128]{1,0:T(8,128)S(1)}, u32[]{:S(2)}, u32[]{:S(2)}) collective-permute-start(f32[448,128]{1,0:T(8,128)} %collective-permute-done.7.refs_7_), channel_id=1, source_target_pairs={{0,8},{4,12},{8,16},{12,20},{16,24},{20,28},{24,0},{28,4},{1,9},{5... | collective-permute-start | bytes 688136 | tf_op jit(solution)/shard_map/ppermute | solution.py:473
  16.7 2.7 %collective-permute-start.9 = (f32[448,128]{1,0:T(8,128)}, f32[448,128]{1,0:T(8,128)S(1)}, u32[]{:S(2)}, u32[]{:S(2)}) collective-permute-start(f32[448,128]{1,0:T(8,128)} %bitcast.7.refs_5_), channel_id=1, source_target_pairs={{0,24},{4,28},{8,0},{12,4},{16,8},{20,12},{24,16},{28,20},{1,25},{... | collective-permute-start | bytes 688136 | tf_op jit(solution)/shard_map/ppermute | solution.py:473
  19.4 0.0 collective-permute-done.6.refs_6_
  19.4 0.0 collective-permute-done.2.refs_3_
  19.4 1.5 %collective-permute-start.8 = (f32[448,128]{1,0:T(8,128)}, f32[448,128]{1,0:T(8,128)S(1)}, u32[]{:S(2)}, u32[]{:S(2)}) collective-permute-start(f32[448,128]{1,0:T(8,128)} %collective-permute-done.7.refs_7_), channel_id=1, source_target_pairs={{0,4},{4,0},{8,12},{12,8},{16,20},{20,16},{24,28},{28,24},{1,5},{5... | collective-permute-start | bytes 688136 | tf_op jit(solution)/shard_map/ppermute | solution.py:478
  20.9 0.5 collective-permute-done.1.refs_2_
  21.4 0.0 copy-done.1
  21.4 2.2 %wave.3 = (f32[4,112,128]{2,1,0:T(8,128)S(1)}, f32[4,112,128]{2,1,0:T(8,128)S(1)}, f32[4,112,128]{2,1,0:T(8,128)S(1)}, f32[4,112,128]{2,1,0:T(8,128)S(1)}) custom-call(s32[2]{0:T(128)S(1)} %pad_add_fusion.rank_ref.place_ref, bf16[256,192]{1,0:T(8,128)(2,1)S(1)} %get-tuple-element.33.there_ref, bf16[128,256]{1,0:T(8,128)(2,1)S(1)} %get-tuple-element.34.back_ref, ...), custom_call_target="tpu_custom_call" | custom-call | flops 1000 | bytes 1000 | tf_op jit(solution)/shard_map/wave/pallas_call | solution.py:132
  23.6 0.1 collective-permute-start.13
  23.7 1.7 %collective-permute-start.14 = (f32[4,112,128]{2,1,0:T(8,128)S(1)}, f32[4,112,128]{2,1,0:T(8,128)S(1)}, u32[]{:S(2)}, u32[]{:S(2)}) collective-permute-start(f32[4,112,128]{2,1,0:T(8,128)S(1)} %get-tuple-element.49), channel_id=1, source_target_pairs={{0,2},{1,3},{2,0},{3,1},{4,6},{5,7},{6,4},{7,5},{8,10},{9,11},{10,... | collective-permute-start | bytes 688136 | tf_op jit(solution)/shard_map/ppermute | solution.py:455
  25.4 0.8 %collective-permute-done.11.refs_11_ = f32[448,128]{1,0:T(8,128)S(1)} collective-permute-done((f32[448,128]{1,0:T(8,128)}, f32[448,128]{1,0:T(8,128)S(1)}, u32[]{:S(2)}, u32[]{:S(2)}) %collective-permute-start.11) | collective-permute-done | bytes 229408 | tf_op jit(solution)/shard_map/ppermute | solution.py:473
  26.2 0.0 collective-permute-start.15
  26.2 4.0 %wave.2 = (f32[2,112,128]{2,1,0:T(8,128)S(1)}, f32[2,112,128]{2,1,0:T(8,128)S(1)}, f32[2,112,128]{2,1,0:T(8,128)S(1)}, f32[2,112,128]{2,1,0:T(8,128)S(1)}, bf16[7,768,768]{2,1,0:T(8,128)(2,1)S(1)}) custom-call(s32[2]{0:T(128)S(1)} %pad_add_fusion.rank_ref.place_ref, bf16[256,192]{1,0:T(8,128)(2,1)S(1)} %get-tuple-element.33.there_ref, ...), custom_call_target="tpu_custom_call" | custom-call | flops 1000 | bytes 1000 | tf_op jit(solution)/shard_map/wave/pallas_call | solution.py:132
  30.2 0.0 collective-permute-done.9.refs_9_
  30.2 1.5 %collective-permute-start.12 = (f32[448,128]{1,0:T(8,128)S(1)}, f32[448,128]{1,0:T(8,128)S(1)}, u32[]{:S(2)}, u32[]{:S(2)}) collective-permute-start(f32[448,128]{1,0:T(8,128)S(1)} %collective-permute-done.11.refs_11_), channel_id=1, source_target_pairs={{0,4},{4,0},{8,12},{12,8},{16,20},{20,16},{24,28},{28,24},{1,5},{5... | collective-permute-start | bytes 688136 | tf_op jit(solution)/shard_map/ppermute | solution.py:478
  31.8 0.0 collective-permute-done.8.refs_8_
  31.8 0.6 %collective-permute-start.10 = (f32[448,128]{1,0:T(8,128)S(1)}, f32[448,128]{1,0:T(8,128)S(1)}, u32[]{:S(2)}, u32[]{:S(2)}) collective-permute-start(f32[448,128]{1,0:T(8,128)S(1)} %collective-permute-done.9.refs_9_), channel_id=1, source_target_pairs={{0,4},{4,0},{8,12},{12,8},{16,20},{20,16},{24,28},{28,24},{1,5},{5... | collective-permute-start | bytes 688136 | tf_op jit(solution)/shard_map/ppermute | solution.py:478
  32.3 0.0 collective-permute-done.13.refs_5_
  32.3 0.7 %collective-permute-start.3 = (f32[2,112,128]{2,1,0:T(8,128)S(1)}, f32[2,112,128]{2,1,0:T(8,128)S(1)}, u32[]{:S(2)}, u32[]{:S(2)}) collective-permute-start(f32[2,112,128]{2,1,0:T(8,128)S(1)} %get-tuple-element.39), channel_id=1, source_target_pairs={{0,1},{1,0},{2,3},{3,2},{4,5},{5,4},{6,7},{7,6},{8,9},{9,8},{10,11... | collective-permute-start | bytes 344072 | tf_op jit(solution)/shard_map/ppermute | solution.py:455
  33.0 0.0 collective-permute-done.14.refs_6_
  33.0 0.9 %collective-permute-start.4 = (f32[2,112,128]{2,1,0:T(8,128)S(1)}, f32[2,112,128]{2,1,0:T(8,128)S(1)}, u32[]{:S(2)}, u32[]{:S(2)}) collective-permute-start(f32[2,112,128]{2,1,0:T(8,128)S(1)} %get-tuple-element.40), channel_id=1, source_target_pairs={{0,2},{1,3},{2,0},{3,1},{4,6},{5,7},{6,4},{7,5},{8,10},{9,11},{10,... | collective-permute-start | bytes 344072 | tf_op jit(solution)/shard_map/ppermute | solution.py:455
  33.9 2.3 %collective-permute-done.15.refs_7_ = f32[4,112,128]{2,1,0:T(8,128)S(1)} collective-permute-done((f32[4,112,128]{2,1,0:T(8,128)S(1)}, f32[4,112,128]{2,1,0:T(8,128)S(1)}, u32[]{:S(2)}, u32[]{:S(2)}) %collective-permute-start.15) | collective-permute-done | bytes 229408 | tf_op jit(solution)/shard_map/ppermute | solution.py:455
  36.2 2.2 %collective-permute-start.5 = (f32[2,112,128]{2,1,0:T(8,128)S(1)}, f32[2,112,128]{2,1,0:T(8,128)S(1)}, u32[]{:S(2)}, u32[]{:S(2)}) collective-permute-start(f32[2,112,128]{2,1,0:T(8,128)S(1)} %get-tuple-element.41), channel_id=1, source_target_pairs={{0,3},{1,2},{2,1},{3,0},{4,7},{5,6},{6,5},{7,4},{8,11},{9,10},{10,... | collective-permute-start | bytes 344072 | tf_op jit(solution)/shard_map/ppermute | solution.py:455
  38.4 4.0 %solve.2.refs_9_ = f32[2,7,32,768]{3,2,1,0:T(8,128)S(1)} custom-call(s32[2]{0:T(128)S(1)} %pad_add_fusion.rank_ref.place_ref, f32[2,7,32,768]{3,2,1,0:T(8,128)S(1)} %bitcast.17, f32[8,768]{1,0:T(8,128)S(1)} %get-tuple-element.31.refs_1_, bf16[7,768,768]{2,1,0:T(8,128)(2,1)S(1)} %get-tuple-element.32.refs_2_, ...), custom_call_target="tpu_custom_call" | custom-call | flops 1000 | bytes 1000 | tf_op jit(solution)/shard_map/solve/pallas_call | solution.py:413
  42.5 0.0 collective-permute-done.12.refs_12_
  42.5 0.9 %collective-permute-done.10.refs_10_ = f32[448,128]{1,0:T(8,128)S(1)} collective-permute-done((f32[448,128]{1,0:T(8,128)S(1)}, f32[448,128]{1,0:T(8,128)S(1)}, u32[]{:S(2)}, u32[]{:S(2)}) %collective-permute-start.10) | collective-permute-done | bytes 229408 | tf_op jit(solution)/shard_map/ppermute | solution.py:478
  43.4 3.7 %ties.1 = f32[448,128]{1,0:T(8,128)S(1)} custom-call(s32[2]{0:T(128)S(1)} %pad_add_fusion.rank_ref.place_ref, s32[1,256]{1,0:T(1,128)} %refs_0_.1, s32[1,256]{1,0:T(1,128)} %bitcast.23, s32[1,256]{1,0:T(1,128)} %refs_2_.1, f32[1,256]{1,0:T(1,128)} %refs_3_.1, f32[1,256]{1,0:T(1,128)} %refs_4_.1, f32[448,128]{1,0:T(8,128)} %bitcast.7.refs_5_, ...), custom_call_target="tpu_custom_call" | custom-call | flops 1000 | bytes 1000 | tf_op jit(solution)/shard_map/ties/pallas_call | solution.py:325
  47.2 0.0 collective-permute-done.3.refs_5_
  47.2 0.0 collective-permute-done.4.refs_6_
  47.2 0.0 collective-permute-done.5.refs_7_
  47.2 3.1 %solve.3 = f32[2,7,32,768]{3,2,1,0:T(8,128)} custom-call(s32[2]{0:T(128)S(1)} %pad_add_fusion.rank_ref.place_ref, f32[2,7,32,768]{3,2,1,0:T(8,128)S(1)} %bitcast.18, f32[8,768]{1,0:T(8,128)S(1)} %get-tuple-element.31.refs_1_, bf16[7,768,768]{2,1,0:T(8,128)(2,1)S(1)} %get-tuple-element.32.refs_2_, bf16[7,768,768]{2,1,0:T(8,128)(2,1)S(1)} %get-tuple-element.37.refs_3_, ...), custom_call_target="tpu_custom_call" | custom-call | flops 1000 | bytes 1000 | tf_op jit(solution)/shard_map/solve/pallas_call | solution.py:413
Async XLA Ops:
  0.0 2.1 %copy-start = (f32[2,1,7,32,768]{4,3,2,1,0:T(8,128)S(1)}, f32[2,1,7,32,768]{4,3,2,1,0:T(8,128)}, u32[]{:S(2)}) copy-start(f32[2,1,7,32,768]{4,3,2,1,0:T(8,128)} %param.14) | copy-start | bytes 4128772
  2.1 8.1 %collective-permute-start = (f32[14,32,768]{2,1,0:T(8,128)S(1)}, f32[14,32,768]{2,1,0:T(8,128)S(1)}, u32[]{:S(2)}, u32[]{:S(2)}) collective-permute-start(f32[14,32,768]{2,1,0:T(8,128)S(1)} %bitcast.14), channel_id=1, source_target_pairs={{0,1},{1,0},{2,3},{3,2},{4,5},{5,4},{6,7},{7,6},{8,9},{9,8},{10,11... | collective-permute-start | bytes 4128776 | tf_op jit(solution)/shard_map/ppermute | solution.py:455
  2.5 16.9 %collective-permute-start.2 = (f32[14,8,768]{2,1,0:T(8,128)}, f32[14,8,768]{2,1,0:T(8,128)S(1)}, u32[]{:S(2)}, u32[]{:S(2)}) collective-permute-start(f32[14,8,768]{2,1,0:T(8,128)} %get-tuple-element.36), channel_id=1, source_target_pairs={{0,3},{1,2},{2,1},{3,0},{4,7},{5,6},{6,5},{7,4},{8,11},{9,10},{10,... | collective-permute-start | bytes 1032200 | tf_op jit(solution)/shard_map/ppermute | solution.py:455
  5.9 9.7 %collective-permute-start.7 = (f32[448,128]{1,0:T(8,128)}, f32[448,128]{1,0:T(8,128)}, u32[]{:S(2)}, u32[]{:S(2)}) collective-permute-start(f32[448,128]{1,0:T(8,128)} %bitcast.7.refs_5_), channel_id=1, source_target_pairs={{0,8},{4,12},{8,16},{12,20},{16,24},{20,28},{24,0},{28,4},{1,9},{5... | collective-permute-start | bytes 688136 | tf_op jit(solution)/shard_map/ppermute | solution.py:473
  7.5 12.0 %collective-permute-start.6 = (f32[448,128]{1,0:T(8,128)}, f32[448,128]{1,0:T(8,128)}, u32[]{:S(2)}, u32[]{:S(2)}) collective-permute-start(f32[448,128]{1,0:T(8,128)} %bitcast.7.refs_5_), channel_id=1, source_target_pairs={{0,4},{4,0},{8,12},{12,8},{16,20},{20,16},{24,28},{28,24},{1,5},{5... | collective-permute-start | bytes 688136 | tf_op jit(solution)/shard_map/ppermute | solution.py:478
  8.9 12.4 %collective-permute-start.1 = (f32[14,8,768]{2,1,0:T(8,128)}, f32[14,8,768]{2,1,0:T(8,128)S(1)}, u32[]{:S(2)}, u32[]{:S(2)}) collective-permute-start(f32[14,8,768]{2,1,0:T(8,128)} %get-tuple-element.35), channel_id=1, source_target_pairs={{0,2},{1,3},{2,0},{3,1},{4,6},{5,7},{6,4},{7,5},{8,10},{9,11},{10,... | collective-permute-start | bytes 1032200 | tf_op jit(solution)/shard_map/ppermute | solution.py:455
  10.2 11.2 %copy-start.1 = (f32[2,1,7,32,768]{4,3,2,1,0:T(8,128)S(1)}, f32[2,1,7,32,768]{4,3,2,1,0:T(8,128)}, u32[]{:S(2)}) copy-start(f32[2,1,7,32,768]{4,3,2,1,0:T(8,128)} %param.14) | copy-start | bytes 4128772
  15.6 10.6 %collective-permute-start.11 = (f32[448,128]{1,0:T(8,128)}, f32[448,128]{1,0:T(8,128)S(1)}, u32[]{:S(2)}, u32[]{:S(2)}) collective-permute-start(f32[448,128]{1,0:T(8,128)} %collective-permute-done.7.refs_7_), channel_id=1, source_target_pairs={{0,8},{4,12},{8,16},{12,20},{16,24},{20,28},{24,0},{28,4},{1,9},{5... | collective-permute-start | bytes 688136 | tf_op jit(solution)/shard_map/ppermute | solution.py:473
  16.7 13.5 %collective-permute-start.9 = (f32[448,128]{1,0:T(8,128)}, f32[448,128]{1,0:T(8,128)S(1)}, u32[]{:S(2)}, u32[]{:S(2)}) collective-permute-start(f32[448,128]{1,0:T(8,128)} %bitcast.7.refs_5_), channel_id=1, source_target_pairs={{0,24},{4,28},{8,0},{12,4},{16,8},{20,12},{24,16},{28,20},{1,25},{... | collective-permute-start | bytes 688136 | tf_op jit(solution)/shard_map/ppermute | solution.py:473
  19.4 12.3 %collective-permute-start.8 = (f32[448,128]{1,0:T(8,128)}, f32[448,128]{1,0:T(8,128)S(1)}, u32[]{:S(2)}, u32[]{:S(2)}) collective-permute-start(f32[448,128]{1,0:T(8,128)} %collective-permute-done.7.refs_7_), channel_id=1, source_target_pairs={{0,4},{4,0},{8,12},{12,8},{16,20},{20,16},{24,28},{28,24},{1,5},{5... | collective-permute-start | bytes 688136 | tf_op jit(solution)/shard_map/ppermute | solution.py:478
  23.6 8.7 %collective-permute-start.13 = (f32[4,112,128]{2,1,0:T(8,128)S(1)}, f32[4,112,128]{2,1,0:T(8,128)S(1)}, u32[]{:S(2)}, u32[]{:S(2)}) collective-permute-start(f32[4,112,128]{2,1,0:T(8,128)S(1)} %get-tuple-element.48), channel_id=1, source_target_pairs={{0,1},{1,0},{2,3},{3,2},{4,5},{5,4},{6,7},{7,6},{8,9},{9,8},{10,11... | collective-permute-start | bytes 688136 | tf_op jit(solution)/shard_map/ppermute | solution.py:455
  23.7 9.3 %collective-permute-start.14 = (f32[4,112,128]{2,1,0:T(8,128)S(1)}, f32[4,112,128]{2,1,0:T(8,128)S(1)}, u32[]{:S(2)}, u32[]{:S(2)}) collective-permute-start(f32[4,112,128]{2,1,0:T(8,128)S(1)} %get-tuple-element.49), channel_id=1, source_target_pairs={{0,2},{1,3},{2,0},{3,1},{4,6},{5,7},{6,4},{7,5},{8,10},{9,11},{10,... | collective-permute-start | bytes 688136 | tf_op jit(solution)/shard_map/ppermute | solution.py:455
  26.2 10.1 %collective-permute-start.15 = (f32[4,112,128]{2,1,0:T(8,128)S(1)}, f32[4,112,128]{2,1,0:T(8,128)S(1)}, u32[]{:S(2)}, u32[]{:S(2)}) collective-permute-start(f32[4,112,128]{2,1,0:T(8,128)S(1)} %get-tuple-element.50), channel_id=1, source_target_pairs={{0,3},{1,2},{2,1},{3,0},{4,7},{5,6},{6,5},{7,4},{8,11},{9,10},{10,... | collective-permute-start | bytes 688136 | tf_op jit(solution)/shard_map/ppermute | solution.py:455
  30.2 12.3 %collective-permute-start.12 = (f32[448,128]{1,0:T(8,128)S(1)}, f32[448,128]{1,0:T(8,128)S(1)}, u32[]{:S(2)}, u32[]{:S(2)}) collective-permute-start(f32[448,128]{1,0:T(8,128)S(1)} %collective-permute-done.11.refs_11_), channel_id=1, source_target_pairs={{0,4},{4,0},{8,12},{12,8},{16,20},{20,16},{24,28},{28,24},{1,5},{5... | collective-permute-start | bytes 688136 | tf_op jit(solution)/shard_map/ppermute | solution.py:478
  31.8 11.7 %collective-permute-start.10 = (f32[448,128]{1,0:T(8,128)S(1)}, f32[448,128]{1,0:T(8,128)S(1)}, u32[]{:S(2)}, u32[]{:S(2)}) collective-permute-start(f32[448,128]{1,0:T(8,128)S(1)} %collective-permute-done.9.refs_9_), channel_id=1, source_target_pairs={{0,4},{4,0},{8,12},{12,8},{16,20},{20,16},{24,28},{28,24},{1,5},{5... | collective-permute-start | bytes 688136 | tf_op jit(solution)/shard_map/ppermute | solution.py:478
  32.3 14.9 %collective-permute-start.3 = (f32[2,112,128]{2,1,0:T(8,128)S(1)}, f32[2,112,128]{2,1,0:T(8,128)S(1)}, u32[]{:S(2)}, u32[]{:S(2)}) collective-permute-start(f32[2,112,128]{2,1,0:T(8,128)S(1)} %get-tuple-element.39), channel_id=1, source_target_pairs={{0,1},{1,0},{2,3},{3,2},{4,5},{5,4},{6,7},{7,6},{8,9},{9,8},{10,11... | collective-permute-start | bytes 344072 | tf_op jit(solution)/shard_map/ppermute | solution.py:455
  33.0 14.2 %collective-permute-start.4 = (f32[2,112,128]{2,1,0:T(8,128)S(1)}, f32[2,112,128]{2,1,0:T(8,128)S(1)}, u32[]{:S(2)}, u32[]{:S(2)}) collective-permute-start(f32[2,112,128]{2,1,0:T(8,128)S(1)} %get-tuple-element.40), channel_id=1, source_target_pairs={{0,2},{1,3},{2,0},{3,1},{4,6},{5,7},{6,4},{7,5},{8,10},{9,11},{10,... | collective-permute-start | bytes 344072 | tf_op jit(solution)/shard_map/ppermute | solution.py:455
  36.2 11.0 %collective-permute-start.5 = (f32[2,112,128]{2,1,0:T(8,128)S(1)}, f32[2,112,128]{2,1,0:T(8,128)S(1)}, u32[]{:S(2)}, u32[]{:S(2)}) collective-permute-start(f32[2,112,128]{2,1,0:T(8,128)S(1)} %get-tuple-element.41), channel_id=1, source_target_pairs={{0,3},{1,2},{2,1},{3,0},{4,7},{5,6},{6,5},{7,4},{8,11},{9,10},{10,... | collective-permute-start | bytes 344072 | tf_op jit(solution)/shard_map/ppermute | solution.py:455

commit v2 on v1

--- a/solution.py
+++ b/solution.py
@@ -68,15 +68,7 @@
     return np.stack(forward), np.stack(inverse), k_pad, m_pad
 
 
-def wave_kernel(
-    source_count, start, m_pad, has_fetch, rank_ref, there_ref, back_ref, *refs
-):
-    refs = list(refs)
-    fetch = None
-    if has_fetch:
-        fetch = pltpu.make_async_copy(
-            refs.pop(source_count).at[1], refs.pop(-5), refs.pop()
-        )
+def wave_kernel(source_count, start, m_pad, rank_ref, there_ref, back_ref, *refs):
     sources, outs = refs[:source_count], refs[source_count:-3]
     buf, shapes, sems = refs[-3:]
     ranks = len(outs)
@@ -94,8 +86,6 @@
             copy = pltpu.make_async_copy(part, buf.at[j, into], sems.at[k, j])
             copy.start()
             copies.append(copy)
-    if fetch is not None:
-        fetch.start()
     if k_pad > used:
         buf[:, pl.ds(used, k_pad - used)] = jnp.zeros(
             (columns, k_pad - used, scens, LANES), F32
@@ -117,38 +107,30 @@
                 outs[k][j, pl.ds(s, rows, stride=scens), :] = out[
                     k * m_pad : k * m_pad + rows, j * LANES : (j + 1) * LANES
                 ]
-    if fetch is not None:
-        fetch.wait()
-
-
-def wave(rank, tables, m_pad, sources, scens, start, width, fetch):
+
+
+def wave(rank, tables, m_pad, sources, scens, start, width):
     rows = sources[0].shape[0]
     ranks = sum(source.shape[0] for source in sources) // rows
     columns = width // LANES
     k_pad = tables[0].shape[1] // 3
-    fetches = [] if fetch is None else [fetch]
     vmem = pl.BlockSpec(memory_space=pltpu.VMEM)
     shape = jax.ShapeDtypeStruct((columns, rows * scens, LANES), F32)
     return pl.pallas_call(
-        functools.partial(
-            wave_kernel, len(sources), start, m_pad, fetch is not None
-        ),
+        functools.partial(wave_kernel, len(sources), start, m_pad),
         in_specs=[pl.BlockSpec(memory_space=pltpu.SMEM), vmem, vmem]
-        + [pl.BlockSpec(memory_space=pl.ANY)] * (len(sources) + len(fetches)),
-        out_specs=[vmem] * (ranks + len(fetches)),
-        out_shape=[pltpu.VMEM(shape.shape, F32)]
-        + [shape] * (ranks - 1)
-        + [pltpu.VMEM(each.shape[1:], each.dtype) for each in fetches],
+        + [pl.BlockSpec(memory_space=pl.ANY)] * len(sources),
+        out_specs=[vmem] * ranks,
+        out_shape=[pltpu.VMEM(shape.shape, F32)] + [shape] * (ranks - 1),
         scratch_shapes=[
             pltpu.VMEM((columns, k_pad, scens, LANES), F32),
             pltpu.VMEM((scens, HALF, width), BF16),
             pltpu.SemaphoreType.DMA((len(sources), columns)),
-        ]
-        + [pltpu.SemaphoreType.DMA for _ in fetches],
+        ],
         compiler_params=pltpu.CompilerParams(vmem_limit_bytes=VMEM_BYTES),
         cost_estimate=SMALL,
         name="wave",
-    )(rank, *tables, *sources, *fetches)
+    )(rank, *tables, *sources)
 
 
 def level_kernel(
@@ -183,7 +165,7 @@
         (inject_hbm, inject_ref),
         (there_ref.at[rank_ref[0]], there_out),
         (back_ref.at[rank_ref[0]], back_out),
-        (zinv_ref.at[0], zinv_out),
+        (zinv_ref, zinv_out),
     ]
     copies = [
         pltpu.make_async_copy(*pair, sems.at[q]) for q, pair in enumerate(pairs)
@@ -245,7 +227,7 @@
             pltpu.VMEM((8, buses), F32),
             pltpu.VMEM(there.shape[1:], BF16),
             pltpu.VMEM(back.shape[1:], BF16),
-            pltpu.VMEM(zinv.shape[1:], BF16),
+            pltpu.VMEM(zinv.shape, BF16),
         ],
         scratch_shapes=[pltpu.VMEM(each.shape, each.dtype) for each in inputs[:5]]
         + [pltpu.SemaphoreType.DMA((len(inputs),))],
@@ -255,82 +237,79 @@
     )(rank, dev_count, *inputs)
 
 
+def add_far(far, blocks, hot):
+    for first in range(0, len(blocks), 2):
+        parts = [split(block) for block in blocks[first : first + 2]]
+        rows = slice(first * NBD, (first + len(parts)) * NBD)
+        for piece in range(2):
+            edges = jnp.concatenate([part[piece] for part in parts], axis=1)
+            far += jnp.dot(edges, hot[rows], preferred_element_type=F32)
+    return far
+
+
 def tie_kernel(
-    h_local, scens, areas, shifts, place_ref, *refs
+    h_local, areas, origins, late_count, place_ref, *refs
 ):
-    lists, blocks, out_ref = refs[:5], refs[5:-9], refs[-9]
-    bus_ref, area_ref, far_ref, res_ref, reac_ref = refs[-8:-3]
-    scaled, held, sems = refs[-3:]
-    list_copies = []
-    for q, pair in enumerate(zip(lists, refs[-8:-3])):
-        copy = pltpu.make_async_copy(*pair, sems.at[len(blocks) + q])
+    lists, refs = refs[:5], refs[5:]
+    early = len(origins) - late_count
+    blocks, refs = refs[:early], refs[early:]
+    far_out, hot_out, adm_out, target_out = refs[:4]
+    bus_ref, area_ref, far_ref, res_ref, reac_ref, held, sems = refs[4:]
+    copies = [
+        pltpu.make_async_copy(*pair, sems.at[q])
+        for q, pair in enumerate(zip(lists, refs[4:9]))
+    ]
+    copies += [
+        pltpu.make_async_copy(block, held.at[q], sems.at[5 + q])
+        for q, block in enumerate(blocks)
+    ]
+    for copy in copies:
         copy.start()
-        list_copies.append(copy)
-    copies = []
-    for q, block in enumerate(blocks):
-        copy = pltpu.make_async_copy(block, held.at[q], sems.at[q])
-        copy.start()
-        copies.append(copy)
-    for copy in list_copies:
+    for copy in copies[:5]:
         copy.wait()
     ties = bus_ref.shape[1]
     edge_ids = lax.broadcasted_iota(jnp.int32, (NBD, ties), 0)
     far_hit = edge_ids == far_ref[...]
-    far = jnp.zeros((2 * h_local * scens, ties), F32)
-
-    def origin(q):
-        ringed = (place_ref[1] + areas - shifts[q // 2]) % areas
-        return ringed ^ 1 if q % 2 else ringed
-
-    for first in range(0, len(blocks), 2):
-        pair = range(first, min(first + 2, len(blocks)))
-        for q in pair:
-            copies[q].wait()
-        parts = [split(held[q]) for q in pair]
-        onehot = jnp.concatenate(
-            [
-                jnp.where(far_hit & (area_ref[...] == origin(q)), 1.0, 0.0)
-                for q in pair
-            ],
-            axis=0,
-        ).astype(BF16)
-        for piece in range(2):
-            edges = jnp.concatenate([part[piece] for part in parts], axis=1)
-            far += jnp.dot(edges, onehot, preferred_element_type=F32)
+    hots = []
+    for step, flip in origins:
+        origin = (place_ref[1] + areas - step) % areas
+        hit = area_ref[...] == (origin ^ 1 if flip else origin)
+        hots.append(jnp.where(far_hit & hit, 1.0, 0.0).astype(BF16))
+    hot_out[...] = jnp.concatenate(hots[early:], axis=0)
+    target_out[...] = jnp.where(edge_ids == bus_ref[...], 1.0, 0.0).astype(BF16)
     resist = res_ref[...]
-    imag_rows = h_local * scens
     for h in range(h_local):
         order = (2 * (place_ref[0] * h_local + h) + 1).astype(F32)
         reactance = reac_ref[...] * order
         denominator = resist * resist + reactance * reactance
-        adm_real = resist / denominator
-        adm_imag = -reactance / denominator
-        real = far[h * scens : (h + 1) * scens]
-        imag = far[imag_rows + h * scens : imag_rows + (h + 1) * scens]
-        scaled[pl.ds(h * scens, scens), :] = adm_real * real - adm_imag * imag
-        scaled[pl.ds(imag_rows + h * scens, scens), :] = (
-            adm_real * imag + adm_imag * real
-        )
-    target = jnp.where(edge_ids == bus_ref[...], 1.0, 0.0).astype(BF16)
-    high, low = split(scaled[...])
-    out_ref[...] = lax.dot_general(
-        high, target, NT_DIMS, preferred_element_type=F32
-    ) + lax.dot_general(low, target, NT_DIMS, preferred_element_type=F32)
-
-
-def tie_currents(place, tie_lists, blocks, areas, shifts, h_local, scens):
+        adm_out[pl.ds(h, 1), :] = resist / denominator
+        adm_out[pl.ds(h_local + h, 1), :] = -reactance / denominator
+    for copy in copies[5:]:
+        copy.wait()
+    far_out[...] = add_far(
+        jnp.zeros(far_out.shape, F32),
+        [held[q] for q in range(early)],
+        jnp.concatenate(hots[:early], axis=0),
+    )
+
+
+def tie_parts(place, tie_lists, blocks, areas, origins, late_count, h_local):
     ties = tie_lists[0].shape[1]
-    rows = 2 * h_local * scens
+    rows = blocks[0].shape[0]
     vmem = pl.BlockSpec(memory_space=pltpu.VMEM)
     return pl.pallas_call(
-        functools.partial(tie_kernel, h_local, scens, areas, shifts),
+        functools.partial(tie_kernel, h_local, areas, origins, late_count),
         in_specs=[pl.BlockSpec(memory_space=pltpu.SMEM)]
         + [pl.BlockSpec(memory_space=pl.ANY)] * (len(tie_lists) + len(blocks)),
-        out_specs=vmem,
-        out_shape=pltpu.VMEM((rows, NBD), F32),
+        out_specs=[vmem] * 4,
+        out_shape=[
+            pltpu.VMEM((rows, ties), F32),
+            pltpu.VMEM((late_count * NBD, ties), BF16),
+            pltpu.VMEM((2 * h_local, ties), F32),
+            pltpu.VMEM((NBD, ties), BF16),
+        ],
         scratch_shapes=[pltpu.VMEM(each.shape, each.dtype) for each in tie_lists]
         + [
-            pltpu.VMEM((rows, ties), F32),
             pltpu.VMEM((len(blocks), rows, NBD), F32),
             pltpu.SemaphoreType.DMA((len(blocks) + len(tie_lists),)),
         ],
@@ -340,54 +319,92 @@
     )(place, *tie_lists, *blocks)
 
 
-def solve_kernel(start, width, has_tie, has_total, ranks, rank_ref, *refs):
+def tie_currents(far, adm, target, scaled, h_local, scens):
+    half = h_local * scens
+    for h in range(h_local):
+        adm_real, adm_imag = adm[h : h + 1], adm[h_local + h : h_local + h + 1]
+        real = far[h * scens : (h + 1) * scens]
+        imag = far[half + h * scens : half + (h + 1) * scens]
+        scaled[pl.ds(h * scens, scens), :] = adm_real * real - adm_imag * imag
+        scaled[pl.ds(half + h * scens, scens), :] = adm_real * imag + adm_imag * real
+    high, low = split(scaled[...])
+    return lax.dot_general(
+        high, target, NT_DIMS, preferred_element_type=F32
+    ) + lax.dot_general(low, target, NT_DIMS, preferred_element_type=F32)
+
+
+def solve_kernel(start, width, ranks, late_count, place_ref, *refs):
     refs = list(refs)
-    base_ref, sat_ref, real_ref, imag_ref = refs[:4]
-    shaped_refs = refs[4 : 4 + ranks]
-    del refs[: 4 + ranks]
-    tie_ref = refs.pop(0) if has_tie else None
-    total_ref = refs.pop(0) if has_total else None
-    out_ref, full = refs[:2]
-    refs = refs[2:]
-    lanes = pl.ds(start, width)
-    stage, sem = refs if has_total else (out_ref, None)
+
+    def take(count):
+        taken, refs[:count] = refs[:count], []
+        return taken
+
+    base_ref, sat_ref, zinv_ref, _ = take(4)
+    shaped_refs = take(ranks)
+    last = late_count > 0
+    if last:
+        total_ref, far_ref, hot_ref, adm_ref, target_ref = take(5)
+        blocks = take(late_count)
+        out_ref, full, stage, sem, scaled, held, block_sems = refs
+        block_copies = [
+            pltpu.make_async_copy(block, held.at[q], block_sems.at[q])
+            for q, block in enumerate(blocks)
+        ]
+        for copy in block_copies:
+            copy.start()
+    else:
+        out_ref, mark_ref, full = refs
+        mark_ref[...] = jnp.zeros(mark_ref.shape, F32)
+        stage = out_ref
     _, h_local, scens, _ = base_ref.shape
     columns = shaped_refs[0].shape[0]
     part = scens // ranks
     for k, ref in enumerate(shaped_refs):
-        quarter = pl.ds(pl.multiple_of((rank_ref[0] ^ k) * part, 8), part)
+        quarter = pl.ds(pl.multiple_of((place_ref[0] ^ k) * part, 8), part)
         for j in range(columns):
             at = pl.ds(j * LANES, LANES)
             for row in range(2 * h_local):
                 full[row, quarter, at] = ref[j, pl.ds(row * part, part), :]
+    if last:
+        for copy in block_copies:
+            copy.wait()
+        far = add_far(
+            far_ref[...], [held[q] for q in range(late_count)], hot_ref[...]
+        )
+        ties = tie_currents(
+            far, adm_ref[...], target_ref[...], scaled, h_local, scens
+        )
+    lanes = pl.ds(start, width)
     sat = sat_ref[0:1, lanes]
     copies = []
     for h in range(h_local):
         parts = []
         for c in range(2):
-            rhs = base_ref[c, h, :, lanes] + sat * full[c * h_local + h]
-            if has_tie:
-                ties = tie_ref[c, h]
+            row = c * h_local + h
+            rhs = base_ref[c, h, :, lanes] + sat * full[row]
+            if last:
+                here = ties[row * scens : (row + 1) * scens]
                 if width > NBD:
-                    rhs = jnp.concatenate([rhs[:, :NBD] + ties, rhs[:, NBD:]], axis=1)
+                    rhs = jnp.concatenate([rhs[:, :NBD] + here, rhs[:, NBD:]], axis=1)
                 else:
-                    rhs = rhs + ties
+                    rhs = rhs + here
             parts.append(rhs.astype(BF16))
         both = jnp.concatenate(parts, axis=0)
         by_real = lax.dot_general(
-            both, real_ref[h, :, lanes], NT_DIMS, preferred_element_type=F32
+            both, zinv_ref[0, h, :, lanes], NT_DIMS, preferred_element_type=F32
         )
         by_imag = lax.dot_general(
-            both, imag_ref[h, :, lanes], NT_DIMS, preferred_element_type=F32
+            both, zinv_ref[1, h, :, lanes], NT_DIMS, preferred_element_type=F32
         )
         real = by_real[:scens] - by_imag[scens:]
         imag = by_real[scens:] + by_imag[:scens]
-        if has_total:
+        if last:
             real = real + total_ref[0, h]
             imag = imag + total_ref[1, h]
         stage[0, h] = real
         stage[1, h] = imag
-        if sem is not None:
+        if last:
             copy = pltpu.make_async_copy(stage.at[:, h], out_ref.at[:, h], sem.at[h])
             copy.start()
             copies.append(copy)
@@ -395,34 +412,46 @@
         copy.wait()
 
 
-def solve(rank, base, sat, zinvs, shaped, tie, total, start, width):
+def solve(place, base, sat, zinvs, shaped, tie, start, width):
     _, h_local, scens, _ = base.shape
     ranks = len(shaped)
     vmem = pl.BlockSpec(memory_space=pltpu.VMEM)
-    operands = [base, sat, *zinvs] + list(shaped)
-    operands += [tie] if tie is not None else []
-    operands += [total] if total is not None else []
+    anywhere = pl.BlockSpec(memory_space=pl.ANY)
+    operands = [base, sat, *zinvs, *shaped]
+    in_specs = [vmem] * len(operands)
     scratch = [pltpu.VMEM((2 * h_local, scens, width), F32)]
-    out_spec = vmem
-    if total is not None:
-        out_spec = pl.BlockSpec(memory_space=pl.ANY)
+    late = []
+    if tie is not None:
+        total, parts, late = tie
+        rows, ties = parts[0].shape
+        operands += [total, *parts, *late]
+        in_specs += [vmem] * (1 + len(parts)) + [anywhere] * len(late)
+        out_specs = anywhere
+        out_shape = jax.ShapeDtypeStruct(base.shape, F32)
         scratch += [
             pltpu.VMEM(base.shape, F32),
             pltpu.SemaphoreType.DMA((h_local,)),
+            pltpu.VMEM((rows, ties), F32),
+            pltpu.VMEM((len(late), rows, NBD), F32),
+            pltpu.SemaphoreType.DMA((len(late),)),
+        ]
+    else:
+        in_specs[3] = anywhere
+        out_specs = [vmem, vmem]
+        out_shape = [
+            pltpu.VMEM(base.shape, F32),
+            pltpu.VMEM((8, LANES), F32),
         ]
     return pl.pallas_call(
-        functools.partial(
-            solve_kernel, start, width, tie is not None, total is not None, ranks
-        ),
-        in_specs=[pl.BlockSpec(memory_space=pltpu.SMEM), vmem, vmem]
-        + [vmem] * (len(operands) - 2),
-        out_specs=out_spec,
-        out_shape=jax.ShapeDtypeStruct(base.shape, F32),
+        functools.partial(solve_kernel, start, width, ranks, len(late)),
+        in_specs=[pl.BlockSpec(memory_space=pltpu.SMEM)] + in_specs,
+        out_specs=out_specs,
+        out_shape=out_shape,
         scratch_shapes=scratch,
         compiler_params=pltpu.CompilerParams(vmem_limit_bytes=VMEM_BYTES),
         cost_estimate=SMALL,
         name="solve",
-    )(rank, *operands)
+    )(place, *operands)
 
 
 def per_device(
@@ -479,7 +508,7 @@
 
     edge = after(edge, *pieces)
     blocks = [edge, exchange(edge)]
-    base, sat, there, back, zinv_real = levels(
+    base, sat, there, back, held = levels(
         place,
         dev_count,
         after(dev_bus, sibling),
@@ -499,52 +528,54 @@
             part,
             starts[index],
             sizes[index],
-            zinv if index == len(sizes) - 1 else None,
         )
 
     waves = [list(run_wave(index)) for index in range(len(sizes))]
-    zinv_imag = waves[-1].pop()
-    shaped = [
-        [outs[0]] + [swap(outs[k], k) for k in range(1, ranks)] for outs in waves
-    ]
     ring = {2: shift(edge, 2)}
     if areas > 4:
         ring[areas - 2] = shift(edge, areas - 2)
     for step in range(4, areas - 2, 2):
         ring[step] = shift(after(ring[step - 2], sat), 2)
-    shifts = [0]
+    late = []
+    origins, late_origins = [(0, 0), (0, 1)], []
     for step, block in ring.items():
+        blocks.append(block)
+        origins.append((step, 0))
         if step == 2:
-            needs = [blocks[-1], far[0], sat]
+            blocks.append(exchange(after(block, blocks[1], far[0], sat)))
+            origins.append((step, 1))
         else:
-            needs = blocks[-1:] if step == areas - 2 else [waves[-1][0]]
-        blocks += [block, exchange(after(block, *needs))]
-        shifts.append(step)
+            needs = blocks[3:4] if step == areas - 2 else [waves[-1][0]]
+            late.append(exchange(after(block, *needs)))
+            late_origins.append((step, 1))
+
     base = base.reshape(2, h_local, scens, buses)
     tie_lists = [
-        tie_bus,
-        tie_area[:, :, 0],
-        tie_far,
-        tie_res,
-        tie_reac,
+        pltpu.with_memory_space_constraint(each, pltpu.HBM)
+        for each in (tie_bus, tie_area[:, :, 0], tie_far, tie_res, tie_reac)
     ]
-    tie_lists = [pltpu.with_memory_space_constraint(t, pltpu.HBM) for t in tie_lists]
-    tie = tie_currents(place, tie_lists, blocks, areas, shifts, h_local, scens)
-    tie = tie.reshape(2, h_local, scens, NBD)
-
-    total = None
-    for start, width, parts in zip(starts, sizes, shaped):
-        total = solve(
-            place,
-            base,
-            sat,
-            (zinv_real, zinv_imag),
-            parts,
-            tie if start == 0 else None,
-            total,
-            start,
-            width,
-        )
+    parts = tie_parts(
+        place, tie_lists, blocks, areas, origins + late_origins, len(late), h_local
+    )
+
+    shaped = []
+    for index, outs in enumerate(waves):
+        if index == len(waves) - 1:
+            outs[-1] = after(outs[-1], parts[0])
+        shaped.append([outs[0]] + [swap(outs[k], k) for k in range(1, ranks)])
+    total, mark = solve(
+        place, base, sat, (held, zinv), shaped[0], None, starts[0], sizes[0]
+    )
+    total = solve(
+        place,
+        base,
+        sat,
+        (held, mark),
+        shaped[1],
+        (total, parts, late),
+        starts[1],
+        sizes[1],
+    )
     return total[:, None]
 
 

time: 50.5 us -> 47 us (0.931)
  starting transfers between devices: 19.6 us -> 17.9 us
  waiting for transfers between devices: 5.04 us -> 3.63 us
    pallas_call x5, Pallas kernels: 17.1 us -> 14.4 us  [the longest x2 8.3 us: solve(): pl.pallas_call(functools.partial(solve_kernel, start, width, ranks, len(l...]
    pallas_call x1, Pallas kernels: 4.9 us -> 7.25 us  [levels(): pl.pallas_call(functools.partial(level_kernel, step), in_specs=[smem] * 2...]
    ppermute x3, starting transfers between devices: 5.4 us -> 3.83 us  [shift(): lax.ppermute(value, 'area', [(a, (a + step) % areas) for a in range(areas)])]
    ppermute x3, waiting for transfers between devices: 1.28 us -> 0.23 us  [shift(): lax.ppermute(value, 'area', [(a, (a + step) % areas) for a in range(areas)])]
    ppermute x4, waiting for transfers between devices: 0.96 us -> 0.01 us  [exchange(): return lax.ppermute(value, 'area', [(a, a ^ 1) for a in range(areas)])]
    ppermute x9, waiting for transfers between devices: 2.8 us -> 3.39 us  [swap(): return lax.ppermute(value, 'harm', [(i, i ^ k) for i in range(ranks)])]
  transfers between devices with their start and end apart: 16 -> 16, of which waited for: 5 -> 3; matrix products, arithmetic and copies ran while one was open for 2% -> 2% of each run, Pallas kernels for 38% -> 37%
where the time goes in v2:
time: 47 us; the launch traced here: 46.8 us
  Pallas kernels  21.6 us (46%)
  starting transfers between devices  17.9 us (38%)
  waiting for transfers between devices  3.63 us (8%)
  local copies, waits for them, and re-layouts  2.79 us (6%)
  between operations  0.81 us (2%)
    ppermute x9, starting transfers between devices, swap(): return lax.ppermute(value, 'harm', [(i, i ^ k) for i in range(ranks)])  9.38 us
    pallas_call x2, Pallas kernels, solve(): pl.pallas_call(functools.partial(solve_kernel, start, width, ranks, len(l...  8.3 us
    pallas_call x1, Pallas kernels, levels(): pl.pallas_call(functools.partial(level_kernel, step), in_specs=[smem] * 2...  7.25 us
    ppermute x4, starting transfers between devices, exchange(): return lax.ppermute(value, 'area', [(a, a ^ 1) for a in range(areas)])  4.65 us
    ppermute x3, starting transfers between devices, shift(): lax.ppermute(value, 'area', [(a, (a + step) % areas) for a in range(areas)])  3.83 us
    pallas_call x2, Pallas kernels, wave(): pl.pallas_call(functools.partial(wave_kernel, len(sources), start, m_pad)...  3.66 us
    ppermute x9, waiting for transfers between devices, swap(): return lax.ppermute(value, 'harm', [(i, i ^ k) for i in range(ranks)])  3.39 us
    pallas_call x1, Pallas kernels, tie_parts(): pl.pallas_call(functools.partial(tie_kernel, h_local, areas, origins, lat...  2.43 us
  transfers between devices with their start and end apart: 16, of which 3 were waited for; matrix products, arithmetic and copies ran while one was open for 2% of the time, Pallas kernels for 37%

profile of v2, /device:TPU:0, one launch (start us, length us, event | category | flops | bytes accessed | tf_op | source)
XLA Modules:
  0.0 46.8 jit_solution(7269770763991972255)
XLA Ops:
  0.0 0.0 copy-start
  0.0 2.1 %constant_dynamic-slice_fusion = (f32[14,8,768]{2,1,0:T(8,128)}, f32[14,8,768]{2,1,0:T(8,128)}) fusion(f32[14,32,768]{2,1,0:T(8,128)} %bitcast.11, s32[]{:T(128)S(6)} %select_n.7, s32[]{:T(128)S(6)} %select_n.6), kind=kLoop, calls=%fused_computation.1 | loop fusion | bytes 1376264 | tf_op jit(solution)/shard_map/dynamic_slice | solution.py:491
  2.1 0.0 copy-done
  2.1 0.5 collective-permute-start
  2.5 2.6 %collective-permute-start.2 = (f32[14,8,768]{2,1,0:T(8,128)}, f32[14,8,768]{2,1,0:T(8,128)S(1)}, u32[]{:S(2)}, u32[]{:S(2)}) collective-permute-start(f32[14,8,768]{2,1,0:T(8,128)} %get-tuple-element.42), channel_id=1, source_target_pairs={{0,3},{1,2},{2,1},{3,0},{4,7},{5,6},{6,5},{7,4},{8,11},{9,10},{10,... | collective-permute-start | bytes 1032200 | tf_op jit(solution)/shard_map/ppermute | solution.py:484
  5.2 0.7 %slice.3 = f32[2,1,7,32,128]{4,3,2,1,0:T(8,128)} slice(f32[2,1,7,32,768]{4,3,2,1,0:T(8,128)S(1)} %copy-done), slice={[0:2], [0:1], [0:7], [0:32], [0:128]} | slice | bytes 458752 | tf_op jit(solution)/shard_map/slice | solution.py:499
  5.9 1.6 %collective-permute-start.9 = (f32[448,128]{1,0:T(8,128)}, f32[448,128]{1,0:T(8,128)}, u32[]{:S(2)}, u32[]{:S(2)}) collective-permute-start(f32[448,128]{1,0:T(8,128)} %bitcast.7.refs_5_), channel_id=1, source_target_pairs={{0,8},{4,12},{8,16},{12,20},{16,24},{20,28},{24,0},{28,4},{1,9},{5... | collective-permute-start | bytes 688136 | tf_op jit(solution)/shard_map/ppermute | solution.py:502
  7.4 1.5 %collective-permute-start.8 = (f32[448,128]{1,0:T(8,128)}, f32[448,128]{1,0:T(8,128)}, u32[]{:S(2)}, u32[]{:S(2)}) collective-permute-start(f32[448,128]{1,0:T(8,128)} %bitcast.7.refs_5_), channel_id=1, source_target_pairs={{0,4},{4,0},{8,12},{12,8},{16,20},{20,16},{24,28},{28,24},{1,5},{5... | collective-permute-start | bytes 688136 | tf_op jit(solution)/shard_map/ppermute | solution.py:507
  8.9 0.5 %collective-permute-start.1 = (f32[14,8,768]{2,1,0:T(8,128)}, f32[14,8,768]{2,1,0:T(8,128)S(1)}, u32[]{:S(2)}, u32[]{:S(2)}) collective-permute-start(f32[14,8,768]{2,1,0:T(8,128)} %get-tuple-element.41), channel_id=1, source_target_pairs={{0,2},{1,3},{2,0},{3,1},{4,6},{5,7},{6,4},{7,5},{8,10},{9,11},{10,... | collective-permute-start | bytes 1032200 | tf_op jit(solution)/shard_map/ppermute | solution.py:484
  9.4 0.0 collective-permute-done.refs_1_
  9.4 2.2 %collective-permute-start.11 = (f32[448,128]{1,0:T(8,128)}, f32[448,128]{1,0:T(8,128)S(1)}, u32[]{:S(2)}, u32[]{:S(2)}) collective-permute-start(f32[448,128]{1,0:T(8,128)} %bitcast.7.refs_5_), channel_id=1, source_target_pairs={{0,24},{4,28},{8,0},{12,4},{16,8},{20,12},{24,16},{28,20},{1,25},{... | collective-permute-start | bytes 688136 | tf_op jit(solution)/shard_map/ppermute | solution.py:502
  12.3 0.1 pad_add_fusion.rank_ref.place_ref
  12.4 0.0 copy-start.1
  12.4 7.2 %levels.1 = (f32[14,32,768]{2,1,0:T(8,128)S(1)}, f32[8,768]{1,0:T(8,128)S(1)}, bf16[256,192]{1,0:T(8,128)(2,1)S(1)}, bf16[128,256]{1,0:T(8,128)(2,1)S(1)}, bf16[2,7,768,768]{3,2,1,0:T(8,128)(2,1)S(1)}) custom-call(s32[2]{0:T(128)S(1)} %pad_add_fusion.rank_ref.place_ref, s32[1]{0:T(128)S(6)} %copy.16.count_ref, s32[1,2048]{1,0:T(1,128)} %bus_hbm, ...), custom_call_target="tpu_custom_call" | custom-call | flops 1000 | bytes 1000 | tf_op jit(solution)/shard_map/levels/pallas_call | solution.py:221
  19.7 0.0 collective-permute-done.9.refs_7_
  19.7 0.0 collective-permute-done.8.refs_6_
  19.7 0.0 collective-permute-done.2.refs_3_
  19.7 0.4 collective-permute-start.10
  20.1 0.0 collective-permute-start.12
  20.1 1.3 %collective-permute-done.1.refs_2_ = f32[14,8,768]{2,1,0:T(8,128)S(1)} collective-permute-done((f32[14,8,768]{2,1,0:T(8,128)}, f32[14,8,768]{2,1,0:T(8,128)S(1)}, u32[]{:S(2)}, u32[]{:S(2)}) %collective-permute-start.1) | collective-permute-done | bytes 344096 | tf_op jit(solution)/shard_map/ppermute | solution.py:484
  21.4 0.0 copy-done.1
  21.4 2.2 %wave.2 = (f32[4,112,128]{2,1,0:T(8,128)S(1)}, f32[4,112,128]{2,1,0:T(8,128)S(1)}, f32[4,112,128]{2,1,0:T(8,128)S(1)}, f32[4,112,128]{2,1,0:T(8,128)S(1)}) custom-call(s32[2]{0:T(128)S(1)} %pad_add_fusion.rank_ref.place_ref, bf16[256,192]{1,0:T(8,128)(2,1)S(1)} %get-tuple-element.39.there_ref, bf16[128,256]{1,0:T(8,128)(2,1)S(1)} %get-tuple-element.40.back_ref, ...), custom_call_target="tpu_custom_call" | custom-call | flops 1000 | bytes 1000 | tf_op jit(solution)/shard_map/wave/pallas_call | solution.py:119
  23.6 0.1 collective-permute-start.3
  23.7 1.7 %collective-permute-start.4 = (f32[4,112,128]{2,1,0:T(8,128)S(1)}, f32[4,112,128]{2,1,0:T(8,128)S(1)}, u32[]{:S(2)}, u32[]{:S(2)}) collective-permute-start(f32[4,112,128]{2,1,0:T(8,128)S(1)} %get-tuple-element.45), channel_id=1, source_target_pairs={{0,2},{1,3},{2,0},{3,1},{4,6},{5,7},{6,4},{7,5},{8,10},{9,11},{10,... | collective-permute-start | bytes 688136 | tf_op jit(solution)/shard_map/ppermute | solution.py:484
  25.4 0.0 collective-permute-done.11.refs_9_
  25.4 0.1 collective-permute-start.5
  25.5 1.5 %wave.3 = (f32[2,112,128]{2,1,0:T(8,128)S(1)}, f32[2,112,128]{2,1,0:T(8,128)S(1)}, f32[2,112,128]{2,1,0:T(8,128)S(1)}, f32[2,112,128]{2,1,0:T(8,128)S(1)}) custom-call(s32[2]{0:T(128)S(1)} %pad_add_fusion.rank_ref.place_ref, bf16[256,192]{1,0:T(8,128)(2,1)S(1)} %get-tuple-element.39.there_ref, bf16[128,256]{1,0:T(8,128)(2,1)S(1)} %get-tuple-element.40.back_ref, ...), custom_call_target="tpu_custom_call" | custom-call | flops 1000 | bytes 1000 | tf_op jit(solution)/shard_map/wave/pallas_call | solution.py:119
  27.0 0.0 collective-permute-done.10.refs_8_
  27.0 1.7 %collective-permute-start.14 = (f32[448,128]{1,0:T(8,128)S(1)}, f32[448,128]{1,0:T(8,128)S(1)}, u32[]{:S(2)}, u32[]{:S(2)}) collective-permute-start(f32[448,128]{1,0:T(8,128)S(1)} %collective-permute-done.11.refs_9_), channel_id=1, source_target_pairs={{0,4},{4,0},{8,12},{12,8},{16,20},{20,16},{24,28},{28,24},{1,5},{5... | collective-permute-start | bytes 688136 | tf_op jit(solution)/shard_map/ppermute | solution.py:507
  28.7 0.2 collective-permute-done.12.refs_10_
  28.9 1.1 %collective-permute-start.15 = (f32[448,128]{1,0:T(8,128)S(1)}, f32[448,128]{1,0:T(8,128)S(1)}, u32[]{:S(2)}, u32[]{:S(2)}) collective-permute-start(f32[448,128]{1,0:T(8,128)S(1)} %collective-permute-done.12.refs_10_), channel_id=1, source_target_pairs={{0,4},{4,0},{8,12},{12,8},{16,20},{20,16},{24,28},{28,24},{1,5},{5... | collective-permute-start | bytes 688136 | tf_op jit(solution)/shard_map/ppermute | solution.py:507
  30.0 2.4 %ties.1 = (f32[448,256]{1,0:T(8,128)S(1)}, bf16[256,256]{1,0:T(8,128)(2,1)S(1)}, f32[14,256]{1,0:T(8,128)S(1)}, bf16[128,256]{1,0:T(8,128)(2,1)S(1)}) custom-call(s32[2]{0:T(128)S(1)} %pad_add_fusion.rank_ref.place_ref, s32[1,256]{1,0:T(1,128)} %refs_0_.1, s32[1,256]{1,0:T(1,128)} %bitcast.21, s32[1,256]{1,0:T(1,128)} %refs_2_.1, f32[1,256]{1,0:T(1,128)} %refs_3_.1, ...), custom_call_target="tpu_custom_call" | custom-call | flops 1000 | bytes 1000 | tf_op jit(solution)/shard_map/ties/pallas_call | solution.py:300
  32.5 0.0 collective-permute-done.3.refs_5_
  32.5 0.1 collective-permute-start.6
  32.5 0.0 collective-permute-done.4.refs_6_
  32.6 1.6 %collective-permute-start.7 = (f32[2,112,128]{2,1,0:T(8,128)S(1)}, f32[2,112,128]{2,1,0:T(8,128)S(1)}, u32[]{:S(2)}, u32[]{:S(2)}) collective-permute-start(f32[2,112,128]{2,1,0:T(8,128)S(1)} %get-tuple-element.50), channel_id=1, source_target_pairs={{0,2},{1,3},{2,0},{3,1},{4,6},{5,7},{6,4},{7,5},{8,10},{9,11},{10,... | collective-permute-start | bytes 344072 | tf_op jit(solution)/shard_map/ppermute | solution.py:484
  34.1 2.1 %collective-permute-done.5.refs_7_ = f32[4,112,128]{2,1,0:T(8,128)S(1)} collective-permute-done((f32[4,112,128]{2,1,0:T(8,128)S(1)}, f32[4,112,128]{2,1,0:T(8,128)S(1)}, u32[]{:S(2)}, u32[]{:S(2)}) %collective-permute-start.5) | collective-permute-done | bytes 229408 | tf_op jit(solution)/shard_map/ppermute | solution.py:484
  36.2 2.2 %collective-permute-start.13 = (f32[2,112,128]{2,1,0:T(8,128)S(1)}, f32[2,112,128]{2,1,0:T(8,128)S(1)}, u32[]{:S(2)}, u32[]{:S(2)}) collective-permute-start(f32[2,112,128]{2,1,0:T(8,128)S(1)} %get-tuple-element.56), channel_id=1, source_target_pairs={{0,3},{1,2},{2,1},{3,0},{4,7},{5,6},{6,5},{7,4},{8,11},{9,10},{10,... | collective-permute-start | bytes 344072 | tf_op jit(solution)/shard_map/ppermute | solution.py:484
  38.4 4.0 %solve.2 = (f32[2,7,32,768]{3,2,1,0:T(8,128)S(1)}, f32[8,128]{1,0:T(8,128)S(1)}) custom-call(s32[2]{0:T(128)S(1)} %pad_add_fusion.rank_ref.place_ref, f32[2,7,32,768]{3,2,1,0:T(8,128)S(1)} %bitcast.16, f32[8,768]{1,0:T(8,128)S(1)} %get-tuple-element.37.refs_1_, bf16[2,7,768,768]{3,2,1,0:T(8,128)(2,1)S(1)} %get-tuple-element.38.refs_2_, ...), custom_call_target="tpu_custom_call" | custom-call | flops 1000 | bytes 1000 | tf_op jit(solution)/shard_map/solve/pallas_call | solution.py:445
  42.5 0.0 collective-permute-done.6.refs_5_
  42.5 0.0 collective-permute-done.7.refs_6_
  42.5 0.0 collective-permute-done.13.refs_7_
  42.5 0.0 collective-permute-done.14.refs_13_
  42.5 0.0 collective-permute-done.15.refs_14_
  42.5 4.3 %solve.3 = f32[2,7,32,768]{3,2,1,0:T(8,128)} custom-call(s32[2]{0:T(128)S(1)} %pad_add_fusion.rank_ref.place_ref, f32[2,7,32,768]{3,2,1,0:T(8,128)S(1)} %bitcast.17, f32[8,768]{1,0:T(8,128)S(1)} %get-tuple-element.37.refs_1_, bf16[2,7,768,768]{3,2,1,0:T(8,128)(2,1)S(1)} %get-tuple-element.38.refs_2_, f32[8,128]{1,0:T(8,128)S(1)} %get-tuple-element.47.refs_3_, ...), custom_call_target="tpu_custom_call" | custom-call | flops 1000 | bytes 1000 | tf_op jit(solution)/shard_map/solve/pallas_call | solution.py:445
Async XLA Ops:
  0.0 2.1 %copy-start = (f32[2,1,7,32,768]{4,3,2,1,0:T(8,128)S(1)}, f32[2,1,7,32,768]{4,3,2,1,0:T(8,128)}, u32[]{:S(2)}) copy-start(f32[2,1,7,32,768]{4,3,2,1,0:T(8,128)} %param.14) | copy-start | bytes 4128772
  2.1 7.4 %collective-permute-start = (f32[14,32,768]{2,1,0:T(8,128)S(1)}, f32[14,32,768]{2,1,0:T(8,128)S(1)}, u32[]{:S(2)}, u32[]{:S(2)}) collective-permute-start(f32[14,32,768]{2,1,0:T(8,128)S(1)} %bitcast.13), channel_id=1, source_target_pairs={{0,1},{1,0},{2,3},{3,2},{4,5},{5,4},{6,7},{7,6},{8,9},{9,8},{10,11... | collective-permute-start | bytes 4128776 | tf_op jit(solution)/shard_map/ppermute | solution.py:484
  2.5 17.2 %collective-permute-start.2 = (f32[14,8,768]{2,1,0:T(8,128)}, f32[14,8,768]{2,1,0:T(8,128)S(1)}, u32[]{:S(2)}, u32[]{:S(2)}) collective-permute-start(f32[14,8,768]{2,1,0:T(8,128)} %get-tuple-element.42), channel_id=1, source_target_pairs={{0,3},{1,2},{2,1},{3,0},{4,7},{5,6},{6,5},{7,4},{8,11},{9,10},{10,... | collective-permute-start | bytes 1032200 | tf_op jit(solution)/shard_map/ppermute | solution.py:484
  5.9 13.8 %collective-permute-start.9 = (f32[448,128]{1,0:T(8,128)}, f32[448,128]{1,0:T(8,128)}, u32[]{:S(2)}, u32[]{:S(2)}) collective-permute-start(f32[448,128]{1,0:T(8,128)} %bitcast.7.refs_5_), channel_id=1, source_target_pairs={{0,8},{4,12},{8,16},{12,20},{16,24},{20,28},{24,0},{28,4},{1,9},{5... | collective-permute-start | bytes 688136 | tf_op jit(solution)/shard_map/ppermute | solution.py:502
  7.4 12.2 %collective-permute-start.8 = (f32[448,128]{1,0:T(8,128)}, f32[448,128]{1,0:T(8,128)}, u32[]{:S(2)}, u32[]{:S(2)}) collective-permute-start(f32[448,128]{1,0:T(8,128)} %bitcast.7.refs_5_), channel_id=1, source_target_pairs={{0,4},{4,0},{8,12},{12,8},{16,20},{20,16},{24,28},{28,24},{1,5},{5... | collective-permute-start | bytes 688136 | tf_op jit(solution)/shard_map/ppermute | solution.py:507
  8.9 12.4 %collective-permute-start.1 = (f32[14,8,768]{2,1,0:T(8,128)}, f32[14,8,768]{2,1,0:T(8,128)S(1)}, u32[]{:S(2)}, u32[]{:S(2)}) collective-permute-start(f32[14,8,768]{2,1,0:T(8,128)} %get-tuple-element.41), channel_id=1, source_target_pairs={{0,2},{1,3},{2,0},{3,1},{4,6},{5,7},{6,4},{7,5},{8,10},{9,11},{10,... | collective-permute-start | bytes 1032200 | tf_op jit(solution)/shard_map/ppermute | solution.py:484
  9.4 16.0 %collective-permute-start.11 = (f32[448,128]{1,0:T(8,128)}, f32[448,128]{1,0:T(8,128)S(1)}, u32[]{:S(2)}, u32[]{:S(2)}) collective-permute-start(f32[448,128]{1,0:T(8,128)} %bitcast.7.refs_5_), channel_id=1, source_target_pairs={{0,24},{4,28},{8,0},{12,4},{16,8},{20,12},{24,16},{28,20},{1,25},{... | collective-permute-start | bytes 688136 | tf_op jit(solution)/shard_map/ppermute | solution.py:502
  12.4 9.0 %copy-start.1 = (f32[2,1,7,32,768]{4,3,2,1,0:T(8,128)S(1)}, f32[2,1,7,32,768]{4,3,2,1,0:T(8,128)}, u32[]{:S(2)}) copy-start(f32[2,1,7,32,768]{4,3,2,1,0:T(8,128)} %param.14) | copy-start | bytes 4128772
  19.7 7.3 %collective-permute-start.10 = (f32[448,128]{1,0:T(8,128)}, f32[448,128]{1,0:T(8,128)S(1)}, u32[]{:S(2)}, u32[]{:S(2)}) collective-permute-start(f32[448,128]{1,0:T(8,128)} %collective-permute-done.9.refs_7_), channel_id=1, source_target_pairs={{0,4},{4,0},{8,12},{12,8},{16,20},{20,16},{24,28},{28,24},{1,5},{5... | collective-permute-start | bytes 688136 | tf_op jit(solution)/shard_map/ppermute | solution.py:507
  20.1 8.8 %collective-permute-start.12 = (f32[448,128]{1,0:T(8,128)}, f32[448,128]{1,0:T(8,128)S(1)}, u32[]{:S(2)}, u32[]{:S(2)}) collective-permute-start(f32[448,128]{1,0:T(8,128)} %collective-permute-done.9.refs_7_), channel_id=1, source_target_pairs={{0,8},{4,12},{8,16},{12,20},{16,24},{20,28},{24,0},{28,4},{1,9},{5... | collective-permute-start | bytes 688136 | tf_op jit(solution)/shard_map/ppermute | solution.py:502
  23.6 8.9 %collective-permute-start.3 = (f32[4,112,128]{2,1,0:T(8,128)S(1)}, f32[4,112,128]{2,1,0:T(8,128)S(1)}, u32[]{:S(2)}, u32[]{:S(2)}) collective-permute-start(f32[4,112,128]{2,1,0:T(8,128)S(1)} %get-tuple-element.44), channel_id=1, source_target_pairs={{0,1},{1,0},{2,3},{3,2},{4,5},{5,4},{6,7},{7,6},{8,9},{9,8},{10,11... | collective-permute-start | bytes 688136 | tf_op jit(solution)/shard_map/ppermute | solution.py:484
  23.7 8.9 %collective-permute-start.4 = (f32[4,112,128]{2,1,0:T(8,128)S(1)}, f32[4,112,128]{2,1,0:T(8,128)S(1)}, u32[]{:S(2)}, u32[]{:S(2)}) collective-permute-start(f32[4,112,128]{2,1,0:T(8,128)S(1)} %get-tuple-element.45), channel_id=1, source_target_pairs={{0,2},{1,3},{2,0},{3,1},{4,6},{5,7},{6,4},{7,5},{8,10},{9,11},{10,... | collective-permute-start | bytes 688136 | tf_op jit(solution)/shard_map/ppermute | solution.py:484
  25.4 10.8 %collective-permute-start.5 = (f32[4,112,128]{2,1,0:T(8,128)S(1)}, f32[4,112,128]{2,1,0:T(8,128)S(1)}, u32[]{:S(2)}, u32[]{:S(2)}) collective-permute-start(f32[4,112,128]{2,1,0:T(8,128)S(1)} %get-tuple-element.46), channel_id=1, source_target_pairs={{0,3},{1,2},{2,1},{3,0},{4,7},{5,6},{6,5},{7,4},{8,11},{9,10},{10,... | collective-permute-start | bytes 688136 | tf_op jit(solution)/shard_map/ppermute | solution.py:484
  27.0 15.5 %collective-permute-start.14 = (f32[448,128]{1,0:T(8,128)S(1)}, f32[448,128]{1,0:T(8,128)S(1)}, u32[]{:S(2)}, u32[]{:S(2)}) collective-permute-start(f32[448,128]{1,0:T(8,128)S(1)} %collective-permute-done.11.refs_9_), channel_id=1, source_target_pairs={{0,4},{4,0},{8,12},{12,8},{16,20},{20,16},{24,28},{28,24},{1,5},{5... | collective-permute-start | bytes 688136 | tf_op jit(solution)/shard_map/ppermute | solution.py:507
  28.9 13.6 %collective-permute-start.15 = (f32[448,128]{1,0:T(8,128)S(1)}, f32[448,128]{1,0:T(8,128)S(1)}, u32[]{:S(2)}, u32[]{:S(2)}) collective-permute-start(f32[448,128]{1,0:T(8,128)S(1)} %collective-permute-done.12.refs_10_), channel_id=1, source_target_pairs={{0,4},{4,0},{8,12},{12,8},{16,20},{20,16},{24,28},{28,24},{1,5},{5... | collective-permute-start | bytes 688136 | tf_op jit(solution)/shard_map/ppermute | solution.py:507
  32.5 10.0 %collective-permute-start.6 = (f32[2,112,128]{2,1,0:T(8,128)S(1)}, f32[2,112,128]{2,1,0:T(8,128)S(1)}, u32[]{:S(2)}, u32[]{:S(2)}) collective-permute-start(f32[2,112,128]{2,1,0:T(8,128)S(1)} %get-tuple-element.49), channel_id=1, source_target_pairs={{0,1},{1,0},{2,3},{3,2},{4,5},{5,4},{6,7},{7,6},{8,9},{9,8},{10,11... | collective-permute-start | bytes 344072 | tf_op jit(solution)/shard_map/ppermute | solution.py:484
  32.6 9.9 %collective-permute-start.7 = (f32[2,112,128]{2,1,0:T(8,128)S(1)}, f32[2,112,128]{2,1,0:T(8,128)S(1)}, u32[]{:S(2)}, u32[]{:S(2)}) collective-permute-start(f32[2,112,128]{2,1,0:T(8,128)S(1)} %get-tuple-element.50), channel_id=1, source_target_pairs={{0,2},{1,3},{2,0},{3,1},{4,6},{5,7},{6,4},{7,5},{8,10},{9,11},{10,... | collective-permute-start | bytes 344072 | tf_op jit(solution)/shard_map/ppermute | solution.py:484
  36.2 6.2 %collective-permute-start.13 = (f32[2,112,128]{2,1,0:T(8,128)S(1)}, f32[2,112,128]{2,1,0:T(8,128)S(1)}, u32[]{:S(2)}, u32[]{:S(2)}) collective-permute-start(f32[2,112,128]{2,1,0:T(8,128)S(1)} %get-tuple-element.56), channel_id=1, source_target_pairs={{0,3},{1,2},{2,1},{3,0},{4,7},{5,6},{6,5},{7,4},{8,11},{9,10},{10,... | collective-permute-start | bytes 344072 | tf_op jit(solution)/shard_map/ppermute | solution.py:484

commit v3 on v2

--- a/solution.py
+++ b/solution.py
@@ -346,13 +346,7 @@
     if last:
         total_ref, far_ref, hot_ref, adm_ref, target_ref = take(5)
         blocks = take(late_count)
-        out_ref, full, stage, sem, scaled, held, block_sems = refs
-        block_copies = [
-            pltpu.make_async_copy(block, held.at[q], block_sems.at[q])
-            for q, block in enumerate(blocks)
-        ]
-        for copy in block_copies:
-            copy.start()
+        out_ref, full, stage, sem, scaled = refs
     else:
         out_ref, mark_ref, full = refs
         mark_ref[...] = jnp.zeros(mark_ref.shape, F32)
@@ -367,11 +361,7 @@
             for row in range(2 * h_local):
                 full[row, quarter, at] = ref[j, pl.ds(row * part, part), :]
     if last:
-        for copy in block_copies:
-            copy.wait()
-        far = add_far(
-            far_ref[...], [held[q] for q in range(late_count)], hot_ref[...]
-        )
+        far = add_far(far_ref[...], [block[...] for block in blocks], hot_ref[...])
         ties = tie_currents(
             far, adm_ref[...], target_ref[...], scaled, h_local, scens
         )
@@ -425,15 +415,13 @@
         total, parts, late = tie
         rows, ties = parts[0].shape
         operands += [total, *parts, *late]
-        in_specs += [vmem] * (1 + len(parts)) + [anywhere] * len(late)
+        in_specs += [vmem] * (1 + len(parts) + len(late))
         out_specs = anywhere
         out_shape = jax.ShapeDtypeStruct(base.shape, F32)
         scratch += [
             pltpu.VMEM(base.shape, F32),
             pltpu.SemaphoreType.DMA((h_local,)),
             pltpu.VMEM((rows, ties), F32),
-            pltpu.VMEM((len(late), rows, NBD), F32),
-            pltpu.SemaphoreType.DMA((len(late),)),
         ]
     else:
         in_specs[3] = anywhere
@@ -535,7 +523,7 @@
     if areas > 4:
         ring[areas - 2] = shift(edge, areas - 2)
     for step in range(4, areas - 2, 2):
-        ring[step] = shift(after(ring[step - 2], sat), 2)
+        ring[step] = shift(after(ring[step - 2], ring[areas - 2], sat), 2)
     late = []
     origins, late_origins = [(0, 0), (0, 1)], []
     for step, block in ring.items():
@@ -560,9 +548,10 @@
 
     shaped = []
     for index, outs in enumerate(waves):
+        got = [outs[0]] + [swap(outs[k], k) for k in range(1, ranks - 1)]
         if index == len(waves) - 1:
-            outs[-1] = after(outs[-1], parts[0])
-        shaped.append([outs[0]] + [swap(outs[k], k) for k in range(1, ranks)])
+            outs[-1] = after(outs[-1], parts[0], got[1])
+        shaped.append(got + [swap(outs[-1], ranks - 1)])
     total, mark = solve(
         place, base, sat, (held, zinv), shaped[0], None, starts[0], sizes[0]
     )

time: 47 us -> 44.7 us (0.951)
  starting transfers between devices: 17.9 us -> 14.9 us
  waiting for transfers between devices: 3.63 us -> 5.42 us
  local copies, waits for them, and re-layouts: 2.79 us -> 2.11 us
  Pallas kernels: 21.6 us -> 21.1 us
    ppermute x9, starting transfers between devices: 9.38 us -> 6.51 us  [swap(): return lax.ppermute(value, 'harm', [(i, i ^ k) for i in range(ranks)])]
    ppermute x3, waiting for transfers between devices: 0.23 us -> 1.72 us  [shift(): lax.ppermute(value, 'area', [(a, (a + step) % areas) for a in range(areas)])]
    slice x1, local copies, waits for them, and re-layouts: 0.7 us -> 0.02 us  [per_device(): edge = volt[..., :NBD].reshape(rows * scens, NBD)]
    ppermute x4, starting transfers between devices: 4.65 us -> 3.97 us  [exchange(): return lax.ppermute(value, 'area', [(a, a ^ 1) for a in range(areas)])]
    pallas_call x2, Pallas kernels: 8.3 us -> 7.64 us  [solve(): pl.pallas_call(functools.partial(solve_kernel, start, width, ranks, len(l...]
    ppermute x3, starting transfers between devices: 3.83 us -> 4.44 us  [shift(): lax.ppermute(value, 'area', [(a, (a + step) % areas) for a in range(areas)])]
  transfers between devices with their start and end apart: 16 -> 16, of which waited for: 3 -> 4; matrix products, arithmetic and copies ran while one was open for 2% -> 0% of each run, Pallas kernels for 37% -> 39%
where the time goes in v3:
time: 44.7 us; the launch traced here: 44.4 us
  Pallas kernels  21.1 us (47%)
  starting transfers between devices  14.9 us (33%)
  waiting for transfers between devices  5.42 us (12%)
  local copies, waits for them, and re-layouts  2.11 us (5%)
  between operations  0.76 us (2%)
    pallas_call x2, Pallas kernels, solve(): pl.pallas_call(functools.partial(solve_kernel, start, width, ranks, len(l...  7.64 us
    pallas_call x1, Pallas kernels, levels(): pl.pallas_call(functools.partial(level_kernel, step), in_specs=[smem] * 2...  7.25 us
    ppermute x9, starting transfers between devices, swap(): return lax.ppermute(value, 'harm', [(i, i ^ k) for i in range(ranks)])  6.51 us
    ppermute x3, starting transfers between devices, shift(): lax.ppermute(value, 'area', [(a, (a + step) % areas) for a in range(areas)])  4.44 us
    ppermute x4, starting transfers between devices, exchange(): return lax.ppermute(value, 'area', [(a, a ^ 1) for a in range(areas)])  3.97 us
    ppermute x9, waiting for transfers between devices, swap(): return lax.ppermute(value, 'harm', [(i, i ^ k) for i in range(ranks)])  3.7 us
    pallas_call x2, Pallas kernels, wave(): pl.pallas_call(functools.partial(wave_kernel, len(sources), start, m_pad)...  3.65 us
    pallas_call x1, Pallas kernels, tie_parts(): pl.pallas_call(functools.partial(tie_kernel, h_local, areas, origins, lat...  2.53 us
  transfers between devices with their start and end apart: 16, of which 4 were waited for; matrix products, arithmetic and copies ran while one was open for 0% of the time, Pallas kernels for 39%

profile of v3, /device:TPU:0, one launch (start us, length us, event | category | flops | bytes accessed | tf_op | source)
XLA Modules:
  0.0 44.4 jit_solution(13590660227647786583)
XLA Ops:
  0.0 0.0 copy-start
  0.0 2.1 %constant_dynamic-slice_fusion = (f32[14,8,768]{2,1,0:T(8,128)}, f32[14,8,768]{2,1,0:T(8,128)}) fusion(f32[14,32,768]{2,1,0:T(8,128)} %bitcast.11, s32[]{:T(128)S(6)} %select_n.7, s32[]{:T(128)S(6)} %select_n.6), kind=kLoop, calls=%fused_computation.1 | loop fusion | bytes 1376264 | tf_op jit(solution)/shard_map/dynamic_slice | solution.py:479
  2.1 0.0 copy-done
  2.1 0.5 %collective-permute-start = (f32[14,32,768]{2,1,0:T(8,128)S(1)}, f32[14,32,768]{2,1,0:T(8,128)S(1)}, u32[]{:S(2)}, u32[]{:S(2)}) collective-permute-start(f32[14,32,768]{2,1,0:T(8,128)S(1)} %bitcast.13), channel_id=1, source_target_pairs={{0,1},{1,0},{2,3},{3,2},{4,5},{5,4},{6,7},{7,6},{8,9},{9,8},{10,11... | collective-permute-start | bytes 4128776 | tf_op jit(solution)/shard_map/ppermute | solution.py:472
  2.5 2.6 %collective-permute-start.2 = (f32[14,8,768]{2,1,0:T(8,128)}, f32[14,8,768]{2,1,0:T(8,128)S(1)}, u32[]{:S(2)}, u32[]{:S(2)}) collective-permute-start(f32[14,8,768]{2,1,0:T(8,128)} %get-tuple-element.42), channel_id=1, source_target_pairs={{0,3},{1,2},{2,1},{3,0},{4,7},{5,6},{6,5},{7,4},{8,11},{9,10},{10,... | collective-permute-start | bytes 1032200 | tf_op jit(solution)/shard_map/ppermute | solution.py:472
  5.2 1.6 %collective-permute-start.9 = (f32[448,128]{1,0:T(8,128)S(1)}, f32[448,128]{1,0:T(8,128)}, u32[]{:S(2)}, u32[]{:S(2)}) collective-permute-start(f32[448,128]{1,0:T(8,128)S(1)} %bitcast.18), channel_id=1, source_target_pairs={{0,8},{4,12},{8,16},{12,20},{16,24},{20,28},{24,0},{28,4},{1,9},{5... | collective-permute-start | bytes 688136 | tf_op jit(solution)/shard_map/ppermute | solution.py:490
  6.8 1.5 %collective-permute-start.8 = (f32[448,128]{1,0:T(8,128)S(1)}, f32[448,128]{1,0:T(8,128)}, u32[]{:S(2)}, u32[]{:S(2)}) collective-permute-start(f32[448,128]{1,0:T(8,128)S(1)} %bitcast.19), channel_id=1, source_target_pairs={{0,4},{4,0},{8,12},{12,8},{16,20},{20,16},{24,28},{28,24},{1,5},{5... | collective-permute-start | bytes 688136 | tf_op jit(solution)/shard_map/ppermute | solution.py:495
  8.3 2.2 %collective-permute-start.11 = (f32[448,128]{1,0:T(8,128)S(1)}, f32[448,128]{1,0:T(8,128)S(1)}, u32[]{:S(2)}, u32[]{:S(2)}) collective-permute-start(f32[448,128]{1,0:T(8,128)S(1)} %bitcast.20), channel_id=1, source_target_pairs={{0,24},{4,28},{8,0},{12,4},{16,8},{20,12},{24,16},{28,20},{1,25},{... | collective-permute-start | bytes 688136 | tf_op jit(solution)/shard_map/ppermute | solution.py:490
  10.6 0.0 collective-permute-done.refs_1_
  10.6 0.5 %collective-permute-start.1 = (f32[14,8,768]{2,1,0:T(8,128)}, f32[14,8,768]{2,1,0:T(8,128)S(1)}, u32[]{:S(2)}, u32[]{:S(2)}) collective-permute-start(f32[14,8,768]{2,1,0:T(8,128)} %get-tuple-element.41), channel_id=1, source_target_pairs={{0,2},{1,3},{2,0},{3,1},{4,6},{5,7},{6,4},{7,5},{8,10},{9,11},{10,... | collective-permute-start | bytes 1032200 | tf_op jit(solution)/shard_map/ppermute | solution.py:472
  11.7 0.1 pad_add_fusion.rank_ref.place_ref
  11.8 0.0 copy-start.1
  11.8 7.2 %levels.1 = (f32[14,32,768]{2,1,0:T(8,128)S(1)}, f32[8,768]{1,0:T(8,128)S(1)}, bf16[256,192]{1,0:T(8,128)(2,1)S(1)}, bf16[128,256]{1,0:T(8,128)(2,1)S(1)}, bf16[2,7,768,768]{3,2,1,0:T(8,128)(2,1)S(1)}) custom-call(s32[2]{0:T(128)S(1)} %pad_add_fusion.rank_ref.place_ref, s32[1]{0:T(128)S(6)} %copy.16.count_ref, s32[1,2048]{1,0:T(1,128)} %bus_hbm, ...), custom_call_target="tpu_custom_call" | custom-call | flops 1000 | bytes 1000 | tf_op jit(solution)/shard_map/levels/pallas_call | solution.py:221
  19.1 0.0 collective-permute-done.9.refs_7_
  19.1 0.0 collective-permute-done.8.refs_6_
  19.1 0.0 collective-permute-done.2.refs_3_
  19.1 0.5 %collective-permute-start.10 = (f32[448,128]{1,0:T(8,128)}, f32[448,128]{1,0:T(8,128)S(1)}, u32[]{:S(2)}, u32[]{:S(2)}) collective-permute-start(f32[448,128]{1,0:T(8,128)} %collective-permute-done.9.refs_7_), channel_id=1, source_target_pairs={{0,4},{4,0},{8,12},{12,8},{16,20},{20,16},{24,28},{28,24},{1,5},{5... | collective-permute-start | bytes 688136 | tf_op jit(solution)/shard_map/ppermute | solution.py:495
  19.5 0.0 collective-permute-done.11.refs_9_
  19.6 0.6 %collective-permute-start.12 = (f32[448,128]{1,0:T(8,128)}, f32[448,128]{1,0:T(8,128)S(1)}, u32[]{:S(2)}, u32[]{:S(2)}) collective-permute-start(f32[448,128]{1,0:T(8,128)} %collective-permute-done.9.refs_7_), channel_id=1, source_target_pairs={{0,8},{4,12},{8,16},{12,20},{16,24},{20,28},{24,0},{28,4},{1,9},{5... | collective-permute-start | bytes 688136 | tf_op jit(solution)/shard_map/ppermute | solution.py:490
  20.1 1.2 %collective-permute-done.1.refs_2_ = f32[14,8,768]{2,1,0:T(8,128)S(1)} collective-permute-done((f32[14,8,768]{2,1,0:T(8,128)}, f32[14,8,768]{2,1,0:T(8,128)S(1)}, u32[]{:S(2)}, u32[]{:S(2)}) %collective-permute-start.1) | collective-permute-done | bytes 344096 | tf_op jit(solution)/shard_map/ppermute | solution.py:472
  21.4 0.0 copy-done.1
  21.4 2.2 %wave.2 = (f32[4,112,128]{2,1,0:T(8,128)S(1)}, f32[4,112,128]{2,1,0:T(8,128)S(1)}, f32[4,112,128]{2,1,0:T(8,128)S(1)}, f32[4,112,128]{2,1,0:T(8,128)S(1)}) custom-call(s32[2]{0:T(128)S(1)} %pad_add_fusion.rank_ref.place_ref, bf16[256,192]{1,0:T(8,128)(2,1)S(1)} %get-tuple-element.39.there_ref, bf16[128,256]{1,0:T(8,128)(2,1)S(1)} %get-tuple-element.40.back_ref, ...), custom_call_target="tpu_custom_call" | custom-call | flops 1000 | bytes 1000 | tf_op jit(solution)/shard_map/wave/pallas_call | solution.py:119
  23.6 0.1 collective-permute-start.3
  23.7 1.7 %collective-permute-start.4 = (f32[4,112,128]{2,1,0:T(8,128)S(1)}, f32[4,112,128]{2,1,0:T(8,128)S(1)}, u32[]{:S(2)}, u32[]{:S(2)}) collective-permute-start(f32[4,112,128]{2,1,0:T(8,128)S(1)} %get-tuple-element.45), channel_id=1, source_target_pairs={{0,2},{1,3},{2,0},{3,1},{4,6},{5,7},{6,4},{7,5},{8,10},{9,11},{10,... | collective-permute-start | bytes 688136 | tf_op jit(solution)/shard_map/ppermute | solution.py:472
  25.4 1.5 %wave.3 = (f32[2,112,128]{2,1,0:T(8,128)S(1)}, f32[2,112,128]{2,1,0:T(8,128)S(1)}, f32[2,112,128]{2,1,0:T(8,128)S(1)}, f32[2,112,128]{2,1,0:T(8,128)S(1)}) custom-call(s32[2]{0:T(128)S(1)} %pad_add_fusion.rank_ref.place_ref, bf16[256,192]{1,0:T(8,128)(2,1)S(1)} %get-tuple-element.39.there_ref, bf16[128,256]{1,0:T(8,128)(2,1)S(1)} %get-tuple-element.40.back_ref, ...), custom_call_target="tpu_custom_call" | custom-call | flops 1000 | bytes 1000 | tf_op jit(solution)/shard_map/wave/pallas_call | solution.py:119
  26.9 0.2 collective-permute-start.6
  27.1 0.0 collective-permute-done.10.refs_8_
  27.1 0.3 collective-permute-start.5
  27.4 1.7 %collective-permute-done.12.refs_10_ = f32[448,128]{1,0:T(8,128)S(1)} collective-permute-done((f32[448,128]{1,0:T(8,128)}, f32[448,128]{1,0:T(8,128)S(1)}, u32[]{:S(2)}, u32[]{:S(2)}) %collective-permute-start.12) | collective-permute-done | bytes 229408 | tf_op jit(solution)/shard_map/ppermute | solution.py:490
  29.1 0.8 %collective-permute-start.14 = (f32[448,128]{1,0:T(8,128)S(1)}, f32[448,128]{1,0:T(8,128)S(1)}, u32[]{:S(2)}, u32[]{:S(2)}) collective-permute-start(f32[448,128]{1,0:T(8,128)S(1)} %collective-permute-done.11.refs_9_), channel_id=1, source_target_pairs={{0,4},{4,0},{8,12},{12,8},{16,20},{20,16},{24,28},{28,24},{1,5},{5... | collective-permute-start | bytes 688136 | tf_op jit(solution)/shard_map/ppermute | solution.py:495
  29.9 0.0 collective-permute-done.6.refs_5_
  29.9 1.2 %collective-permute-start.15 = (f32[448,128]{1,0:T(8,128)S(1)}, f32[448,128]{1,0:T(8,128)S(1)}, u32[]{:S(2)}, u32[]{:S(2)}) collective-permute-start(f32[448,128]{1,0:T(8,128)S(1)} %collective-permute-done.12.refs_10_), channel_id=1, source_target_pairs={{0,4},{4,0},{8,12},{12,8},{16,20},{20,16},{24,28},{28,24},{1,5},{5... | collective-permute-start | bytes 688136 | tf_op jit(solution)/shard_map/ppermute | solution.py:495
  31.1 2.5 %ties.1 = (f32[448,256]{1,0:T(8,128)S(1)}, bf16[256,256]{1,0:T(8,128)(2,1)S(1)}, f32[14,256]{1,0:T(8,128)S(1)}, bf16[128,256]{1,0:T(8,128)(2,1)S(1)}) custom-call(s32[2]{0:T(128)S(1)} %pad_add_fusion.rank_ref.place_ref, s32[1,256]{1,0:T(1,128)} %refs_0_.1, s32[1,256]{1,0:T(1,128)} %bitcast.25, s32[1,256]{1,0:T(1,128)} %refs_2_.1, f32[1,256]{1,0:T(1,128)} %refs_3_.1, ...), custom_call_target="tpu_custom_call" | custom-call | flops 1000 | bytes 1000 | tf_op jit(solution)/shard_map/ties/pallas_call | solution.py:300
  33.7 0.0 collective-permute-done.3.refs_5_
  33.7 0.6 %collective-permute-start.7 = (f32[2,112,128]{2,1,0:T(8,128)S(1)}, f32[2,112,128]{2,1,0:T(8,128)S(1)}, u32[]{:S(2)}, u32[]{:S(2)}) collective-permute-start(f32[2,112,128]{2,1,0:T(8,128)S(1)} %get-tuple-element.50), channel_id=1, source_target_pairs={{0,2},{1,3},{2,0},{3,1},{4,6},{5,7},{6,4},{7,5},{8,10},{9,11},{10,... | collective-permute-start | bytes 344072 | tf_op jit(solution)/shard_map/ppermute | solution.py:472
  34.3 0.0 collective-permute-done.4.refs_6_
  34.3 0.0 collective-permute-start.13
  34.3 2.0 %collective-permute-done.5.refs_7_ = f32[4,112,128]{2,1,0:T(8,128)S(1)} collective-permute-done((f32[4,112,128]{2,1,0:T(8,128)S(1)}, f32[4,112,128]{2,1,0:T(8,128)S(1)}, u32[]{:S(2)}, u32[]{:S(2)}) %collective-permute-start.5) | collective-permute-done | bytes 229408 | tf_op jit(solution)/shard_map/ppermute | solution.py:472
  36.2 4.0 %solve.2 = (f32[2,7,32,768]{3,2,1,0:T(8,128)S(1)}, f32[8,128]{1,0:T(8,128)S(1)}) custom-call(s32[2]{0:T(128)S(1)} %pad_add_fusion.rank_ref.place_ref, f32[2,7,32,768]{3,2,1,0:T(8,128)S(1)} %bitcast.16, f32[8,768]{1,0:T(8,128)S(1)} %get-tuple-element.37.refs_1_, bf16[2,7,768,768]{3,2,1,0:T(8,128)(2,1)S(1)} %get-tuple-element.38.refs_2_, ...), custom_call_target="tpu_custom_call" | custom-call | flops 1000 | bytes 1000 | tf_op jit(solution)/shard_map/solve/pallas_call | solution.py:433
  40.3 0.0 collective-permute-done.7.refs_6_
  40.3 0.5 %collective-permute-done.13.refs_7_ = f32[2,112,128]{2,1,0:T(8,128)S(1)} collective-permute-done((f32[2,112,128]{2,1,0:T(8,128)S(1)}, f32[2,112,128]{2,1,0:T(8,128)S(1)}, u32[]{:S(2)}, u32[]{:S(2)}) %collective-permute-start.13) | collective-permute-done | bytes 114720 | tf_op jit(solution)/shard_map/ppermute | solution.py:472
  40.7 0.0 collective-permute-done.14.refs_13_
  40.7 0.0 collective-permute-done.15.refs_14_
  40.7 3.6 %solve.3 = f32[2,7,32,768]{3,2,1,0:T(8,128)} custom-call(s32[2]{0:T(128)S(1)} %pad_add_fusion.rank_ref.place_ref, f32[2,7,32,768]{3,2,1,0:T(8,128)S(1)} %bitcast.17, f32[8,768]{1,0:T(8,128)S(1)} %get-tuple-element.37.refs_1_, bf16[2,7,768,768]{3,2,1,0:T(8,128)(2,1)S(1)} %get-tuple-element.38.refs_2_, f32[8,128]{1,0:T(8,128)S(1)} %get-tuple-element.47.refs_3_, ...), custom_call_target="tpu_custom_call" | custom-call | flops 1000 | bytes 1000 | tf_op jit(solution)/shard_map/solve/pallas_call | solution.py:433
  (1 shorter events, 0.0 us)
Async XLA Ops:
  0.0 2.1 %copy-start = (f32[2,1,7,32,768]{4,3,2,1,0:T(8,128)S(1)}, f32[2,1,7,32,768]{4,3,2,1,0:T(8,128)}, u32[]{:S(2)}) copy-start(f32[2,1,7,32,768]{4,3,2,1,0:T(8,128)} %param.14) | copy-start | bytes 4128772
  2.1 8.5 %collective-permute-start = (f32[14,32,768]{2,1,0:T(8,128)S(1)}, f32[14,32,768]{2,1,0:T(8,128)S(1)}, u32[]{:S(2)}, u32[]{:S(2)}) collective-permute-start(f32[14,32,768]{2,1,0:T(8,128)S(1)} %bitcast.13), channel_id=1, source_target_pairs={{0,1},{1,0},{2,3},{3,2},{4,5},{5,4},{6,7},{7,6},{8,9},{9,8},{10,11... | collective-permute-start | bytes 4128776 | tf_op jit(solution)/shard_map/ppermute | solution.py:472
  2.5 16.5 %collective-permute-start.2 = (f32[14,8,768]{2,1,0:T(8,128)}, f32[14,8,768]{2,1,0:T(8,128)S(1)}, u32[]{:S(2)}, u32[]{:S(2)}) collective-permute-start(f32[14,8,768]{2,1,0:T(8,128)} %get-tuple-element.42), channel_id=1, source_target_pairs={{0,3},{1,2},{2,1},{3,0},{4,7},{5,6},{6,5},{7,4},{8,11},{9,10},{10,... | collective-permute-start | bytes 1032200 | tf_op jit(solution)/shard_map/ppermute | solution.py:472
  5.2 13.9 %collective-permute-start.9 = (f32[448,128]{1,0:T(8,128)S(1)}, f32[448,128]{1,0:T(8,128)}, u32[]{:S(2)}, u32[]{:S(2)}) collective-permute-start(f32[448,128]{1,0:T(8,128)S(1)} %bitcast.18), channel_id=1, source_target_pairs={{0,8},{4,12},{8,16},{12,20},{16,24},{20,28},{24,0},{28,4},{1,9},{5... | collective-permute-start | bytes 688136 | tf_op jit(solution)/shard_map/ppermute | solution.py:490
  6.8 12.2 %collective-permute-start.8 = (f32[448,128]{1,0:T(8,128)S(1)}, f32[448,128]{1,0:T(8,128)}, u32[]{:S(2)}, u32[]{:S(2)}) collective-permute-start(f32[448,128]{1,0:T(8,128)S(1)} %bitcast.19), channel_id=1, source_target_pairs={{0,4},{4,0},{8,12},{12,8},{16,20},{20,16},{24,28},{28,24},{1,5},{5... | collective-permute-start | bytes 688136 | tf_op jit(solution)/shard_map/ppermute | solution.py:495
  8.3 11.3 %collective-permute-start.11 = (f32[448,128]{1,0:T(8,128)S(1)}, f32[448,128]{1,0:T(8,128)S(1)}, u32[]{:S(2)}, u32[]{:S(2)}) collective-permute-start(f32[448,128]{1,0:T(8,128)S(1)} %bitcast.20), channel_id=1, source_target_pairs={{0,24},{4,28},{8,0},{12,4},{16,8},{20,12},{24,16},{28,20},{1,25},{... | collective-permute-start | bytes 688136 | tf_op jit(solution)/shard_map/ppermute | solution.py:490
  10.6 10.8 %collective-permute-start.1 = (f32[14,8,768]{2,1,0:T(8,128)}, f32[14,8,768]{2,1,0:T(8,128)S(1)}, u32[]{:S(2)}, u32[]{:S(2)}) collective-permute-start(f32[14,8,768]{2,1,0:T(8,128)} %get-tuple-element.41), channel_id=1, source_target_pairs={{0,2},{1,3},{2,0},{3,1},{4,6},{5,7},{6,4},{7,5},{8,10},{9,11},{10,... | collective-permute-start | bytes 1032200 | tf_op jit(solution)/shard_map/ppermute | solution.py:472
  11.8 9.6 %copy-start.1 = (f32[2,1,7,32,768]{4,3,2,1,0:T(8,128)S(1)}, f32[2,1,7,32,768]{4,3,2,1,0:T(8,128)}, u32[]{:S(2)}) copy-start(f32[2,1,7,32,768]{4,3,2,1,0:T(8,128)} %param.14) | copy-start | bytes 4128772
  19.1 8.0 %collective-permute-start.10 = (f32[448,128]{1,0:T(8,128)}, f32[448,128]{1,0:T(8,128)S(1)}, u32[]{:S(2)}, u32[]{:S(2)}) collective-permute-start(f32[448,128]{1,0:T(8,128)} %collective-permute-done.9.refs_7_), channel_id=1, source_target_pairs={{0,4},{4,0},{8,12},{12,8},{16,20},{20,16},{24,28},{28,24},{1,5},{5... | collective-permute-start | bytes 688136 | tf_op jit(solution)/shard_map/ppermute | solution.py:495
  19.6 9.5 %collective-permute-start.12 = (f32[448,128]{1,0:T(8,128)}, f32[448,128]{1,0:T(8,128)S(1)}, u32[]{:S(2)}, u32[]{:S(2)}) collective-permute-start(f32[448,128]{1,0:T(8,128)} %collective-permute-done.9.refs_7_), channel_id=1, source_target_pairs={{0,8},{4,12},{8,16},{12,20},{16,24},{20,28},{24,0},{28,4},{1,9},{5... | collective-permute-start | bytes 688136 | tf_op jit(solution)/shard_map/ppermute | solution.py:490
  23.6 10.1 %collective-permute-start.3 = (f32[4,112,128]{2,1,0:T(8,128)S(1)}, f32[4,112,128]{2,1,0:T(8,128)S(1)}, u32[]{:S(2)}, u32[]{:S(2)}) collective-permute-start(f32[4,112,128]{2,1,0:T(8,128)S(1)} %get-tuple-element.44), channel_id=1, source_target_pairs={{0,1},{1,0},{2,3},{3,2},{4,5},{5,4},{6,7},{7,6},{8,9},{9,8},{10,11... | collective-permute-start | bytes 688136 | tf_op jit(solution)/shard_map/ppermute | solution.py:472
  23.7 10.6 %collective-permute-start.4 = (f32[4,112,128]{2,1,0:T(8,128)S(1)}, f32[4,112,128]{2,1,0:T(8,128)S(1)}, u32[]{:S(2)}, u32[]{:S(2)}) collective-permute-start(f32[4,112,128]{2,1,0:T(8,128)S(1)} %get-tuple-element.45), channel_id=1, source_target_pairs={{0,2},{1,3},{2,0},{3,1},{4,6},{5,7},{6,4},{7,5},{8,10},{9,11},{10,... | collective-permute-start | bytes 688136 | tf_op jit(solution)/shard_map/ppermute | solution.py:472
  26.9 3.0 %collective-permute-start.6 = (f32[2,112,128]{2,1,0:T(8,128)S(1)}, f32[2,112,128]{2,1,0:T(8,128)S(1)}, u32[]{:S(2)}, u32[]{:S(2)}) collective-permute-start(f32[2,112,128]{2,1,0:T(8,128)S(1)} %get-tuple-element.49), channel_id=1, source_target_pairs={{0,1},{1,0},{2,3},{3,2},{4,5},{5,4},{6,7},{7,6},{8,9},{9,8},{10,11... | collective-permute-start | bytes 344072 | tf_op jit(solution)/shard_map/ppermute | solution.py:472
  27.1 9.1 %collective-permute-start.5 = (f32[4,112,128]{2,1,0:T(8,128)S(1)}, f32[4,112,128]{2,1,0:T(8,128)S(1)}, u32[]{:S(2)}, u32[]{:S(2)}) collective-permute-start(f32[4,112,128]{2,1,0:T(8,128)S(1)} %get-tuple-element.46), channel_id=1, source_target_pairs={{0,3},{1,2},{2,1},{3,0},{4,7},{5,6},{6,5},{7,4},{8,11},{9,10},{10,... | collective-permute-start | bytes 688136 | tf_op jit(solution)/shard_map/ppermute | solution.py:472
  29.1 11.6 %collective-permute-start.14 = (f32[448,128]{1,0:T(8,128)S(1)}, f32[448,128]{1,0:T(8,128)S(1)}, u32[]{:S(2)}, u32[]{:S(2)}) collective-permute-start(f32[448,128]{1,0:T(8,128)S(1)} %collective-permute-done.11.refs_9_), channel_id=1, source_target_pairs={{0,4},{4,0},{8,12},{12,8},{16,20},{20,16},{24,28},{28,24},{1,5},{5... | collective-permute-start | bytes 688136 | tf_op jit(solution)/shard_map/ppermute | solution.py:495
  29.9 10.8 %collective-permute-start.15 = (f32[448,128]{1,0:T(8,128)S(1)}, f32[448,128]{1,0:T(8,128)S(1)}, u32[]{:S(2)}, u32[]{:S(2)}) collective-permute-start(f32[448,128]{1,0:T(8,128)S(1)} %collective-permute-done.12.refs_10_), channel_id=1, source_target_pairs={{0,4},{4,0},{8,12},{12,8},{16,20},{20,16},{24,28},{28,24},{1,5},{5... | collective-permute-start | bytes 688136 | tf_op jit(solution)/shard_map/ppermute | solution.py:495
  33.7 6.6 %collective-permute-start.7 = (f32[2,112,128]{2,1,0:T(8,128)S(1)}, f32[2,112,128]{2,1,0:T(8,128)S(1)}, u32[]{:S(2)}, u32[]{:S(2)}) collective-permute-start(f32[2,112,128]{2,1,0:T(8,128)S(1)} %get-tuple-element.50), channel_id=1, source_target_pairs={{0,2},{1,3},{2,0},{3,1},{4,6},{5,7},{6,4},{7,5},{8,10},{9,11},{10,... | collective-permute-start | bytes 344072 | tf_op jit(solution)/shard_map/ppermute | solution.py:472
  34.3 6.5 %collective-permute-start.13 = (f32[2,112,128]{2,1,0:T(8,128)S(1)}, f32[2,112,128]{2,1,0:T(8,128)S(1)}, u32[]{:S(2)}, u32[]{:S(2)}) collective-permute-start(f32[2,112,128]{2,1,0:T(8,128)S(1)} %get-tuple-element.56), channel_id=1, source_target_pairs={{0,3},{1,2},{2,1},{3,0},{4,7},{5,6},{6,5},{7,4},{8,11},{9,10},{10,... | collective-permute-start | bytes 344072 | tf_op jit(solution)/shard_map/ppermute | solution.py:472

commit v4 on v3

--- a/solution.py
+++ b/solution.py
@@ -150,6 +150,7 @@
     there_out,
     back_out,
     zinv_out,
+    turned_out,
     bus_ref,
     cond_ref,
     sat_ref,
@@ -165,7 +166,11 @@
         (inject_hbm, inject_ref),
         (there_ref.at[rank_ref[0]], there_out),
         (back_ref.at[rank_ref[0]], back_out),
-        (zinv_ref, zinv_out),
+    ]
+    pairs += [
+        (zinv_ref.at[c, h], zinv_out.at[c, h])
+        for h in range(zinv_ref.shape[1])
+        for c in range(2)
     ]
     copies = [
         pltpu.make_async_copy(*pair, sems.at[q]) for q, pair in enumerate(pairs)
@@ -202,11 +207,15 @@
         copy.wait()
     for row in range(volt_ref.shape[0]):
         base_ref[row] = inject_ref[row] + cond * volt_ref[row]
-    for copy in copies[5:]:
-        copy.wait()
-
-
-def levels(rank, dev_count, dev_bus, dev_cond, dev_sat, volt, inject, tables, zinv):
+    for copy in copies[5:7]:
+        copy.wait()
+    turned = turned_out.shape[2]
+    for q, copy in enumerate(copies[7:]):
+        copy.wait()
+        turned_out[q % 2, q // 2] = zinv_out[q % 2, q // 2, :, :turned].T
+
+
+def levels(rank, dev_count, dev_bus, dev_cond, dev_sat, volt, inject, tables, zinv, turned):
     slots = dev_bus.shape[1]
     buses = volt.shape[-1]
     step = 512 if slots % 512 == 0 else slots
@@ -221,16 +230,17 @@
     return pl.pallas_call(
         functools.partial(level_kernel, step),
         in_specs=[smem] * 2 + [anywhere] * len(inputs),
-        out_specs=[vmem] * 5,
+        out_specs=[vmem] * 6,
         out_shape=[
             pltpu.VMEM(volt.shape, F32),
             pltpu.VMEM((8, buses), F32),
             pltpu.VMEM(there.shape[1:], BF16),
             pltpu.VMEM(back.shape[1:], BF16),
             pltpu.VMEM(zinv.shape, BF16),
+            pltpu.VMEM(zinv.shape[:2] + (turned, buses), BF16),
         ],
         scratch_shapes=[pltpu.VMEM(each.shape, each.dtype) for each in inputs[:5]]
-        + [pltpu.SemaphoreType.DMA((len(inputs),))],
+        + [pltpu.SemaphoreType.DMA((len(inputs) + 2 * zinv.shape[1],))],
         compiler_params=pltpu.CompilerParams(vmem_limit_bytes=VMEM_BYTES),
         cost_estimate=SMALL,
         name="levels",
@@ -381,12 +391,16 @@
                     rhs = rhs + here
             parts.append(rhs.astype(BF16))
         both = jnp.concatenate(parts, axis=0)
-        by_real = lax.dot_general(
-            both, zinv_ref[0, h, :, lanes], NT_DIMS, preferred_element_type=F32
-        )
-        by_imag = lax.dot_general(
-            both, zinv_ref[1, h, :, lanes], NT_DIMS, preferred_element_type=F32
-        )
+        if last:
+            by_real = jnp.dot(both, zinv_ref[0, h], preferred_element_type=F32)
+            by_imag = jnp.dot(both, zinv_ref[1, h], preferred_element_type=F32)
+        else:
+            by_real = lax.dot_general(
+                both, zinv_ref[0, h, :, lanes], NT_DIMS, preferred_element_type=F32
+            )
+            by_imag = lax.dot_general(
+                both, zinv_ref[1, h, :, lanes], NT_DIMS, preferred_element_type=F32
+            )
         real = by_real[:scens] - by_imag[scens:]
         imag = by_real[scens:] + by_imag[:scens]
         if last:
@@ -496,7 +510,7 @@
 
     edge = after(edge, *pieces)
     blocks = [edge, exchange(edge)]
-    base, sat, there, back, held = levels(
+    base, sat, there, back, held, turned = levels(
         place,
         dev_count,
         after(dev_bus, sibling),
@@ -506,6 +520,7 @@
         inject.reshape(flat.shape),
         (jnp.asarray(there), jnp.asarray(back)),
         zinv,
+        sizes[-1],
     )
     def run_wave(index):
         return wave(
@@ -559,7 +574,7 @@
         place,
         base,
         sat,
-        (held, mark),
+        (turned, mark),
         shaped[1],
         (total, parts, late),
         starts[1],

time: 44.7 us -> 44 us (0.984)
    pallas_call x2, Pallas kernels: 7.64 us -> 6.99 us  [solve(): pl.pallas_call(functools.partial(solve_kernel, start, width, ranks, len(l...]
  transfers between devices with their start and end apart: 16 -> 16, of which waited for: 4 -> 4; matrix products, arithmetic and copies ran while one was open for 0% -> 0% of each run, Pallas kernels for 39% -> 40%
where the time goes in v4:
time: 44 us; the launch traced here: 43.7 us
  Pallas kernels  20.7 us (47%)
  starting transfers between devices  14.8 us (34%)
  waiting for transfers between devices  5.29 us (12%)
  local copies, waits for them, and re-layouts  2.11 us (5%)
  between operations  0.76 us (2%)
    pallas_call x1, Pallas kernels, levels(): pl.pallas_call(functools.partial(level_kernel, step), in_specs=[smem] * 2...  7.49 us
    pallas_call x2, Pallas kernels, solve(): pl.pallas_call(functools.partial(solve_kernel, start, width, ranks, len(l...  6.99 us
    ppermute x9, starting transfers between devices, swap(): return lax.ppermute(value, 'harm', [(i, i ^ k) for i in range(ranks)])  6.64 us
    ppermute x3, starting transfers between devices, shift(): lax.ppermute(value, 'area', [(a, (a + step) % areas) for a in range(areas)])  4.21 us
    ppermute x4, starting transfers between devices, exchange(): return lax.ppermute(value, 'area', [(a, a ^ 1) for a in range(areas)])  3.97 us
    pallas_call x2, Pallas kernels, wave(): pl.pallas_call(functools.partial(wave_kernel, len(sources), start, m_pad)...  3.65 us
    ppermute x9, waiting for transfers between devices, swap(): return lax.ppermute(value, 'harm', [(i, i ^ k) for i in range(ranks)])  3.58 us
    pallas_call x1, Pallas kernels, tie_parts(): pl.pallas_call(functools.partial(tie_kernel, h_local, areas, origins, lat...  2.53 us
  transfers between devices with their start and end apart: 16, of which 4 were waited for; matrix products, arithmetic and copies ran while one was open for 0% of the time, Pallas kernels for 40%

profile of v4, /device:TPU:0, one launch (start us, length us, event | category | flops | bytes accessed | tf_op | source)
XLA Modules:
  0.0 43.7 jit_solution(5442644234893894477)
XLA Ops:
  0.0 0.0 copy-start
  0.0 2.1 %constant_dynamic-slice_fusion = (f32[14,8,768]{2,1,0:T(8,128)}, f32[14,8,768]{2,1,0:T(8,128)}) fusion(f32[14,32,768]{2,1,0:T(8,128)} %bitcast.11, s32[]{:T(128)S(6)} %select_n.7, s32[]{:T(128)S(6)} %select_n.6), kind=kLoop, calls=%fused_computation.1 | loop fusion | bytes 1376264 | tf_op jit(solution)/shard_map/dynamic_slice | solution.py:493
  2.1 0.0 copy-done
  2.1 0.5 %collective-permute-start = (f32[14,32,768]{2,1,0:T(8,128)S(1)}, f32[14,32,768]{2,1,0:T(8,128)S(1)}, u32[]{:S(2)}, u32[]{:S(2)}) collective-permute-start(f32[14,32,768]{2,1,0:T(8,128)S(1)} %bitcast.13), channel_id=1, source_target_pairs={{0,1},{1,0},{2,3},{3,2},{4,5},{5,4},{6,7},{7,6},{8,9},{9,8},{10,11... | collective-permute-start | bytes 4128776 | tf_op jit(solution)/shard_map/ppermute | solution.py:486
  2.5 2.6 %collective-permute-start.2 = (f32[14,8,768]{2,1,0:T(8,128)}, f32[14,8,768]{2,1,0:T(8,128)S(1)}, u32[]{:S(2)}, u32[]{:S(2)}) collective-permute-start(f32[14,8,768]{2,1,0:T(8,128)} %get-tuple-element.44), channel_id=1, source_target_pairs={{0,3},{1,2},{2,1},{3,0},{4,7},{5,6},{6,5},{7,4},{8,11},{9,10},{10,... | collective-permute-start | bytes 1032200 | tf_op jit(solution)/shard_map/ppermute | solution.py:486
  5.2 1.6 %collective-permute-start.9 = (f32[448,128]{1,0:T(8,128)S(1)}, f32[448,128]{1,0:T(8,128)}, u32[]{:S(2)}, u32[]{:S(2)}) collective-permute-start(f32[448,128]{1,0:T(8,128)S(1)} %bitcast.18), channel_id=1, source_target_pairs={{0,8},{4,12},{8,16},{12,20},{16,24},{20,28},{24,0},{28,4},{1,9},{5... | collective-permute-start | bytes 688136 | tf_op jit(solution)/shard_map/ppermute | solution.py:504
  6.8 1.5 %collective-permute-start.8 = (f32[448,128]{1,0:T(8,128)S(1)}, f32[448,128]{1,0:T(8,128)}, u32[]{:S(2)}, u32[]{:S(2)}) collective-permute-start(f32[448,128]{1,0:T(8,128)S(1)} %bitcast.19), channel_id=1, source_target_pairs={{0,4},{4,0},{8,12},{12,8},{16,20},{20,16},{24,28},{28,24},{1,5},{5... | collective-permute-start | bytes 688136 | tf_op jit(solution)/shard_map/ppermute | solution.py:509
  8.3 2.2 %collective-permute-start.11 = (f32[448,128]{1,0:T(8,128)S(1)}, f32[448,128]{1,0:T(8,128)S(1)}, u32[]{:S(2)}, u32[]{:S(2)}) collective-permute-start(f32[448,128]{1,0:T(8,128)S(1)} %bitcast.20), channel_id=1, source_target_pairs={{0,24},{4,28},{8,0},{12,4},{16,8},{20,12},{24,16},{28,20},{1,25},{... | collective-permute-start | bytes 688136 | tf_op jit(solution)/shard_map/ppermute | solution.py:504
  10.6 0.0 collective-permute-done.refs_1_
  10.6 0.5 %collective-permute-start.1 = (f32[14,8,768]{2,1,0:T(8,128)}, f32[14,8,768]{2,1,0:T(8,128)S(1)}, u32[]{:S(2)}, u32[]{:S(2)}) collective-permute-start(f32[14,8,768]{2,1,0:T(8,128)} %get-tuple-element.43), channel_id=1, source_target_pairs={{0,2},{1,3},{2,0},{3,1},{4,6},{5,7},{6,4},{7,5},{8,10},{9,11},{10,... | collective-permute-start | bytes 1032200 | tf_op jit(solution)/shard_map/ppermute | solution.py:486
  11.7 0.1 pad_add_fusion.rank_ref.place_ref
  11.8 0.0 copy-start.1
  11.8 7.5 %levels.1 = (f32[14,32,768]{2,1,0:T(8,128)S(1)}, f32[8,768]{1,0:T(8,128)S(1)}, bf16[256,192]{1,0:T(8,128)(2,1)S(1)}, bf16[128,256]{1,0:T(8,128)(2,1)S(1)}, bf16[...) custom-call(s32[2]{0:T(128)S(1)} %pad_add_fusion.rank_ref.place_ref, s32[1]{0:T(128)S(6)} %copy.16.count_ref, ...), custom_call_target="tpu_custom_call" | custom-call | flops 1000 | bytes 1000 | tf_op jit(solution)/shard_map/levels/pallas_call | solution.py:230
  19.3 0.0 collective-permute-done.9.refs_7_
  19.3 0.0 collective-permute-done.8.refs_6_
  19.3 0.0 collective-permute-done.2.refs_3_
  19.3 0.5 %collective-permute-start.10 = (f32[448,128]{1,0:T(8,128)}, f32[448,128]{1,0:T(8,128)S(1)}, u32[]{:S(2)}, u32[]{:S(2)}) collective-permute-start(f32[448,128]{1,0:T(8,128)} %collective-permute-done.9.refs_7_), channel_id=1, source_target_pairs={{0,4},{4,0},{8,12},{12,8},{16,20},{20,16},{24,28},{28,24},{1,5},{5... | collective-permute-start | bytes 688136 | tf_op jit(solution)/shard_map/ppermute | solution.py:509
  19.8 0.0 collective-permute-done.11.refs_9_
  19.8 0.3 collective-permute-start.12
  20.1 1.2 %collective-permute-done.1.refs_2_ = f32[14,8,768]{2,1,0:T(8,128)S(1)} collective-permute-done((f32[14,8,768]{2,1,0:T(8,128)}, f32[14,8,768]{2,1,0:T(8,128)S(1)}, u32[]{:S(2)}, u32[]{:S(2)}) %collective-permute-start.1) | collective-permute-done | bytes 344096 | tf_op jit(solution)/shard_map/ppermute | solution.py:486
  21.4 0.0 copy-done.1
  21.4 2.2 %wave.2 = (f32[4,112,128]{2,1,0:T(8,128)S(1)}, f32[4,112,128]{2,1,0:T(8,128)S(1)}, f32[4,112,128]{2,1,0:T(8,128)S(1)}, f32[4,112,128]{2,1,0:T(8,128)S(1)}) custom-call(s32[2]{0:T(128)S(1)} %pad_add_fusion.rank_ref.place_ref, bf16[256,192]{1,0:T(8,128)(2,1)S(1)} %get-tuple-element.41.there_ref, bf16[128,256]{1,0:T(8,128)(2,1)S(1)} %get-tuple-element.42.back_ref, ...), custom_call_target="tpu_custom_call" | custom-call | flops 1000 | bytes 1000 | tf_op jit(solution)/shard_map/wave/pallas_call | solution.py:119
  23.6 0.1 collective-permute-start.3
  23.7 1.7 %collective-permute-start.4 = (f32[4,112,128]{2,1,0:T(8,128)S(1)}, f32[4,112,128]{2,1,0:T(8,128)S(1)}, u32[]{:S(2)}, u32[]{:S(2)}) collective-permute-start(f32[4,112,128]{2,1,0:T(8,128)S(1)} %get-tuple-element.47), channel_id=1, source_target_pairs={{0,2},{1,3},{2,0},{3,1},{4,6},{5,7},{6,4},{7,5},{8,10},{9,11},{10,... | collective-permute-start | bytes 688136 | tf_op jit(solution)/shard_map/ppermute | solution.py:486
  25.4 1.5 %wave.3 = (f32[2,112,128]{2,1,0:T(8,128)S(1)}, f32[2,112,128]{2,1,0:T(8,128)S(1)}, f32[2,112,128]{2,1,0:T(8,128)S(1)}, f32[2,112,128]{2,1,0:T(8,128)S(1)}) custom-call(s32[2]{0:T(128)S(1)} %pad_add_fusion.rank_ref.place_ref, bf16[256,192]{1,0:T(8,128)(2,1)S(1)} %get-tuple-element.41.there_ref, bf16[128,256]{1,0:T(8,128)(2,1)S(1)} %get-tuple-element.42.back_ref, ...), custom_call_target="tpu_custom_call" | custom-call | flops 1000 | bytes 1000 | tf_op jit(solution)/shard_map/wave/pallas_call | solution.py:119
  26.9 0.2 collective-permute-start.6
  27.1 0.0 collective-permute-done.10.refs_8_
  27.1 0.3 collective-permute-start.5
  27.4 1.7 %collective-permute-done.12.refs_10_ = f32[448,128]{1,0:T(8,128)S(1)} collective-permute-done((f32[448,128]{1,0:T(8,128)}, f32[448,128]{1,0:T(8,128)S(1)}, u32[]{:S(2)}, u32[]{:S(2)}) %collective-permute-start.12) | collective-permute-done | bytes 229408 | tf_op jit(solution)/shard_map/ppermute | solution.py:504
  29.1 0.8 %collective-permute-start.14 = (f32[448,128]{1,0:T(8,128)S(1)}, f32[448,128]{1,0:T(8,128)S(1)}, u32[]{:S(2)}, u32[]{:S(2)}) collective-permute-start(f32[448,128]{1,0:T(8,128)S(1)} %collective-permute-done.11.refs_9_), channel_id=1, source_target_pairs={{0,4},{4,0},{8,12},{12,8},{16,20},{20,16},{24,28},{28,24},{1,5},{5... | collective-permute-start | bytes 688136 | tf_op jit(solution)/shard_map/ppermute | solution.py:509
  29.9 0.0 collective-permute-done.6.refs_5_
  29.9 1.2 %collective-permute-start.15 = (f32[448,128]{1,0:T(8,128)S(1)}, f32[448,128]{1,0:T(8,128)S(1)}, u32[]{:S(2)}, u32[]{:S(2)}) collective-permute-start(f32[448,128]{1,0:T(8,128)S(1)} %collective-permute-done.12.refs_10_), channel_id=1, source_target_pairs={{0,4},{4,0},{8,12},{12,8},{16,20},{20,16},{24,28},{28,24},{1,5},{5... | collective-permute-start | bytes 688136 | tf_op jit(solution)/shard_map/ppermute | solution.py:509
  31.1 2.5 %ties.1 = (f32[448,256]{1,0:T(8,128)S(1)}, bf16[256,256]{1,0:T(8,128)(2,1)S(1)}, f32[14,256]{1,0:T(8,128)S(1)}, bf16[128,256]{1,0:T(8,128)(2,1)S(1)}) custom-call(s32[2]{0:T(128)S(1)} %pad_add_fusion.rank_ref.place_ref, s32[1,256]{1,0:T(1,128)} %refs_0_.1, s32[1,256]{1,0:T(1,128)} %bitcast.25, s32[1,256]{1,0:T(1,128)} %refs_2_.1, f32[1,256]{1,0:T(1,128)} %refs_3_.1, ...), custom_call_target="tpu_custom_call" | custom-call | flops 1000 | bytes 1000 | tf_op jit(solution)/shard_map/ties/pallas_call | solution.py:310
  33.7 0.0 collective-permute-done.3.refs_5_
  33.7 0.7 %collective-permute-start.7 = (f32[2,112,128]{2,1,0:T(8,128)S(1)}, f32[2,112,128]{2,1,0:T(8,128)S(1)}, u32[]{:S(2)}, u32[]{:S(2)}) collective-permute-start(f32[2,112,128]{2,1,0:T(8,128)S(1)} %get-tuple-element.52), channel_id=1, source_target_pairs={{0,2},{1,3},{2,0},{3,1},{4,6},{5,7},{6,4},{7,5},{8,10},{9,11},{10,... | collective-permute-start | bytes 344072 | tf_op jit(solution)/shard_map/ppermute | solution.py:486
  34.4 0.0 collective-permute-done.4.refs_6_
  34.4 0.0 collective-permute-start.13
  34.4 1.8 %collective-permute-done.5.refs_7_ = f32[4,112,128]{2,1,0:T(8,128)S(1)} collective-permute-done((f32[4,112,128]{2,1,0:T(8,128)S(1)}, f32[4,112,128]{2,1,0:T(8,128)S(1)}, u32[]{:S(2)}, u32[]{:S(2)}) %collective-permute-start.5) | collective-permute-done | bytes 229408 | tf_op jit(solution)/shard_map/ppermute | solution.py:486
  36.2 4.0 %solve.2 = (f32[2,7,32,768]{3,2,1,0:T(8,128)S(1)}, f32[8,128]{1,0:T(8,128)S(1)}) custom-call(s32[2]{0:T(128)S(1)} %pad_add_fusion.rank_ref.place_ref, f32[2,7,32,768]{3,2,1,0:T(8,128)S(1)} %bitcast.16, f32[8,768]{1,0:T(8,128)S(1)} %get-tuple-element.38.refs_1_, bf16[2,7,768,768]{3,2,1,0:T(8,128)(2,1)S(1)} %get-tuple-element.40.refs_2_, ...), custom_call_target="tpu_custom_call" | custom-call | flops 1000 | bytes 1000 | tf_op jit(solution)/shard_map/solve/pallas_call | solution.py:447
  40.2 0.0 collective-permute-done.7.refs_6_
  40.3 0.5 %collective-permute-done.13.refs_7_ = f32[2,112,128]{2,1,0:T(8,128)S(1)} collective-permute-done((f32[2,112,128]{2,1,0:T(8,128)S(1)}, f32[2,112,128]{2,1,0:T(8,128)S(1)}, u32[]{:S(2)}, u32[]{:S(2)}) %collective-permute-start.13) | collective-permute-done | bytes 114720 | tf_op jit(solution)/shard_map/ppermute | solution.py:486
  40.7 0.0 collective-permute-done.14.refs_13_
  40.7 0.0 collective-permute-done.15.refs_14_
  40.7 3.0 %solve.3 = f32[2,7,32,768]{3,2,1,0:T(8,128)} custom-call(s32[2]{0:T(128)S(1)} %pad_add_fusion.rank_ref.place_ref, f32[2,7,32,768]{3,2,1,0:T(8,128)S(1)} %bitcast.17, f32[8,768]{1,0:T(8,128)S(1)} %get-tuple-element.38.refs_1_, bf16[2,7,256,768]{3,2,1,0:T(8,128)(2,1)S(1)} %get-tuple-element.39.refs_2_, f32[8,128]{1,0:T(8,128)S(1)} %get-tuple-element.49.refs_3_, ...), custom_call_target="tpu_custom_call" | custom-call | flops 1000 | bytes 1000 | tf_op jit(solution)/shard_map/solve/pallas_call | solution.py:447
  (1 shorter events, 0.0 us)
Async XLA Ops:
  0.0 2.1 %copy-start = (f32[2,1,7,32,768]{4,3,2,1,0:T(8,128)S(1)}, f32[2,1,7,32,768]{4,3,2,1,0:T(8,128)}, u32[]{:S(2)}) copy-start(f32[2,1,7,32,768]{4,3,2,1,0:T(8,128)} %param.14) | copy-start | bytes 4128772
  2.1 8.5 %collective-permute-start = (f32[14,32,768]{2,1,0:T(8,128)S(1)}, f32[14,32,768]{2,1,0:T(8,128)S(1)}, u32[]{:S(2)}, u32[]{:S(2)}) collective-permute-start(f32[14,32,768]{2,1,0:T(8,128)S(1)} %bitcast.13), channel_id=1, source_target_pairs={{0,1},{1,0},{2,3},{3,2},{4,5},{5,4},{6,7},{7,6},{8,9},{9,8},{10,11... | collective-permute-start | bytes 4128776 | tf_op jit(solution)/shard_map/ppermute | solution.py:486
  2.5 16.8 %collective-permute-start.2 = (f32[14,8,768]{2,1,0:T(8,128)}, f32[14,8,768]{2,1,0:T(8,128)S(1)}, u32[]{:S(2)}, u32[]{:S(2)}) collective-permute-start(f32[14,8,768]{2,1,0:T(8,128)} %get-tuple-element.44), channel_id=1, source_target_pairs={{0,3},{1,2},{2,1},{3,0},{4,7},{5,6},{6,5},{7,4},{8,11},{9,10},{10,... | collective-permute-start | bytes 1032200 | tf_op jit(solution)/shard_map/ppermute | solution.py:486
  5.2 14.1 %collective-permute-start.9 = (f32[448,128]{1,0:T(8,128)S(1)}, f32[448,128]{1,0:T(8,128)}, u32[]{:S(2)}, u32[]{:S(2)}) collective-permute-start(f32[448,128]{1,0:T(8,128)S(1)} %bitcast.18), channel_id=1, source_target_pairs={{0,8},{4,12},{8,16},{12,20},{16,24},{20,28},{24,0},{28,4},{1,9},{5... | collective-permute-start | bytes 688136 | tf_op jit(solution)/shard_map/ppermute | solution.py:504
  6.8 12.5 %collective-permute-start.8 = (f32[448,128]{1,0:T(8,128)S(1)}, f32[448,128]{1,0:T(8,128)}, u32[]{:S(2)}, u32[]{:S(2)}) collective-permute-start(f32[448,128]{1,0:T(8,128)S(1)} %bitcast.19), channel_id=1, source_target_pairs={{0,4},{4,0},{8,12},{12,8},{16,20},{20,16},{24,28},{28,24},{1,5},{5... | collective-permute-start | bytes 688136 | tf_op jit(solution)/shard_map/ppermute | solution.py:509
  8.3 11.5 %collective-permute-start.11 = (f32[448,128]{1,0:T(8,128)S(1)}, f32[448,128]{1,0:T(8,128)S(1)}, u32[]{:S(2)}, u32[]{:S(2)}) collective-permute-start(f32[448,128]{1,0:T(8,128)S(1)} %bitcast.20), channel_id=1, source_target_pairs={{0,24},{4,28},{8,0},{12,4},{16,8},{20,12},{24,16},{28,20},{1,25},{... | collective-permute-start | bytes 688136 | tf_op jit(solution)/shard_map/ppermute | solution.py:504
  10.6 10.8 %collective-permute-start.1 = (f32[14,8,768]{2,1,0:T(8,128)}, f32[14,8,768]{2,1,0:T(8,128)S(1)}, u32[]{:S(2)}, u32[]{:S(2)}) collective-permute-start(f32[14,8,768]{2,1,0:T(8,128)} %get-tuple-element.43), channel_id=1, source_target_pairs={{0,2},{1,3},{2,0},{3,1},{4,6},{5,7},{6,4},{7,5},{8,10},{9,11},{10,... | collective-permute-start | bytes 1032200 | tf_op jit(solution)/shard_map/ppermute | solution.py:486
  11.8 9.6 %copy-start.1 = (f32[2,1,7,32,768]{4,3,2,1,0:T(8,128)S(1)}, f32[2,1,7,32,768]{4,3,2,1,0:T(8,128)}, u32[]{:S(2)}) copy-start(f32[2,1,7,32,768]{4,3,2,1,0:T(8,128)} %param.14) | copy-start | bytes 4128772
  19.3 7.8 %collective-permute-start.10 = (f32[448,128]{1,0:T(8,128)}, f32[448,128]{1,0:T(8,128)S(1)}, u32[]{:S(2)}, u32[]{:S(2)}) collective-permute-start(f32[448,128]{1,0:T(8,128)} %collective-permute-done.9.refs_7_), channel_id=1, source_target_pairs={{0,4},{4,0},{8,12},{12,8},{16,20},{20,16},{24,28},{28,24},{1,5},{5... | collective-permute-start | bytes 688136 | tf_op jit(solution)/shard_map/ppermute | solution.py:509
  19.8 9.3 %collective-permute-start.12 = (f32[448,128]{1,0:T(8,128)}, f32[448,128]{1,0:T(8,128)S(1)}, u32[]{:S(2)}, u32[]{:S(2)}) collective-permute-start(f32[448,128]{1,0:T(8,128)} %collective-permute-done.9.refs_7_), channel_id=1, source_target_pairs={{0,8},{4,12},{8,16},{12,20},{16,24},{20,28},{24,0},{28,4},{1,9},{5... | collective-permute-start | bytes 688136 | tf_op jit(solution)/shard_map/ppermute | solution.py:504
  23.6 10.1 %collective-permute-start.3 = (f32[4,112,128]{2,1,0:T(8,128)S(1)}, f32[4,112,128]{2,1,0:T(8,128)S(1)}, u32[]{:S(2)}, u32[]{:S(2)}) collective-permute-start(f32[4,112,128]{2,1,0:T(8,128)S(1)} %get-tuple-element.46), channel_id=1, source_target_pairs={{0,1},{1,0},{2,3},{3,2},{4,5},{5,4},{6,7},{7,6},{8,9},{9,8},{10,11... | collective-permute-start | bytes 688136 | tf_op jit(solution)/shard_map/ppermute | solution.py:486
  23.7 10.7 %collective-permute-start.4 = (f32[4,112,128]{2,1,0:T(8,128)S(1)}, f32[4,112,128]{2,1,0:T(8,128)S(1)}, u32[]{:S(2)}, u32[]{:S(2)}) collective-permute-start(f32[4,112,128]{2,1,0:T(8,128)S(1)} %get-tuple-element.47), channel_id=1, source_target_pairs={{0,2},{1,3},{2,0},{3,1},{4,6},{5,7},{6,4},{7,5},{8,10},{9,11},{10,... | collective-permute-start | bytes 688136 | tf_op jit(solution)/shard_map/ppermute | solution.py:486
  26.9 3.0 %collective-permute-start.6 = (f32[2,112,128]{2,1,0:T(8,128)S(1)}, f32[2,112,128]{2,1,0:T(8,128)S(1)}, u32[]{:S(2)}, u32[]{:S(2)}) collective-permute-start(f32[2,112,128]{2,1,0:T(8,128)S(1)} %get-tuple-element.51), channel_id=1, source_target_pairs={{0,1},{1,0},{2,3},{3,2},{4,5},{5,4},{6,7},{7,6},{8,9},{9,8},{10,11... | collective-permute-start | bytes 344072 | tf_op jit(solution)/shard_map/ppermute | solution.py:486
  27.1 9.1 %collective-permute-start.5 = (f32[4,112,128]{2,1,0:T(8,128)S(1)}, f32[4,112,128]{2,1,0:T(8,128)S(1)}, u32[]{:S(2)}, u32[]{:S(2)}) collective-permute-start(f32[4,112,128]{2,1,0:T(8,128)S(1)} %get-tuple-element.48), channel_id=1, source_target_pairs={{0,3},{1,2},{2,1},{3,0},{4,7},{5,6},{6,5},{7,4},{8,11},{9,10},{10,... | collective-permute-start | bytes 688136 | tf_op jit(solution)/shard_map/ppermute | solution.py:486
  29.1 11.6 %collective-permute-start.14 = (f32[448,128]{1,0:T(8,128)S(1)}, f32[448,128]{1,0:T(8,128)S(1)}, u32[]{:S(2)}, u32[]{:S(2)}) collective-permute-start(f32[448,128]{1,0:T(8,128)S(1)} %collective-permute-done.11.refs_9_), channel_id=1, source_target_pairs={{0,4},{4,0},{8,12},{12,8},{16,20},{20,16},{24,28},{28,24},{1,5},{5... | collective-permute-start | bytes 688136 | tf_op jit(solution)/shard_map/ppermute | solution.py:509
  29.9 10.8 %collective-permute-start.15 = (f32[448,128]{1,0:T(8,128)S(1)}, f32[448,128]{1,0:T(8,128)S(1)}, u32[]{:S(2)}, u32[]{:S(2)}) collective-permute-start(f32[448,128]{1,0:T(8,128)S(1)} %collective-permute-done.12.refs_10_), channel_id=1, source_target_pairs={{0,4},{4,0},{8,12},{12,8},{16,20},{20,16},{24,28},{28,24},{1,5},{5... | collective-permute-start | bytes 688136 | tf_op jit(solution)/shard_map/ppermute | solution.py:509
  33.7 6.6 %collective-permute-start.7 = (f32[2,112,128]{2,1,0:T(8,128)S(1)}, f32[2,112,128]{2,1,0:T(8,128)S(1)}, u32[]{:S(2)}, u32[]{:S(2)}) collective-permute-start(f32[2,112,128]{2,1,0:T(8,128)S(1)} %get-tuple-element.52), channel_id=1, source_target_pairs={{0,2},{1,3},{2,0},{3,1},{4,6},{5,7},{6,4},{7,5},{8,10},{9,11},{10,... | collective-permute-start | bytes 344072 | tf_op jit(solution)/shard_map/ppermute | solution.py:486
  34.4 6.3 %collective-permute-start.13 = (f32[2,112,128]{2,1,0:T(8,128)S(1)}, f32[2,112,128]{2,1,0:T(8,128)S(1)}, u32[]{:S(2)}, u32[]{:S(2)}) collective-permute-start(f32[2,112,128]{2,1,0:T(8,128)S(1)} %get-tuple-element.58), channel_id=1, source_target_pairs={{0,3},{1,2},{2,1},{3,0},{4,7},{5,6},{6,5},{7,4},{8,11},{9,10},{10,... | collective-permute-start | bytes 344072 | tf_op jit(solution)/shard_map/ppermute | solution.py:486

commit v5 on v4

--- a/solution.py
+++ b/solution.py
@@ -66,6 +66,36 @@
         high, low = np_split(back)
         inverse.append(np.concatenate([high, low], axis=0))
     return np.stack(forward), np.stack(inverse), k_pad, m_pad
+
+
+def piece_kernel(partners, place_ref, volt_ref, *refs):
+    outs, sems = refs[:-1], refs[-1]
+    copies = []
+    for q, (out, k) in enumerate(zip(outs, partners)):
+        part = out.shape[1]
+        at = pl.ds(pl.multiple_of((place_ref[0] ^ k) * part, 8), part)
+        copies.append(pltpu.make_async_copy(volt_ref.at[:, at], out, sems.at[q]))
+    for copy in copies:
+        copy.start()
+    for copy in copies:
+        copy.wait()
+
+
+def send_pieces(place, volt, partners, part):
+    shape = jax.ShapeDtypeStruct((volt.shape[0], part, volt.shape[2]), F32)
+    vmem = pl.BlockSpec(memory_space=pltpu.VMEM)
+    return pl.pallas_call(
+        functools.partial(piece_kernel, partners),
+        in_specs=[
+            pl.BlockSpec(memory_space=pltpu.SMEM),
+            pl.BlockSpec(memory_space=pl.ANY),
+        ],
+        out_specs=[vmem] * len(partners),
+        out_shape=[pltpu.VMEM(shape.shape, F32)] * len(partners),
+        scratch_shapes=[pltpu.SemaphoreType.DMA((len(partners),))],
+        cost_estimate=SMALL,
+        name="pieces",
+    )(place, volt)
 
 
 def wave_kernel(source_count, start, m_pad, rank_ref, there_ref, back_ref, *refs):
@@ -488,11 +518,13 @@
     sizes = chunk_sizes(buses)
     starts = [buses - sum(sizes[: i + 1]) for i in range(len(sizes))]
 
-    def piece(k):
-        at = (0, (rank ^ k) * part, 0)
-        return lax.dynamic_slice(flat, at, (rows, part, buses))
-
-    pieces = [piece(k) for k in range(ranks - 1, 1, -1)]
+    partners = tuple(range(ranks - 1, 1, -1))
+    pieces = send_pieces(
+        jnp.full((1,), rank, jnp.int32),
+        pltpu.with_memory_space_constraint(flat, pltpu.HBM),
+        partners,
+        part,
+    )
     flat_now, *pieces = lax.optimization_barrier((flat, *pieces))
     far = [swap(each, ranks - 1 - q) for q, each in enumerate(pieces)]
     sibling = swap(flat_now, 1)

time: 44 us -> 44.9 us (1.020)
  Pallas kernels: 20.7 us -> 22 us
  local copies, waits for them, and re-layouts: 2.11 us -> 1.44 us
    dynamic_slice x1 -> x0, local copies, waits for them, and re-layouts: 2.08 us -> none  [piece(): return lax.dynamic_slice(flat, at, (rows, part, buses))]
    ppermute x9, waiting for transfers between devices: 3.58 us -> 1.74 us  [swap(): return lax.ppermute(value, 'harm', [(i, i ^ k) for i in range(ranks)])]
    pallas_call x0 -> x1, Pallas kernels: none -> 1.21 us  [send_pieces(): pl.pallas_call(functools.partial(piece_kernel, partners), in_specs=[pl.Bl...]
    ppermute x3, waiting for transfers between devices: 1.7 us -> 2.85 us  [shift(): lax.ppermute(value, 'area', [(a, (a + step) % areas) for a in range(areas)])]
    ppermute x4, waiting for transfers between devices: 0.01 us -> 1.14 us  [exchange(): return lax.ppermute(value, 'area', [(a, a ^ 1) for a in range(areas)])]
    unnamed x4 -> x8, local copies, waits for them, and re-layouts: 0.01 us -> 0.74 us
    slice x1, local copies, waits for them, and re-layouts: 0.02 us -> 0.7 us  [per_device(): edge = volt[..., :NBD].reshape(rows * scens, NBD)]
  transfers between devices with their start and end apart: 16 -> 16, of which waited for: 4 -> 6; matrix products, arithmetic and copies ran while one was open for 0% -> 2% of each run, Pallas kernels for 40% -> 40%
where the time goes in v5:
time: 44.9 us; the launch traced here: 44.7 us
  Pallas kernels  22 us (49%)
  starting transfers between devices  14.8 us (33%)
  waiting for transfers between devices  5.73 us (13%)
  local copies, waits for them, and re-layouts  1.44 us (3%)
  between operations  0.77 us (2%)
    pallas_call x1, Pallas kernels, levels(): pl.pallas_call(functools.partial(level_kernel, step), in_specs=[smem] * 2...  7.49 us
    pallas_call x2, Pallas kernels, solve(): pl.pallas_call(functools.partial(solve_kernel, start, width, ranks, len(l...  6.99 us
    ppermute x9, starting transfers between devices, swap(): return lax.ppermute(value, 'harm', [(i, i ^ k) for i in range(ranks)])  6.48 us
    ppermute x3, starting transfers between devices, shift(): lax.ppermute(value, 'area', [(a, (a + step) % areas) for a in range(areas)])  4.39 us
    ppermute x4, starting transfers between devices, exchange(): return lax.ppermute(value, 'area', [(a, a ^ 1) for a in range(areas)])  3.9 us
    pallas_call x2, Pallas kernels, wave(): pl.pallas_call(functools.partial(wave_kernel, len(sources), start, m_pad)...  3.66 us
    ppermute x3, waiting for transfers between devices, shift(): lax.ppermute(value, 'area', [(a, (a + step) % areas) for a in range(areas)])  2.85 us
    pallas_call x1, Pallas kernels, tie_parts(): pl.pallas_call(functools.partial(tie_kernel, h_local, areas, origins, lat...  2.6 us
  transfers between devices with their start and end apart: 16, of which 6 were waited for; matrix products, arithmetic and copies ran while one was open for 2% of the time, Pallas kernels for 40%

profile of v5, /device:TPU:0, one launch (start us, length us, event | category | flops | bytes accessed | tf_op | source)
XLA Modules:
  0.0 44.7 jit_solution(1493906347665650685)
XLA Ops:
  0.0 0.0 copy-start
  0.0 1.2 %pieces.1 = (f32[14,8,768]{2,1,0:T(8,128)S(1)}, f32[14,8,768]{2,1,0:T(8,128)S(1)}) custom-call(s32[1]{0:T(128)} %bitcast.place_ref, f32[14,32,768]{2,1,0:T(8,128)} %bitcast.11), custom_call_target="tpu_custom_call" | custom-call | flops 1000 | bytes 1000 | tf_op jit(solution)/shard_map/pieces/pallas_call | solution.py:87
  1.2 0.0 copy-start.3
  1.2 0.7 %copy-done.3 = f32[14,8,768]{2,1,0:T(8,128)} copy-done((f32[14,8,768]{2,1,0:T(8,128)}, f32[14,8,768]{2,1,0:T(8,128)S(1)}, u32[]{:S(2)}) %copy-start.3) | copy-done | bytes 344088
  2.0 0.0 copy-start.2
  2.0 0.0 copy-done
  2.0 0.5 %collective-permute-start = (f32[14,32,768]{2,1,0:T(8,128)S(1)}, f32[14,32,768]{2,1,0:T(8,128)S(1)}, u32[]{:S(2)}, u32[]{:S(2)}) collective-permute-start(f32[14,32,768]{2,1,0:T(8,128)S(1)} %bitcast.13), channel_id=1, source_target_pairs={{0,1},{1,0},{2,3},{3,2},{4,5},{5,4},{6,7},{7,6},{8,9},{9,8},{10,11... | collective-permute-start | bytes 4128776 | tf_op jit(solution)/shard_map/ppermute | solution.py:516
  2.4 2.6 %collective-permute-start.2 = (f32[14,8,768]{2,1,0:T(8,128)}, f32[14,8,768]{2,1,0:T(8,128)S(1)}, u32[]{:S(2)}, u32[]{:S(2)}) collective-permute-start(f32[14,8,768]{2,1,0:T(8,128)} %copy-done.3), channel_id=1, source_target_pairs={{0,3},{1,2},{2,1},{3,0},{4,7},{5,6},{6,5},{7,4},{8,11},{9,10},{10,... | collective-permute-start | bytes 1032200 | tf_op jit(solution)/shard_map/ppermute | solution.py:516
  5.0 0.7 %slice.3 = f32[2,1,7,32,128]{4,3,2,1,0:T(8,128)} slice(f32[2,1,7,32,768]{4,3,2,1,0:T(8,128)S(1)} %copy-done), slice={[0:2], [0:1], [0:7], [0:32], [0:128]} | slice | bytes 458752 | tf_op jit(solution)/shard_map/slice | solution.py:533
  5.7 1.6 %collective-permute-start.9 = (f32[448,128]{1,0:T(8,128)}, f32[448,128]{1,0:T(8,128)}, u32[]{:S(2)}, u32[]{:S(2)}) collective-permute-start(f32[448,128]{1,0:T(8,128)} %bitcast.7.refs_5_), channel_id=1, source_target_pairs={{0,8},{4,12},{8,16},{12,20},{16,24},{20,28},{24,0},{28,4},{1,9},{5... | collective-permute-start | bytes 688136 | tf_op jit(solution)/shard_map/ppermute | solution.py:536
  7.3 1.5 %collective-permute-start.8 = (f32[448,128]{1,0:T(8,128)}, f32[448,128]{1,0:T(8,128)}, u32[]{:S(2)}, u32[]{:S(2)}) collective-permute-start(f32[448,128]{1,0:T(8,128)} %bitcast.7.refs_5_), channel_id=1, source_target_pairs={{0,4},{4,0},{8,12},{12,8},{16,20},{20,16},{24,28},{28,24},{1,5},{5... | collective-permute-start | bytes 688136 | tf_op jit(solution)/shard_map/ppermute | solution.py:541
  8.8 2.2 %collective-permute-start.11 = (f32[448,128]{1,0:T(8,128)}, f32[448,128]{1,0:T(8,128)}, u32[]{:S(2)}, u32[]{:S(2)}) collective-permute-start(f32[448,128]{1,0:T(8,128)} %bitcast.7.refs_5_), channel_id=1, source_target_pairs={{0,24},{4,28},{8,0},{12,4},{16,8},{20,12},{24,16},{28,20},{1,25},{... | collective-permute-start | bytes 688136 | tf_op jit(solution)/shard_map/ppermute | solution.py:536
  11.1 0.0 copy-done.2
  11.1 0.0 collective-permute-done.refs_1_
  11.1 0.5 %collective-permute-start.1 = (f32[14,8,768]{2,1,0:T(8,128)}, f32[14,8,768]{2,1,0:T(8,128)S(1)}, u32[]{:S(2)}, u32[]{:S(2)}) collective-permute-start(f32[14,8,768]{2,1,0:T(8,128)} %copy-done.2), channel_id=1, source_target_pairs={{0,2},{1,3},{2,0},{3,1},{4,6},{5,7},{6,4},{7,5},{8,10},{9,11},{10,... | collective-permute-start | bytes 1032200 | tf_op jit(solution)/shard_map/ppermute | solution.py:516
  12.2 0.1 pad_add_fusion.rank_ref.place_ref
  12.3 7.5 %levels.1 = (f32[14,32,768]{2,1,0:T(8,128)S(1)}, f32[8,768]{1,0:T(8,128)S(1)}, bf16[256,192]{1,0:T(8,128)(2,1)S(1)}, bf16[128,256]{1,0:T(8,128)(2,1)S(1)}, bf16[...) custom-call(s32[2]{0:T(128)S(1)} %pad_add_fusion.rank_ref.place_ref, s32[1]{0:T(128)S(6)} %copy.16.count_ref, ...), custom_call_target="tpu_custom_call" | custom-call | flops 1000 | bytes 1000 | tf_op jit(solution)/shard_map/levels/pallas_call | solution.py:260
  19.8 0.0 collective-permute-done.9.refs_7_
  19.8 0.0 collective-permute-done.8.refs_6_
  19.8 0.0 collective-permute-done.2.refs_3_
  19.8 0.4 collective-permute-start.10
  20.2 0.2 collective-permute-done.11.refs_9_
  20.4 0.6 %collective-permute-start.12 = (f32[448,128]{1,0:T(8,128)}, f32[448,128]{1,0:T(8,128)S(1)}, u32[]{:S(2)}, u32[]{:S(2)}) collective-permute-start(f32[448,128]{1,0:T(8,128)} %collective-permute-done.9.refs_7_), channel_id=1, source_target_pairs={{0,8},{4,12},{8,16},{12,20},{16,24},{20,28},{24,0},{28,4},{1,9},{5... | collective-permute-start | bytes 688136 | tf_op jit(solution)/shard_map/ppermute | solution.py:536
  21.0 0.3 collective-permute-done.1.refs_2_
  21.2 0.0 copy-done.1
  21.2 2.2 %wave.2 = (f32[4,112,128]{2,1,0:T(8,128)S(1)}, f32[4,112,128]{2,1,0:T(8,128)S(1)}, f32[4,112,128]{2,1,0:T(8,128)S(1)}, f32[4,112,128]{2,1,0:T(8,128)S(1)}) custom-call(s32[2]{0:T(128)S(1)} %pad_add_fusion.rank_ref.place_ref, bf16[256,192]{1,0:T(8,128)(2,1)S(1)} %get-tuple-element.45.there_ref, bf16[128,256]{1,0:T(8,128)(2,1)S(1)} %get-tuple-element.46.back_ref, ...), custom_call_target="tpu_custom_call" | custom-call | flops 1000 | bytes 1000 | tf_op jit(solution)/shard_map/wave/pallas_call | solution.py:149
  23.5 0.1 collective-permute-start.3
  23.5 1.8 %collective-permute-start.4 = (f32[4,112,128]{2,1,0:T(8,128)S(1)}, f32[4,112,128]{2,1,0:T(8,128)S(1)}, u32[]{:S(2)}, u32[]{:S(2)}) collective-permute-start(f32[4,112,128]{2,1,0:T(8,128)S(1)} %get-tuple-element.51), channel_id=1, source_target_pairs={{0,2},{1,3},{2,0},{3,1},{4,6},{5,7},{6,4},{7,5},{8,10},{9,11},{10,... | collective-permute-start | bytes 688136 | tf_op jit(solution)/shard_map/ppermute | solution.py:516
  25.3 1.5 %wave.3 = (f32[2,112,128]{2,1,0:T(8,128)S(1)}, f32[2,112,128]{2,1,0:T(8,128)S(1)}, f32[2,112,128]{2,1,0:T(8,128)S(1)}, f32[2,112,128]{2,1,0:T(8,128)S(1)}) custom-call(s32[2]{0:T(128)S(1)} %pad_add_fusion.rank_ref.place_ref, bf16[256,192]{1,0:T(8,128)(2,1)S(1)} %get-tuple-element.45.there_ref, bf16[128,256]{1,0:T(8,128)(2,1)S(1)} %get-tuple-element.46.back_ref, ...), custom_call_target="tpu_custom_call" | custom-call | flops 1000 | bytes 1000 | tf_op jit(solution)/shard_map/wave/pallas_call | solution.py:149
  26.8 0.2 collective-permute-start.6
  27.0 0.0 collective-permute-done.10.refs_8_
  27.0 0.3 collective-permute-start.5
  27.3 2.7 %collective-permute-done.12.refs_10_ = f32[448,128]{1,0:T(8,128)S(1)} collective-permute-done((f32[448,128]{1,0:T(8,128)}, f32[448,128]{1,0:T(8,128)S(1)}, u32[]{:S(2)}, u32[]{:S(2)}) %collective-permute-start.12) | collective-permute-done | bytes 229408 | tf_op jit(solution)/shard_map/ppermute | solution.py:536
  29.9 0.8 %collective-permute-start.14 = (f32[448,128]{1,0:T(8,128)}, f32[448,128]{1,0:T(8,128)S(1)}, u32[]{:S(2)}, u32[]{:S(2)}) collective-permute-start(f32[448,128]{1,0:T(8,128)} %collective-permute-done.11.refs_9_), channel_id=1, source_target_pairs={{0,4},{4,0},{8,12},{12,8},{16,20},{20,16},{24,28},{28,24},{1,5},{5... | collective-permute-start | bytes 688136 | tf_op jit(solution)/shard_map/ppermute | solution.py:541
  30.7 0.0 collective-permute-done.6.refs_5_
  30.8 1.2 %collective-permute-start.15 = (f32[448,128]{1,0:T(8,128)S(1)}, f32[448,128]{1,0:T(8,128)S(1)}, u32[]{:S(2)}, u32[]{:S(2)}) collective-permute-start(f32[448,128]{1,0:T(8,128)S(1)} %collective-permute-done.12.refs_10_), channel_id=1, source_target_pairs={{0,4},{4,0},{8,12},{12,8},{16,20},{20,16},{24,28},{28,24},{1,5},{5... | collective-permute-start | bytes 688136 | tf_op jit(solution)/shard_map/ppermute | solution.py:541
  32.0 2.6 %ties.1 = (f32[448,256]{1,0:T(8,128)S(1)}, bf16[256,256]{1,0:T(8,128)(2,1)S(1)}, f32[14,256]{1,0:T(8,128)S(1)}, bf16[128,256]{1,0:T(8,128)(2,1)S(1)}) custom-call(s32[2]{0:T(128)S(1)} %pad_add_fusion.rank_ref.place_ref, s32[1,256]{1,0:T(1,128)} %refs_0_.1, s32[1,256]{1,0:T(1,128)} %bitcast.21, s32[1,256]{1,0:T(1,128)} %refs_2_.1, f32[1,256]{1,0:T(1,128)} %refs_3_.1, ...), custom_call_target="tpu_custom_call" | custom-call | flops 1000 | bytes 1000 | tf_op jit(solution)/shard_map/ties/pallas_call | solution.py:340
  34.6 0.0 collective-permute-done.3.refs_5_
  34.6 0.5 %collective-permute-start.7 = (f32[2,112,128]{2,1,0:T(8,128)S(1)}, f32[2,112,128]{2,1,0:T(8,128)S(1)}, u32[]{:S(2)}, u32[]{:S(2)}) collective-permute-start(f32[2,112,128]{2,1,0:T(8,128)S(1)} %get-tuple-element.56), channel_id=1, source_target_pairs={{0,2},{1,3},{2,0},{3,1},{4,6},{5,7},{6,4},{7,5},{8,10},{9,11},{10,... | collective-permute-start | bytes 344072 | tf_op jit(solution)/shard_map/ppermute | solution.py:516
  35.1 0.0 collective-permute-done.4.refs_6_
  35.1 0.0 collective-permute-start.13
  35.1 1.0 %collective-permute-done.5.refs_7_ = f32[4,112,128]{2,1,0:T(8,128)S(1)} collective-permute-done((f32[4,112,128]{2,1,0:T(8,128)S(1)}, f32[4,112,128]{2,1,0:T(8,128)S(1)}, u32[]{:S(2)}, u32[]{:S(2)}) %collective-permute-start.5) | collective-permute-done | bytes 229408 | tf_op jit(solution)/shard_map/ppermute | solution.py:516
  36.1 4.0 %solve.2 = (f32[2,7,32,768]{3,2,1,0:T(8,128)S(1)}, f32[8,128]{1,0:T(8,128)S(1)}) custom-call(s32[2]{0:T(128)S(1)} %pad_add_fusion.rank_ref.place_ref, f32[2,7,32,768]{3,2,1,0:T(8,128)S(1)} %bitcast.16, f32[8,768]{1,0:T(8,128)S(1)} %get-tuple-element.42.refs_1_, bf16[2,7,768,768]{3,2,1,0:T(8,128)(2,1)S(1)} %get-tuple-element.44.refs_2_, ...), custom_call_target="tpu_custom_call" | custom-call | flops 1000 | bytes 1000 | tf_op jit(solution)/shard_map/solve/pallas_call | solution.py:477
  40.2 0.4 collective-permute-done.7.refs_6_
  40.6 0.0 collective-permute-done.13.refs_7_
  40.6 0.0 collective-permute-done.14.refs_13_
  40.6 1.1 %collective-permute-done.15.refs_14_ = f32[448,128]{1,0:T(8,128)S(1)} collective-permute-done((f32[448,128]{1,0:T(8,128)S(1)}, f32[448,128]{1,0:T(8,128)S(1)}, u32[]{:S(2)}, u32[]{:S(2)}) %collective-permute-start.15) | collective-permute-done | bytes 229408 | tf_op jit(solution)/shard_map/ppermute | solution.py:541
  41.7 3.0 %solve.3 = f32[2,7,32,768]{3,2,1,0:T(8,128)} custom-call(s32[2]{0:T(128)S(1)} %pad_add_fusion.rank_ref.place_ref, f32[2,7,32,768]{3,2,1,0:T(8,128)S(1)} %bitcast.17, f32[8,768]{1,0:T(8,128)S(1)} %get-tuple-element.42.refs_1_, bf16[2,7,256,768]{3,2,1,0:T(8,128)(2,1)S(1)} %get-tuple-element.43.refs_2_, f32[8,128]{1,0:T(8,128)S(1)} %get-tuple-element.53.refs_3_, ...), custom_call_target="tpu_custom_call" | custom-call | flops 1000 | bytes 1000 | tf_op jit(solution)/shard_map/solve/pallas_call | solution.py:477
  (1 shorter events, 0.0 us)
Async XLA Ops:
  0.0 2.0 %copy-start = (f32[2,1,7,32,768]{4,3,2,1,0:T(8,128)S(1)}, f32[2,1,7,32,768]{4,3,2,1,0:T(8,128)}, u32[]{:S(2)}) copy-start(f32[2,1,7,32,768]{4,3,2,1,0:T(8,128)} %param.14) | copy-start | bytes 4128772
  1.2 0.7 %copy-start.3 = (f32[14,8,768]{2,1,0:T(8,128)}, f32[14,8,768]{2,1,0:T(8,128)S(1)}, u32[]{:S(2)}) copy-start(f32[14,8,768]{2,1,0:T(8,128)S(1)} %get-tuple-element.48) | copy-start | bytes 1032196
  2.0 9.1 %copy-start.2 = (f32[14,8,768]{2,1,0:T(8,128)}, f32[14,8,768]{2,1,0:T(8,128)S(1)}, u32[]{:S(2)}) copy-start(f32[14,8,768]{2,1,0:T(8,128)S(1)} %get-tuple-element.47) | copy-start | bytes 1032196
  2.0 9.1 %collective-permute-start = (f32[14,32,768]{2,1,0:T(8,128)S(1)}, f32[14,32,768]{2,1,0:T(8,128)S(1)}, u32[]{:S(2)}, u32[]{:S(2)}) collective-permute-start(f32[14,32,768]{2,1,0:T(8,128)S(1)} %bitcast.13), channel_id=1, source_target_pairs={{0,1},{1,0},{2,3},{3,2},{4,5},{5,4},{6,7},{7,6},{8,9},{9,8},{10,11... | collective-permute-start | bytes 4128776 | tf_op jit(solution)/shard_map/ppermute | solution.py:516
  2.4 17.4 %collective-permute-start.2 = (f32[14,8,768]{2,1,0:T(8,128)}, f32[14,8,768]{2,1,0:T(8,128)S(1)}, u32[]{:S(2)}, u32[]{:S(2)}) collective-permute-start(f32[14,8,768]{2,1,0:T(8,128)} %copy-done.3), channel_id=1, source_target_pairs={{0,3},{1,2},{2,1},{3,0},{4,7},{5,6},{6,5},{7,4},{8,11},{9,10},{10,... | collective-permute-start | bytes 1032200 | tf_op jit(solution)/shard_map/ppermute | solution.py:516
  5.7 14.1 %collective-permute-start.9 = (f32[448,128]{1,0:T(8,128)}, f32[448,128]{1,0:T(8,128)}, u32[]{:S(2)}, u32[]{:S(2)}) collective-permute-start(f32[448,128]{1,0:T(8,128)} %bitcast.7.refs_5_), channel_id=1, source_target_pairs={{0,8},{4,12},{8,16},{12,20},{16,24},{20,28},{24,0},{28,4},{1,9},{5... | collective-permute-start | bytes 688136 | tf_op jit(solution)/shard_map/ppermute | solution.py:536
  7.3 12.5 %collective-permute-start.8 = (f32[448,128]{1,0:T(8,128)}, f32[448,128]{1,0:T(8,128)}, u32[]{:S(2)}, u32[]{:S(2)}) collective-permute-start(f32[448,128]{1,0:T(8,128)} %bitcast.7.refs_5_), channel_id=1, source_target_pairs={{0,4},{4,0},{8,12},{12,8},{16,20},{20,16},{24,28},{28,24},{1,5},{5... | collective-permute-start | bytes 688136 | tf_op jit(solution)/shard_map/ppermute | solution.py:541
  8.8 11.6 %collective-permute-start.11 = (f32[448,128]{1,0:T(8,128)}, f32[448,128]{1,0:T(8,128)}, u32[]{:S(2)}, u32[]{:S(2)}) collective-permute-start(f32[448,128]{1,0:T(8,128)} %bitcast.7.refs_5_), channel_id=1, source_target_pairs={{0,24},{4,28},{8,0},{12,4},{16,8},{20,12},{24,16},{28,20},{1,25},{... | collective-permute-start | bytes 688136 | tf_op jit(solution)/shard_map/ppermute | solution.py:536
  11.1 10.2 %collective-permute-start.1 = (f32[14,8,768]{2,1,0:T(8,128)}, f32[14,8,768]{2,1,0:T(8,128)S(1)}, u32[]{:S(2)}, u32[]{:S(2)}) collective-permute-start(f32[14,8,768]{2,1,0:T(8,128)} %copy-done.2), channel_id=1, source_target_pairs={{0,2},{1,3},{2,0},{3,1},{4,6},{5,7},{6,4},{7,5},{8,10},{9,11},{10,... | collective-permute-start | bytes 1032200 | tf_op jit(solution)/shard_map/ppermute | solution.py:516
  12.3 9.0 %copy-start.1 = (f32[2,1,7,32,768]{4,3,2,1,0:T(8,128)S(1)}, f32[2,1,7,32,768]{4,3,2,1,0:T(8,128)}, u32[]{:S(2)}) copy-start(f32[2,1,7,32,768]{4,3,2,1,0:T(8,128)} %param.14) | copy-start | bytes 4128772
  19.8 7.2 %collective-permute-start.10 = (f32[448,128]{1,0:T(8,128)}, f32[448,128]{1,0:T(8,128)S(1)}, u32[]{:S(2)}, u32[]{:S(2)}) collective-permute-start(f32[448,128]{1,0:T(8,128)} %collective-permute-done.9.refs_7_), channel_id=1, source_target_pairs={{0,4},{4,0},{8,12},{12,8},{16,20},{20,16},{24,28},{28,24},{1,5},{5... | collective-permute-start | bytes 688136 | tf_op jit(solution)/shard_map/ppermute | solution.py:541
  20.4 9.5 %collective-permute-start.12 = (f32[448,128]{1,0:T(8,128)}, f32[448,128]{1,0:T(8,128)S(1)}, u32[]{:S(2)}, u32[]{:S(2)}) collective-permute-start(f32[448,128]{1,0:T(8,128)} %collective-permute-done.9.refs_7_), channel_id=1, source_target_pairs={{0,8},{4,12},{8,16},{12,20},{16,24},{20,28},{24,0},{28,4},{1,9},{5... | collective-permute-start | bytes 688136 | tf_op jit(solution)/shard_map/ppermute | solution.py:536
  23.5 11.1 %collective-permute-start.3 = (f32[4,112,128]{2,1,0:T(8,128)S(1)}, f32[4,112,128]{2,1,0:T(8,128)S(1)}, u32[]{:S(2)}, u32[]{:S(2)}) collective-permute-start(f32[4,112,128]{2,1,0:T(8,128)S(1)} %get-tuple-element.50), channel_id=1, source_target_pairs={{0,1},{1,0},{2,3},{3,2},{4,5},{5,4},{6,7},{7,6},{8,9},{9,8},{10,11... | collective-permute-start | bytes 688136 | tf_op jit(solution)/shard_map/ppermute | solution.py:516
  23.5 11.6 %collective-permute-start.4 = (f32[4,112,128]{2,1,0:T(8,128)S(1)}, f32[4,112,128]{2,1,0:T(8,128)S(1)}, u32[]{:S(2)}, u32[]{:S(2)}) collective-permute-start(f32[4,112,128]{2,1,0:T(8,128)S(1)} %get-tuple-element.51), channel_id=1, source_target_pairs={{0,2},{1,3},{2,0},{3,1},{4,6},{5,7},{6,4},{7,5},{8,10},{9,11},{10,... | collective-permute-start | bytes 688136 | tf_op jit(solution)/shard_map/ppermute | solution.py:516
  26.8 4.0 %collective-permute-start.6 = (f32[2,112,128]{2,1,0:T(8,128)S(1)}, f32[2,112,128]{2,1,0:T(8,128)S(1)}, u32[]{:S(2)}, u32[]{:S(2)}) collective-permute-start(f32[2,112,128]{2,1,0:T(8,128)S(1)} %get-tuple-element.55), channel_id=1, source_target_pairs={{0,1},{1,0},{2,3},{3,2},{4,5},{5,4},{6,7},{7,6},{8,9},{9,8},{10,11... | collective-permute-start | bytes 344072 | tf_op jit(solution)/shard_map/ppermute | solution.py:516
  27.0 9.1 %collective-permute-start.5 = (f32[4,112,128]{2,1,0:T(8,128)S(1)}, f32[4,112,128]{2,1,0:T(8,128)S(1)}, u32[]{:S(2)}, u32[]{:S(2)}) collective-permute-start(f32[4,112,128]{2,1,0:T(8,128)S(1)} %get-tuple-element.52), channel_id=1, source_target_pairs={{0,3},{1,2},{2,1},{3,0},{4,7},{5,6},{6,5},{7,4},{8,11},{9,10},{10,... | collective-permute-start | bytes 688136 | tf_op jit(solution)/shard_map/ppermute | solution.py:516
  29.9 10.7 %collective-permute-start.14 = (f32[448,128]{1,0:T(8,128)}, f32[448,128]{1,0:T(8,128)S(1)}, u32[]{:S(2)}, u32[]{:S(2)}) collective-permute-start(f32[448,128]{1,0:T(8,128)} %collective-permute-done.11.refs_9_), channel_id=1, source_target_pairs={{0,4},{4,0},{8,12},{12,8},{16,20},{20,16},{24,28},{28,24},{1,5},{5... | collective-permute-start | bytes 688136 | tf_op jit(solution)/shard_map/ppermute | solution.py:541
  30.8 11.0 %collective-permute-start.15 = (f32[448,128]{1,0:T(8,128)S(1)}, f32[448,128]{1,0:T(8,128)S(1)}, u32[]{:S(2)}, u32[]{:S(2)}) collective-permute-start(f32[448,128]{1,0:T(8,128)S(1)} %collective-permute-done.12.refs_10_), channel_id=1, source_target_pairs={{0,4},{4,0},{8,12},{12,8},{16,20},{20,16},{24,28},{28,24},{1,5},{5... | collective-permute-start | bytes 688136 | tf_op jit(solution)/shard_map/ppermute | solution.py:541
  34.6 6.0 %collective-permute-start.7 = (f32[2,112,128]{2,1,0:T(8,128)S(1)}, f32[2,112,128]{2,1,0:T(8,128)S(1)}, u32[]{:S(2)}, u32[]{:S(2)}) collective-permute-start(f32[2,112,128]{2,1,0:T(8,128)S(1)} %get-tuple-element.56), channel_id=1, source_target_pairs={{0,2},{1,3},{2,0},{3,1},{4,6},{5,7},{6,4},{7,5},{8,10},{9,11},{10,... | collective-permute-start | bytes 344072 | tf_op jit(solution)/shard_map/ppermute | solution.py:516
  35.1 5.5 %collective-permute-start.13 = (f32[2,112,128]{2,1,0:T(8,128)S(1)}, f32[2,112,128]{2,1,0:T(8,128)S(1)}, u32[]{:S(2)}, u32[]{:S(2)}) collective-permute-start(f32[2,112,128]{2,1,0:T(8,128)S(1)} %get-tuple-element.62), channel_id=1, source_target_pairs={{0,3},{1,2},{2,1},{3,0},{4,7},{5,6},{6,5},{7,4},{8,11},{9,10},{10,... | collective-permute-start | bytes 344072 | tf_op jit(solution)/shard_map/ppermute | solution.py:516
